TPU v7x, 512 devices: a whole 4x4x16 slice. The times are simulated.
512 devices in a mesh: rows: 16 (over z_lo, y), cols: 32 (over z_hi, x, core).
Axes of the slice: x: 4, y: 4, z: 16 (z_hi: 4, z_lo: 4; z = z_hi * 4 + z_lo), core: 2. Of those that a mesh axis runs over, the one named last changes fastest.
Arguments:
- iterate: bfloat16 [3584, 18432], P('rows', 'cols'), may hold values from -1 to 1, as said below
Outputs:
- update: bfloat16 [3584, 18432], P('rows', 'cols')
Inputs may be any that keep to these rules, and one draw needn't show every extreme that they name: `iterate`: entries are of size about 1/sqrt(18432) times a row scale between 0.6 and 1.3; no further structure is promised.
All inputs are finite; a program needn't handle non-finite values.
Results may differ from a plain program's by a relative error of at most 0.029.
Values may be sent and summed in bfloat16 or wider, within the bound.
No kernel may reach another device: no remote copies, remote signals or barrier semaphores. Data moves between devices by JAX's collectives and lax.ppermute only.
A program may use at most 64 MiB of HBM per device.

v0:
```python
import math

import jax
import jax.numpy as jnp
from jax import lax
from jax.sharding import PartitionSpec as P

D = 3584
FF = 18432


coef_linear = 3.4445
coef_cubic = -4.775
coef_quintic = 2.0315


def shards(iterate):
    columns = lax.all_gather(iterate, "rows", axis=0, tiled=True)
    tile = lax.psum_scatter(
        lax.dot_general(
            columns, iterate, (((1,), (1,)), ((), ())), preferred_element_type=jnp.float32
        ).astype(jnp.bfloat16),
        "cols",
        scatter_dimension=0,
        tiled=True,
    )
    gram_col = lax.all_gather(tile, "cols", axis=0, tiled=True)
    gram_row = lax.all_gather(tile, "rows", axis=1, tiled=True)
    square = lax.dot_general(
        gram_col, gram_row, (((0,), (1,)), ((), ())), preferred_element_type=jnp.float32
    )
    poly_tile = (coef_cubic * tile.T.astype(jnp.float32) + coef_quintic * square).astype(
        jnp.bfloat16
    )
    product = jnp.dot(
        lax.all_gather(poly_tile, "cols", axis=1, tiled=True),
        columns,
        preferred_element_type=jnp.float32,
    )
    step = coef_linear * iterate.astype(jnp.float32) + product
    return (0.2 * math.sqrt(max(D, FF)) * step).astype(jnp.bfloat16)


def solution(mesh):
    placed = (P("rows", "cols"),)
    return jax.shard_map(
        shards, mesh=mesh, in_specs=placed, out_specs=P("rows", "cols"), check_vma=False
    )
```

profile of v0, /device:TPU:1, one launch (start us, length us, event | category | flops | bytes accessed | tf_op | source)
XLA Modules:
  0.0 392.0 jit_solution(11575645744819245500)
XLA Ops:
  6.5 0.0 all-gather.4.cloned.1.call-start
  6.5 0.7 all-gather.4.cloned.1.call-update
  7.3 0.0 reduce-scatter.2.cloned.1.call-start
  7.3 92.7 %all-gather.4.cloned.1.call-done = bf16[3584,576]{1,0:T(8,128)(2,1)} async-done(((bf16[224,576]{1,0:T(8,128)(2,1)}), bf16[3584,576]{1,0:T(8,128)(2,1)}) %all-gather.4.cloned.1.call-update) | async-done | bytes 4128784 | tf_op jit(solution)/shard_map/all_gather | solution.py:18
  100.0 5.2 %convolution_convert_fusion = bf16[3584,224]{1,0:T(8,128)(2,1)} fusion(bf16[3584,576]{1,0:T(8,128)(2,1)} %all-gather.4.cloned.1.call-done, bf16[224,576]{1,0:T(8,128)(2,1)} %param.1), kind=kOutput, calls=%fused_computation | convolution fusion | flops 925646848 | bytes 5992448 | tf_op jit(solution)/shard_map/dot_general | solution.py:20
  105.2 0.0 reduce-scatter.2.cloned.1.call-update
  105.3 0.0 all-gather.6.cloned.1.call-start
  105.3 125.0 %reduce-scatter.2.cloned.1.call-done = bf16[112,224]{1,0:T(8,128)(2,1)} async-done(((bf16[3584,224]{1,0:T(8,128)(2,1)}), bf16[112,224]{1,0:T(8,128)(2,1)}) %reduce-scatter.2.cloned.1.call-update) | async-done | bytes 50192 | tf_op jit(solution)/shard_map/reduce_scatter | solution.py:19
  230.3 0.0 all-gather.6.cloned.1.call-update
  230.4 0.0 all-gather.8.cloned.1.call-start
  230.4 0.9 copy.2
  231.3 0.0 copy-start
  231.4 38.5 %all_gather.14 = bf16[112,3584]{0,1:T(8,128)(2,1)S(1)} all-gather(bf16[112,224]{0,1:T(8,128)(2,1)S(1)} %copy.2), channel_id=1, replica_groups=mesh['rows'=16,'cols'=32] {'rows'}, dimensions={1}, use_global_device_ids=true | all-gather | bytes 852992 | tf_op jit(solution)/shard_map/all_gather | solution.py:28
  269.9 36.7 %all-gather.6.cloned.1.call-done = bf16[3584,224]{1,0:T(8,128)(2,1)} async-done(((bf16[112,224]{1,0:T(8,128)(2,1)}), bf16[3584,224]{1,0:T(8,128)(2,1)}) %all-gather.6.cloned.1.call-update) | async-done | bytes 1605648 | tf_op jit(solution)/shard_map/all_gather | solution.py:27
  306.6 2.7 fusion.3
  309.2 0.0 all-gather.8.cloned.1.call-update
  309.3 71.2 %all-gather.8.cloned.1.call-done = bf16[224,3584]{0,1:T(8,128)(2,1)} async-done(((bf16[224,112]{0,1:T(8,128)(2,1)}), bf16[224,3584]{0,1:T(8,128)(2,1)}) %all-gather.8.cloned.1.call-update) | async-done | bytes 1605648 | tf_op jit(solution)/shard_map/all_gather | solution.py:36
  380.5 0.0 copy-done
  380.5 5.0 %fusion.1 = bf16[224,576]{1,0:T(8,128)(2,1)} fusion(bf16[224,3584]{0,1:T(8,128)(2,1)} %all-gather.8.cloned.1.call-done, bf16[3584,576]{1,0:T(8,128)(2,1)} %all-gather.4.cloned.1.call-done, bf16[224,576]{1,0:T(8,128)(2,1)S(1)} %copy-done), kind=kOutput, calls=%fused_computation.3 | convolution fusion | flops 925489152 | bytes 6250496 | tf_op jit(solution)/shard_map/dot_general | solution.py:35
Async XLA Ops:
  6.5 93.5 %all-gather.4.cloned.1.call-start = ((), (), s32[]{:S(2)}) async-start(), calls=%async_computation.1 | async-start | bytes 4874240 | tf_op jit(solution)/shard_map/all_gather | solution.py:18
  7.3 223.1 %reduce-scatter.2.cloned.1.call-start = ((), (), s32[]{:S(2)}) async-start(), calls=%async_computation.2 | async-start | bytes 1892352 | tf_op jit(solution)/shard_map/reduce_scatter | solution.py:19
  105.3 201.3 %all-gather.6.cloned.1.call-start = ((), (), s32[]{:S(2)}) async-start(), calls=%async_computation.3 | async-start | bytes 1892352 | tf_op jit(solution)/shard_map/all_gather | solution.py:27
  230.4 150.1 %all-gather.8.cloned.1.call-start = ((), (), s32[]{:S(2)}) async-start(), calls=%async_computation.4 | async-start | bytes 1892352 | tf_op jit(solution)/shard_map/all_gather | solution.py:36
  231.3 149.1 %copy-start = (bf16[224,576]{1,0:T(8,128)(2,1)S(1)}, bf16[224,576]{1,0:T(8,128)(2,1)}, u32[]{:S(2)}) copy-start(bf16[224,576]{1,0:T(8,128)(2,1)} %param.1) | copy-start | bytes 774148
Sparse Core Ops, SparseCore 0:
  9.4 90.5 all-gather.3
  105.4 124.9 reduce-scatter.1
  233.5 73.0 all-gather.5
  309.6 70.8 all-gather.7
where the time goes:
time: 392 us
  waiting for transfers between devices  326 us (83%)
  blocking collectives  38.5 us (10%)
  between operations  13.1 us (3%)
  matrix products  12.9 us (3%)
    reduce_scatter x1, waiting for transfers between devices, shards(): lax.psum_scatter(lax.dot_general(columns, iterate, (((1,), (1,)), ((), ()...  125 us
    all_gather x1, waiting for transfers between devices, shards(): columns = lax.all_gather(iterate, 'rows', axis=0, tiled=True)  92.7 us
    all_gather x1, waiting for transfers between devices, shards(): lax.all_gather(poly_tile, 'cols', axis=1, tiled=True)  71.2 us
    all_gather x1, blocking collectives, shards(): gram_row = lax.all_gather(tile, 'rows', axis=1, tiled=True)  38.5 us
    all_gather x1, waiting for transfers between devices, shards(): gram_col = lax.all_gather(tile, 'cols', axis=0, tiled=True)  36.7 us
  transfers between devices with their start and end apart: 4, of which 4 were waited for; matrix products, arithmetic and copies ran while one was open for 0% of the time, Pallas kernels for 0%

commit v1 on v0

v1 whole, which is shorter than its diff:
```python
import math

import jax
import jax.numpy as jnp
from jax import lax
from jax.sharding import Mesh
from jax.sharding import PartitionSpec as P

D = 3584
FF = 18432

coef_linear = 3.4445
coef_cubic = -4.775
coef_quintic = 2.0315

SWAP = [(0, 1), (1, 0)]


def product(lhs, rhs, contract):
    return lax.dot_general(
        lhs, rhs, ((contract[:1], contract[1:]), ((), ())), preferred_element_type=jnp.float32
    )


def total(parts):
    return jnp.sum(parts.astype(jnp.float32), axis=0)


def shards(iterate):
    core = lax.axis_index("core")
    rows, cols = iterate.shape
    left = lax.all_gather(iterate, "y", axis=0).reshape(4 * rows, cols)
    right = lax.all_gather(iterate, "z_lo", axis=0).reshape(4 * rows, cols)

    tile = product(left, right, (1, 1)).astype(jnp.bfloat16).reshape(2, 2 * rows, 4 * rows)
    away = lax.dynamic_index_in_dim(tile, 1 - core, 0, keepdims=False)
    kept = lax.dynamic_index_in_dim(tile, core, 0, keepdims=False)
    half = kept.astype(jnp.float32) + lax.ppermute(away, "core", SWAP).astype(jnp.float32)
    pieces = half.astype(jnp.bfloat16).reshape(4, rows // 2, 4 * rows)
    piece = total(lax.all_to_all(pieces, "x", 0, 0, tiled=True)).astype(jnp.bfloat16)
    piece = total(lax.all_gather(piece, "z_hi", axis=0)).astype(jnp.bfloat16)
    mine = lax.all_gather(piece, "x", axis=0).reshape(2 * rows, 4 * rows)
    other = lax.ppermute(mine, "core", SWAP)
    gram = jnp.concatenate(
        [jnp.where(core == 0, mine, other), jnp.where(core == 0, other, mine)], axis=0
    )

    once = product(gram, right, (1, 0)).astype(jnp.bfloat16).reshape(4, rows, cols)
    once = total(lax.all_to_all(once, "y", 0, 0, tiled=True))
    ours = lax.all_gather(once.astype(jnp.bfloat16), "y", axis=0).reshape(4 * rows, cols)
    twice = product(gram, ours, (0, 0)).astype(jnp.bfloat16).reshape(4, rows, cols)
    twice = total(lax.all_to_all(twice, "z_lo", 0, 0, tiled=True))

    step = coef_linear * iterate.astype(jnp.float32) + coef_cubic * once + coef_quintic * twice
    return (0.2 * math.sqrt(max(D, FF)) * step).astype(jnp.bfloat16)


def solution(mesh):
    axes = ("z_lo", "y", "z_hi", "x", "core")
    fine = Mesh(mesh.devices.reshape(4, 4, 4, 4, 2), axes)
    placed = P(axes[:2], axes[2:])
    return jax.shard_map(
        shards, mesh=fine, in_specs=(placed,), out_specs=placed, check_vma=False
    )
```

time: 392 us -> 196 us (0.50)
  waiting for transfers between devices: 326 us -> 4.16 us
  blocking collectives: 38.5 us -> 163 us
  starting transfers between devices: 0.12 us -> 14.2 us
  between operations: 13.1 us -> 0.12 us
  matrix products: 12.9 us -> 5.62 us
    all_gather x3 -> x0, waiting for transfers between devices: 201 us -> none  [the longest x1 92.7 us: shards(): columns = lax.all_gather(iterate, 'rows', axis=0, tiled=True)]
    reduce_scatter x1 -> x0, waiting for transfers between devices: 125 us -> none  [shards(): lax.psum_scatter(lax.dot_general(columns, iterate, (((1,), (1,)), ((), ()...]
    all_gather x1 -> x5, blocking collectives: 38.5 us -> 102 us  [the longest x1 39.3 us: shards(): piece = total(lax.all_gather(piece, 'z_hi', axis=0)).astype(jnp.bfloat16)]
    all_to_all x0 -> x3, blocking collectives: none -> 61.5 us  [the longest x1 28.2 us: shards(): twice = total(lax.all_to_all(twice, 'z_lo', 0, 0, tiled=True))]
    ppermute x0 -> x2, starting transfers between devices: none -> 14.2 us  [the longest x1 8.38 us: shards(): lax.ppermute(away, 'core', SWAP).astype(jnp.float32)]
    dot_general x3, matrix products: 12.9 us -> 5.62 us  [product(): lax.dot_general(lhs, rhs, ((contract[:1], contract[1:]), ((), ())), prefe...]
    ppermute x0 -> x2, waiting for transfers between devices: none -> 4.16 us  [the longest x1 2.26 us: shards(): lax.ppermute(away, 'core', SWAP).astype(jnp.float32)]
  transfers between devices with their start and end apart: 4 -> 2, of which waited for: 4 -> 2; matrix products, arithmetic and copies ran while one was open for 0% -> 0% of each run, Pallas kernels for 0% -> 0%
where the time goes in v1:
time: 196 us; the launch traced here: 195 us
  blocking collectives  163 us (83%)
  starting transfers between devices  14.2 us (7%)
  matrix products  5.62 us (3%)
  local copies, waits for them, and re-layouts  4.38 us (2%)
  waiting for transfers between devices  4.16 us (2%)
  other arithmetic  3.02 us (2%)
    all_gather x1, blocking collectives, shards(): piece = total(lax.all_gather(piece, 'z_hi', axis=0)).astype(jnp.bfloat16)  39.3 us
    all_to_all x1, blocking collectives, shards(): twice = total(lax.all_to_all(twice, 'z_lo', 0, 0, tiled=True))  28.2 us
    all_gather x1, blocking collectives, shards(): right = lax.all_gather(iterate, 'z_lo', axis=0).reshape(4 * rows, cols)  23.7 us
    all_to_all x1, blocking collectives, shards(): once = total(lax.all_to_all(once, 'y', 0, 0, tiled=True))  18.5 us
    all_to_all x1, blocking collectives, shards(): lax.all_to_all(pieces, 'x', 0, 0, tiled=True)  14.8 us
    all_gather x1, blocking collectives, shards(): left = lax.all_gather(iterate, 'y', axis=0).reshape(4 * rows, cols)  14.1 us
    all_gather x1, blocking collectives, shards(): lax.all_gather(once.astype(jnp.bfloat16), 'y', axis=0)  12.8 us
    all_gather x1, blocking collectives, shards(): mine = lax.all_gather(piece, 'x', axis=0).reshape(2 * rows, 4 * rows)  12.1 us
  transfers between devices with their start and end apart: 2, of which 2 were waited for; matrix products, arithmetic and copies ran while one was open for 0% of the time, Pallas kernels for 0%

profile of v1, /device:TPU:1, one launch (start us, length us, event | category | flops | bytes accessed | tf_op | source)
XLA Modules:
  0.0 195.0 jit_solution(8931993839217352473)
XLA Ops:
  0.0 23.7 %all-gather.1 = bf16[896,576]{1,0:T(8,128)(2,1)S(1)} all-gather(bf16[224,576]{1,0:T(8,128)(2,1)} %param.1), channel_id=3, replica_groups=mesh['z_lo'=4,'y'=4,'z_hi'=4,'x'=4,'core'=2] {'z_lo'}, dimensions={0}, use_global_device_ids=true | all-gather | bytes 1290240 | tf_op jit(solution)/shard_map/all_gather | solution.py:33
  23.7 0.0 copy-done
  23.7 14.1 %all-gather = bf16[896,576]{1,0:T(8,128)(2,1)} all-gather(bf16[224,576]{1,0:T(8,128)(2,1)S(1)} %copy-done), channel_id=2, replica_groups=mesh['z_lo'=4,'y'=4,'z_hi'=4,'x'=4,'core'=2] {'y'}, dimensions={0}, use_global_device_ids=true | all-gather | bytes 1290240 | tf_op jit(solution)/shard_map/all_gather | solution.py:32
  37.7 2.8 %convolution_convert_fusion = bf16[896,896]{1,0:T(8,128)(2,1)S(1)} fusion(bf16[896,576]{1,0:T(8,128)(2,1)} %all-gather, bf16[896,576]{1,0:T(8,128)(2,1)S(1)} %all-gather.1), kind=kOutput, calls=%fused_computation.2 | convolution fusion | flops 925646848 | bytes 3670016 | tf_op jit(solution)/shard_map/dot_general | solution.py:20
  40.5 1.0 dynamic-slice_bitcast_fusion
  41.5 8.4 %collective-permute-start = (bf16[448,896]{1,0:T(8,128)(2,1)}, bf16[448,896]{1,0:T(8,128)(2,1)}, u32[]{:S(2)}, u32[]{:S(2)}) collective-permute-start(bf16[448,896]{1,0:T(8,128)(2,1)} %dynamic-slice_bitcast_fusion), channel_id=1, source_target_pairs={{0,1},{1,0},{2,3},{3,2},{4,5},{5,4},{6,7},{7,6},{8,9},{9,8},{10,11... | collective-permute-start | bytes 2408456 | tf_op jit(solution)/shard_map/ppermute | solution.py:38
  49.9 2.3 %collective-permute-done = bf16[448,896]{1,0:T(8,128)(2,1)} collective-permute-done((bf16[448,896]{1,0:T(8,128)(2,1)}, bf16[448,896]{1,0:T(8,128)(2,1)}, u32[]{:S(2)}, u32[]{:S(2)}) %collective-permute-start) | collective-permute-done | bytes 802848 | tf_op jit(solution)/shard_map/ppermute | solution.py:38
  52.1 1.4 fusion
  53.5 14.8 %all_to_all.15 = bf16[4,112,896]{2,1,0:T(8,128)(2,1)S(1)} all-to-all(bf16[4,112,896]{2,1,0:T(8,128)(2,1)S(1)} %bitcast.16), channel_id=1, replica_groups=mesh['z_lo'=4,'y'=4,'z_hi'=4,'x'=4,'core'=2] {'x'}, dimensions={0} | all-to-all | bytes 1605632 | tf_op jit(solution)/shard_map/all_to_all | solution.py:40
  68.3 0.1 reduce_sum.42
  68.4 39.3 %all-gather.2 = bf16[448,896]{1,0:T(8,128)(2,1)S(1)} all-gather(bf16[112,896]{1,0:T(8,128)(2,1)S(1)} %reduce_sum.42), channel_id=4, replica_groups=mesh['z_lo'=4,'y'=4,'z_hi'=4,'x'=4,'core'=2] {'z_hi'}, dimensions={0}, use_global_device_ids=true | all-gather | bytes 1003520 | tf_op jit(solution)/shard_map/all_gather | solution.py:41
  107.7 0.1 reduce_sum.43
  107.9 12.1 %all-gather.3 = bf16[448,896]{1,0:T(8,128)(2,1)S(1)} all-gather(bf16[112,896]{1,0:T(8,128)(2,1)S(1)} %reduce_sum.43), channel_id=5, replica_groups=mesh['z_lo'=4,'y'=4,'z_hi'=4,'x'=4,'core'=2] {'x'}, dimensions={0}, use_global_device_ids=true | all-gather | bytes 1003520 | tf_op jit(solution)/shard_map/all_gather | solution.py:42
  120.0 5.8 %collective-permute-start.1 = (bf16[448,896]{1,0:T(8,128)(2,1)S(1)}, bf16[448,896]{1,0:T(8,128)(2,1)S(1)}, u32[]{:S(2)}, u32[]{:S(2)}) collective-permute-start(bf16[448,896]{1,0:T(8,128)(2,1)S(1)} %all-gather.3), channel_id=1, source_target_pairs={{0,1},{1,0},{2,3},{3,2},{4,5},{5,4},{6,7},{7,6},{8,9},{9,8},{10,11... | collective-permute-start | bytes 2408456 | tf_op jit(solution)/shard_map/ppermute | solution.py:43
  125.8 1.9 collective-permute-done.1
  127.7 0.2 broadcast_select_fusion.1
  127.9 0.0 copy-start.1
  127.9 0.0 copy-start.3
  127.9 0.9 copy-done.1
  128.8 0.3 copy-done.3
  129.1 1.4 convolution_convert_fusion.2
  130.5 1.1 copy.4
  131.6 18.5 %all_to_all.16 = bf16[4,224,576]{2,1,0:T(8,128)(2,1)S(1)} all-to-all(bf16[4,224,576]{2,1,0:T(8,128)(2,1)S(1)} %bitcast.14), channel_id=1, replica_groups=mesh['z_lo'=4,'y'=4,'z_hi'=4,'x'=4,'core'=2] {'y'}, dimensions={0} | all-to-all | bytes 2064384 | tf_op jit(solution)/shard_map/all_to_all | solution.py:49
  150.2 0.2 convert_reduce_fusion.1
  150.4 12.8 %all-gather.4 = bf16[896,576]{1,0:T(8,128)(2,1)S(1)} all-gather(bf16[224,576]{1,0:T(8,128)(2,1)S(1)} %convert_element_type.58), channel_id=6, replica_groups=mesh['z_lo'=4,'y'=4,'z_hi'=4,'x'=4,'core'=2] {'y'}, dimensions={0}, use_global_device_ids=true | all-gather | bytes 1290240 | tf_op jit(solution)/shard_map/all_gather | solution.py:50
  163.2 0.0 copy-done.2
  163.2 0.0 copy-done.4
  163.2 1.4 convolution_convert_fusion.1
  164.6 1.1 copy.5
  165.7 28.2 %all_to_all.17 = bf16[4,224,576]{2,1,0:T(8,128)(2,1)S(1)} all-to-all(bf16[4,224,576]{2,1,0:T(8,128)(2,1)S(1)} %bitcast.15), channel_id=1, replica_groups=mesh['z_lo'=4,'y'=4,'z_hi'=4,'x'=4,'core'=2] {'z_lo'}, dimensions={0} | all-to-all | bytes 2064384 | tf_op jit(solution)/shard_map/all_to_all | solution.py:52
  193.9 0.2 convert_reduce_fusion
  194.1 0.9 multiply_convert_fusion
  (4 shorter events, 0.0 us)
Async XLA Ops:
  0.0 23.7 %copy-start = (bf16[224,576]{1,0:T(8,128)(2,1)S(1)}, bf16[224,576]{1,0:T(8,128)(2,1)}, u32[]{:S(2)}) copy-start(bf16[224,576]{1,0:T(8,128)(2,1)} %param.1) | copy-start | bytes 774148
  41.5 10.6 %collective-permute-start = (bf16[448,896]{1,0:T(8,128)(2,1)}, bf16[448,896]{1,0:T(8,128)(2,1)}, u32[]{:S(2)}, u32[]{:S(2)}) collective-permute-start(bf16[448,896]{1,0:T(8,128)(2,1)} %dynamic-slice_bitcast_fusion), channel_id=1, source_target_pairs={{0,1},{1,0},{2,3},{3,2},{4,5},{5,4},{6,7},{7,6},{8,9},{9,8},{10,11... | collective-permute-start | bytes 2408456 | tf_op jit(solution)/shard_map/ppermute | solution.py:38
  120.0 7.8 %collective-permute-start.1 = (bf16[448,896]{1,0:T(8,128)(2,1)S(1)}, bf16[448,896]{1,0:T(8,128)(2,1)S(1)}, u32[]{:S(2)}, u32[]{:S(2)}) collective-permute-start(bf16[448,896]{1,0:T(8,128)(2,1)S(1)} %all-gather.3), channel_id=1, source_target_pairs={{0,1},{1,0},{2,3},{3,2},{4,5},{5,4},{6,7},{7,6},{8,9},{9,8},{10,11... | collective-permute-start | bytes 2408456 | tf_op jit(solution)/shard_map/ppermute | solution.py:43
  127.9 0.9 copy-start.1
  127.9 1.2 copy-start.3
  150.2 13.0 %copy-start.2 = (bf16[448,896]{1,0:T(8,128)(2,1)S(1)}, bf16[448,896]{1,0:T(8,128)(2,1)}, u32[]{:S(2)}) copy-start(bf16[448,896]{1,0:T(8,128)(2,1)} %copy-done.1) | copy-start | bytes 2408452
  150.2 13.0 %copy-start.4 = (bf16[448,896]{1,0:T(8,128)(2,1)S(1)}, bf16[448,896]{1,0:T(8,128)(2,1)}, u32[]{:S(2)}) copy-start(bf16[448,896]{1,0:T(8,128)(2,1)} %copy-done.3) | copy-start | bytes 2408452

commit v2 on v1

v2 whole, which is shorter than its diff:
```python
import math

import jax
import jax.numpy as jnp
from jax import lax
from jax.sharding import Mesh
from jax.sharding import PartitionSpec as P

D = 3584
FF = 18432

coef_linear = 3.4445
coef_cubic = -4.775
coef_quintic = 2.0315

SWAP = [(0, 1), (1, 0)]

SAME_Y = [[4 * y + (s - y) % 4 for s in range(4)] for y in range(4)]
SAME_X = [[4 * ((s - x) % 4) + x for s in range(4)] for x in range(4)]
SAME_S = [[4 * y + (s - y) % 4 for y in range(4)] for s in range(4)]
SAME_Y_CORES = [[2 * i + core for i in group for core in range(2)] for group in SAME_Y]


def product(lhs, rhs, contract):
    return lax.dot_general(
        lhs, rhs, ((contract[:1], contract[1:]), ((), ())), preferred_element_type=jnp.float32
    )


def total(parts):
    return jnp.sum(parts.astype(jnp.float32), axis=0)


def shards(iterate):
    core = lax.axis_index("core")
    rows, cols = iterate.shape
    right = lax.all_gather(iterate, "z_lo", axis=0).reshape(4 * rows, cols)
    left = lax.all_gather(iterate, "y", axis=0).reshape(4 * rows, cols)
    whole = lax.all_gather(right, "y", axis=0).reshape(16 * rows, cols)

    tile = product(left, right, (1, 1)).astype(jnp.bfloat16).reshape(4, 2, rows // 2, 4 * rows)
    away = lax.dynamic_index_in_dim(tile, 1 - core, 1, keepdims=False)
    kept = lax.dynamic_index_in_dim(tile, core, 1, keepdims=False)
    half = kept.astype(jnp.float32) + lax.ppermute(away, "core", SWAP).astype(jnp.float32)
    half = lax.all_to_all(
        half.astype(jnp.bfloat16), ("y", "x"), 0, 0, tiled=True, axis_index_groups=SAME_Y
    )
    piece = total(half).astype(jnp.bfloat16)
    piece = total(lax.all_gather(piece, "z_hi", axis=0)).astype(jnp.bfloat16)

    mine = lax.all_gather(piece, ("y", "x"), axis=0, axis_index_groups=SAME_S)
    other = lax.ppermute(mine, "core", SWAP)
    gram = lax.all_gather(piece, ("y", "x", "core"), axis=0, axis_index_groups=SAME_Y_CORES)
    gram = gram.reshape(4 * rows, 4 * rows)
    band = jnp.stack([jnp.where(core == 0, mine, other), jnp.where(core == 0, other, mine)], axis=0)
    band = band.transpose(0, 2, 1, 3).reshape(rows, 16 * rows)

    once = product(band, whole, (1, 0)).astype(jnp.bfloat16)
    once = lax.all_gather(once, ("y", "x"), axis=0, axis_index_groups=SAME_X)
    twice = product(gram, once.reshape(4 * rows, cols), (0, 0))
    twice = twice.astype(jnp.bfloat16).reshape(4, rows, cols)
    twice = total(lax.all_to_all(twice, "z_lo", 0, 0, tiled=True))
    once = lax.dynamic_index_in_dim(once, lax.axis_index("y"), 0, keepdims=False)

    step = coef_linear * iterate.astype(jnp.float32) + coef_cubic * once.astype(jnp.float32)
    step = step + coef_quintic * twice
    return (0.2 * math.sqrt(max(D, FF)) * step).astype(jnp.bfloat16)


def solution(mesh):
    axes = ("z_lo", "y", "z_hi", "x", "core")
    fine = Mesh(mesh.devices.reshape(4, 4, 4, 4, 2), axes)
    placed = P(axes[:2], axes[2:])
    return jax.shard_map(
        shards, mesh=fine, in_specs=(placed,), out_specs=placed, check_vma=False
    )
```

time: 196 us -> 200 us (1.020)
  blocking collectives: 163 us -> 124 us
  waiting for transfers between devices: 4.16 us -> 31.4 us
  between operations: 0.12 us -> 13.5 us
  starting transfers between devices: 14.2 us -> 17.1 us
  matrix products: 5.62 us -> 8.14 us
    all_to_all x3 -> x1, blocking collectives: 61.5 us -> 14.6 us  [shards(): lax.all_to_all(half.astype(jnp.bfloat16), ('y', 'x'), 0, 0, tiled=True, a...]
    all_to_all x0 -> x1, waiting for transfers between devices: none -> 27.3 us  [shards(): twice = total(lax.all_to_all(twice, 'z_lo', 0, 0, tiled=True))]
    all_gather x2, blocking collectives: 24.9 us -> 31.7 us  [the longest x1 17.3 us: shards(): once = lax.all_gather(once, ('y', 'x'), axis=0, axis_index_groups=SAME_X)]
    all_to_all x0 -> x1, starting transfers between devices: none -> 6.22 us  [shards(): twice = total(lax.all_to_all(twice, 'z_lo', 0, 0, tiled=True))]
    dot_general x3, matrix products: 5.62 us -> 8.14 us  [product(): lax.dot_general(lhs, rhs, ((contract[:1], contract[1:]), ((), ())), prefe...]
  transfers between devices with their start and end apart: 2 -> 5, of which waited for: 2 -> 3; matrix products, arithmetic and copies ran while one was open for 0% -> 4% of each run, Pallas kernels for 0% -> 0%
where the time goes in v2:
time: 200 us
  blocking collectives  124 us (62%)
  waiting for transfers between devices  31.4 us (16%)
  starting transfers between devices  17.1 us (9%)
  between operations  13.5 us (7%)
  matrix products  8.14 us (4%)
  local copies, waits for them, and re-layouts  3.22 us (2%)
  other arithmetic  2.53 us (1%)
    all_gather x1, blocking collectives, shards(): piece = total(lax.all_gather(piece, 'z_hi', axis=0)).astype(jnp.bfloat16)  37.4 us
    all_to_all x1, waiting for transfers between devices, shards(): twice = total(lax.all_to_all(twice, 'z_lo', 0, 0, tiled=True))  27.3 us
    all_gather x1, blocking collectives, shards(): right = lax.all_gather(iterate, 'z_lo', axis=0).reshape(4 * rows, cols)  24.4 us
    all_gather x1, blocking collectives, shards(): once = lax.all_gather(once, ('y', 'x'), axis=0, axis_index_groups=SAME_X)  17.3 us
    all_gather x1, blocking collectives, shards(): left = lax.all_gather(iterate, 'y', axis=0).reshape(4 * rows, cols)  16 us
    all_to_all x1, blocking collectives, shards(): lax.all_to_all(half.astype(jnp.bfloat16), ('y', 'x'), 0, 0, tiled=True, a...  14.6 us
    all_gather x1, blocking collectives, shards(): mine = lax.all_gather(piece, ('y', 'x'), axis=0, axis_index_groups=SAME_S)  14.4 us
    dot_general x3, matrix products, product(): lax.dot_general(lhs, rhs, ((contract[:1], contract[1:]), ((), ())), prefe...  8.14 us
  transfers between devices with their start and end apart: 5, of which 3 were waited for; matrix products, arithmetic and copies ran while one was open for 4% of the time, Pallas kernels for 0%

profile of v2, /device:TPU:1, one launch (start us, length us, event | category | flops | bytes accessed | tf_op | source)
XLA Modules:
  0.0 200.0 jit_solution(3360367331401276790)
XLA Ops:
  6.5 0.0 all-gather.12.cloned.1.call-start
  6.5 24.4 %all-gather.1 = bf16[896,576]{1,0:T(8,128)(2,1)} all-gather(bf16[224,576]{1,0:T(8,128)(2,1)} %param.1), channel_id=3, replica_groups=mesh['z_lo'=4,'y'=4,'z_hi'=4,'x'=4,'core'=2] {'z_lo'}, dimensions={0}, use_global_device_ids=true | all-gather | bytes 1290240 | tf_op jit(solution)/shard_map/all_gather | solution.py:37
  30.9 0.0 all-gather.12.cloned.1.call-update
  30.9 0.0 all-gather.10.cloned.1.call-start
  31.0 0.0 copy-done.1
  31.0 16.0 %all-gather = bf16[896,576]{1,0:T(8,128)(2,1)S(1)} all-gather(bf16[224,576]{1,0:T(8,128)(2,1)S(1)} %copy-done.1), channel_id=2, replica_groups=mesh['z_lo'=4,'y'=4,'z_hi'=4,'x'=4,'core'=2] {'y'}, dimensions={0}, use_global_device_ids=true | all-gather | bytes 1290240 | tf_op jit(solution)/shard_map/all_gather | solution.py:38
  47.0 1.5 convolution_convert_fusion
  48.6 1.0 dynamic-slice_bitcast_fusion
  49.5 6.6 %collective-permute-start = (bf16[4,112,896]{2,1,0:T(8,128)(2,1)}, bf16[4,112,896]{2,1,0:T(8,128)(2,1)S(1)}, u32[]{:S(2)}, u32[]{:S(2)}) collective-permute-start(bf16[4,112,896]{2,1,0:T(8,128)(2,1)} %dynamic-slice_bitcast_fusion), channel_id=1, source_target_pairs={{0,1},{1,0},{2,3},{3,2},{4,5},{5,4},{6,7},{7,6},{8,9},{9,8},{10,11... | collective-permute-start | bytes 2408456 | tf_op jit(solution)/shard_map/ppermute | solution.py:44
  56.2 2.1 %collective-permute-done = bf16[4,112,896]{2,1,0:T(8,128)(2,1)S(1)} collective-permute-done((bf16[4,112,896]{2,1,0:T(8,128)(2,1)}, bf16[4,112,896]{2,1,0:T(8,128)(2,1)S(1)}, u32[]{:S(2)}, u32[]{:S(2)}) %collective-permute-start) | collective-permute-done | bytes 802848 | tf_op jit(solution)/shard_map/ppermute | solution.py:44
  58.3 0.2 fusion
  58.5 14.6 %all_to_all.10 = bf16[4,112,896]{2,1,0:T(8,128)(2,1)S(1)} all-to-all(bf16[4,112,896]{2,1,0:T(8,128)(2,1)S(1)} %fusion), channel_id=1, replica_groups={{0,2,4,6},{38,32,34,36},{68,70,64,66},{98,100,102,96},{1,3,5,7},{39,33,..., dimensions={0} | all-to-all | bytes 1605632 | tf_op jit(solution)/shard_map/all_to_all | solution.py:45
  73.1 0.1 reduce_sum.33
  73.2 37.4 %all-gather.2 = bf16[448,896]{1,0:T(8,128)(2,1)S(1)} all-gather(bf16[112,896]{1,0:T(8,128)(2,1)S(1)} %reduce_sum.33), channel_id=4, replica_groups=mesh['z_lo'=4,'y'=4,'z_hi'=4,'x'=4,'core'=2] {'z_hi'}, dimensions={0}, use_global_device_ids=true | all-gather | bytes 1003520 | tf_op jit(solution)/shard_map/all_gather | solution.py:49
  110.6 0.8 reduce_sum.34
  111.5 0.0 all-gather.10.cloned.1.call-update
  111.5 14.4 %all-gather.3 = bf16[448,896]{1,0:T(8,128)(2,1)S(1)} all-gather(bf16[112,896]{1,0:T(8,128)(2,1)} %reduce_sum.34), channel_id=5, replica_groups={{0,38,68,98},{2,32,70,100},{4,34,64,102},{6,36,66,96},{1,39,69,99},{3,3..., dimensions={0}, use_global_device_ids=true | all-gather | bytes 1003520 | tf_op jit(solution)/shard_map/all_gather | solution.py:51
  125.9 4.2 %collective-permute-start.1 = (bf16[4,112,896]{2,1,0:T(8,128)(2,1)S(1)}, bf16[4,112,896]{2,1,0:T(8,128)(2,1)S(1)}, u32[]{:S(2)}, u32[]{:S(2)}) collective-permute-start(bf16[4,112,896]{2,1,0:T(8,128)(2,1)S(1)} %bitcast.34), channel_id=1, source_target_pairs={{0,1},{1,0},{2,3},{3,2},{4,5},{5,4},{6,7},{7,6},{8,9},{9,8},{10,11... | collective-permute-start | bytes 2408456 | tf_op jit(solution)/shard_map/ppermute | solution.py:52
  130.2 1.9 collective-permute-done.1
  132.1 0.2 select_bitcast_fusion.1
  132.2 0.2 maximum_bitcast_fusion
  132.4 0.6 copy.5
  133.0 0.2 copy.7
  133.2 0.0 all-gather.12.cloned.1.call-done
  133.3 3.8 %convolution_convert_fusion.2 = bf16[224,576]{1,0:T(8,128)(2,1)S(1)} fusion(bf16[224,3584]{1,0:T(8,128)(2,1)S(1)} %bitcast.40, bf16[3584,576]{1,0:T(8,128)(2,1)} %all-gather.12.cloned.1.call-done), kind=kOutput, calls=%fused_computation.6 | convolution fusion | flops 924973056 | bytes 5992448 | tf_op jit(solution)/shard_map/dot_general | solution.py:25
  137.0 17.3 %all-gather.4 = bf16[896,576]{1,0:T(8,128)(2,1)S(1)} all-gather(bf16[224,576]{1,0:T(8,128)(2,1)S(1)} %convolution_convert_fusion.2), channel_id=6, replica_groups={{0,32,64,96},{98,2,34,66},{68,100,4,36},{38,70,102,6},{1,33,65,97},{99,..., dimensions={0}, use_global_device_ids=true | all-gather | bytes 1290240 | tf_op jit(solution)/shard_map/all_gather | solution.py:59
  154.3 2.8 %convolution_convert_fusion.1 = bf16[896,576]{0,1:T(8,128)(2,1)S(1)} fusion(bf16[896,896]{1,0:T(8,128)(2,1)} %all-gather.10.cloned.1.call-done, bf16[896,576]{1,0:T(8,128)(2,1)S(1)} %all-gather.4), kind=kOutput, calls=%fused_computation.5 | convolution fusion | flops 925360128 | bytes 3670016 | tf_op jit(solution)/shard_map/dot_general | solution.py:25
  157.1 1.4 copy.6
  158.6 6.2 %all-to-all-start.1 = ((bf16[4,224,576]{2,1,0:T(8,128)(2,1)}), bf16[4,224,576]{2,1,0:T(8,128)(2,1)S(1)}, u32[]{:S(2)}, u32[]{:S(2)}) async-start(bf16[4,224,576]{2,1,0:T(8,128)(2,1)} %bitcast.10), calls=%async_computation.1 | async-start | bytes 2293760 | tf_op jit(solution)/shard_map/all_to_all | solution.py:62
  164.8 27.3 %all-to-all-done.1 = bf16[4,224,576]{2,1,0:T(8,128)(2,1)S(1)} async-done(((bf16[4,224,576]{2,1,0:T(8,128)(2,1)}), bf16[4,224,576]{2,1,0:T(8,128)(2,1)S(1)}, u32[]{:S(2)}, u32[]{:S(2)}) %all-to-all-start.1) | async-done | bytes 1032224 | tf_op jit(solution)/shard_map/all_to_all | solution.py:62
  192.1 0.2 convert_reduce_fusion
  192.3 0.9 fusion.3
  (4 shorter events, 0.0 us)
Async XLA Ops:
  6.5 24.5 %copy-start.1 = (bf16[224,576]{1,0:T(8,128)(2,1)S(1)}, bf16[224,576]{1,0:T(8,128)(2,1)}, u32[]{:S(2)}) copy-start(bf16[224,576]{1,0:T(8,128)(2,1)} %param.1) | copy-start | bytes 774148
  6.5 126.7 %all-gather.12.cloned.1.call-start = ((), (), s32[]{:S(2)}) async-start(), calls=%async_computation.3 | async-start | bytes 5734400 | tf_op jit(solution)/shard_map/all_gather | solution.py:39
  30.9 16.1 %copy-start = (bf16[896,576]{1,0:T(8,128)(2,1)S(1)}, bf16[896,576]{1,0:T(8,128)(2,1)}, u32[]{:S(2)}) copy-start(bf16[896,576]{1,0:T(8,128)(2,1)} %all-gather.1) | copy-start | bytes 3096580
  30.9 123.3 %all-gather.10.cloned.1.call-start = ((), (), s32[]{:S(2)}) async-start(), calls=%async_computation.2 | async-start | bytes 1806336 | tf_op jit(solution)/shard_map/all_gather | solution.py:53
  49.5 8.8 %collective-permute-start = (bf16[4,112,896]{2,1,0:T(8,128)(2,1)}, bf16[4,112,896]{2,1,0:T(8,128)(2,1)S(1)}, u32[]{:S(2)}, u32[]{:S(2)}) collective-permute-start(bf16[4,112,896]{2,1,0:T(8,128)(2,1)} %dynamic-slice_bitcast_fusion), channel_id=1, source_target_pairs={{0,1},{1,0},{2,3},{3,2},{4,5},{5,4},{6,7},{7,6},{8,9},{9,8},{10,11... | collective-permute-start | bytes 2408456 | tf_op jit(solution)/shard_map/ppermute | solution.py:44
  125.9 6.1 %collective-permute-start.1 = (bf16[4,112,896]{2,1,0:T(8,128)(2,1)S(1)}, bf16[4,112,896]{2,1,0:T(8,128)(2,1)S(1)}, u32[]{:S(2)}, u32[]{:S(2)}) collective-permute-start(bf16[4,112,896]{2,1,0:T(8,128)(2,1)S(1)} %bitcast.34), channel_id=1, source_target_pairs={{0,1},{1,0},{2,3},{3,2},{4,5},{5,4},{6,7},{7,6},{8,9},{9,8},{10,11... | collective-permute-start | bytes 2408456 | tf_op jit(solution)/shard_map/ppermute | solution.py:52
  158.6 33.5 %all-to-all-start.1 = ((bf16[4,224,576]{2,1,0:T(8,128)(2,1)}), bf16[4,224,576]{2,1,0:T(8,128)(2,1)S(1)}, u32[]{:S(2)}, u32[]{:S(2)}) async-start(bf16[4,224,576]{2,1,0:T(8,128)(2,1)} %bitcast.10), calls=%async_computation.1 | async-start | bytes 2293760 | tf_op jit(solution)/shard_map/all_to_all | solution.py:62
Sparse Core Ops, SparseCore 0:
  31.1 63.5 all-gather.11
  111.6 35.4 all-gather.9

commit v3 on v1

v3 whole, which is shorter than its diff:
```python
import functools
import math

import jax
import jax.numpy as jnp
from jax import lax
from jax.experimental import pallas as pl
from jax.experimental.pallas import tpu as pltpu
from jax.sharding import Mesh
from jax.sharding import PartitionSpec as P

D = 3584
FF = 18432

coef_linear = 3.4445
coef_cubic = -4.775
coef_quintic = 2.0315

SWAP = [(0, 1), (1, 0)]
VMEM = pl.BlockSpec(memory_space=pltpu.VMEM)
SMEM = pl.BlockSpec(memory_space=pltpu.SMEM)


def call(kernel, shape, in_specs, flops):
    size = 2 * math.prod(shape)
    return pl.pallas_call(
        kernel,
        out_shape=jax.ShapeDtypeStruct(shape, jnp.bfloat16),
        in_specs=in_specs,
        out_specs=VMEM,
        compiler_params=pltpu.CompilerParams(vmem_limit_bytes=32 * 1024 * 1024),
        cost_estimate=pl.CostEstimate(flops=flops, bytes_accessed=4 * size, transcendentals=0),
    )


def dot(lhs, rhs, rhs_dim):
    return lax.dot_general(
        lhs, rhs, (((1,), (rhs_dim,)), ((), ())), preferred_element_type=jnp.float32
    )


def gram_kernel(left, right, right_other, out):
    blocks, _, rows, cols = left.shape
    tile = dot(left[:, 0].reshape(blocks * rows, cols), right[...], 1)
    tile += dot(left[:, 1].reshape(blocks * rows, cols), right_other[...], 1)
    out[...] = tile.astype(out.dtype).reshape(out.shape)


def product_kernel(core, mine, other, right, out):
    blocks, rows, inner = mine.shape
    for half, place in ((mine, core[0]), (other, 1 - core[0])):
        half = dot(half[...].reshape(blocks * rows, inner), right[...], 0)
        half = half.astype(out.dtype).reshape(blocks, 1, rows, out.shape[-1])
        out[:, pl.ds(place, 1)] = half


def total(parts):
    return jnp.sum(parts.astype(jnp.float32), axis=0)


def shards(iterate):
    core = lax.axis_index("core")
    rows, cols = iterate.shape
    half = rows // 2
    halves = iterate.reshape(2, half, cols)
    away = lax.dynamic_index_in_dim(halves, 1 - core, 0, keepdims=False)
    kept = lax.dynamic_index_in_dim(halves, core, 0, keepdims=False)
    kept = jnp.stack([kept, lax.ppermute(away, "core", SWAP)])
    right = lax.all_gather(iterate, "z_lo", axis=0).reshape(4 * rows, cols)
    right_other = lax.ppermute(right, "core", SWAP)
    left = lax.all_gather(kept, "y", axis=0)

    tile = call(gram_kernel, (4, half, 4 * rows), [VMEM] * 3, 2 * 4 * half * 4 * rows * 2 * cols)(
        left, right, right_other
    )
    piece = total(lax.all_to_all(tile, "x", 0, 0, tiled=True)).astype(jnp.bfloat16)
    piece = total(lax.all_gather(piece, "z_hi", axis=0)).astype(jnp.bfloat16)
    mine = lax.all_gather(piece, "x", axis=0)
    other = lax.ppermute(mine, "core", SWAP)

    multiply = call(
        product_kernel,
        (4, 2, half, cols),
        [SMEM] + [VMEM] * 3,
        2 * 4 * rows * 4 * rows * cols,
    )
    multiply = functools.partial(multiply, core.astype(jnp.int32).reshape(1), mine, other)

    def gram_times(array):
        parts = multiply(array).reshape(4, rows, cols)
        return total(lax.all_to_all(parts, "y", 0, 0, tiled=True))

    once = gram_times(right)
    gathered = lax.all_gather(once.astype(jnp.bfloat16), "z_lo", axis=0)
    twice = gram_times(gathered.reshape(4 * rows, cols))

    step = coef_linear * iterate.astype(jnp.float32) + coef_cubic * once + coef_quintic * twice
    return (0.2 * math.sqrt(max(D, FF)) * step).astype(jnp.bfloat16)


def solution(mesh):
    axes = ("z_lo", "y", "z_hi", "x", "core")
    fine = Mesh(mesh.devices.reshape(4, 4, 4, 4, 2), axes)
    placed = P(axes[:2], axes[2:])
    return jax.shard_map(
        shards, mesh=fine, in_specs=(placed,), out_specs=placed, check_vma=False
    )
```

time: 196 us -> 186 us (0.949)
  blocking collectives: 163 us -> 156 us
  matrix products: 5.62 us -> 0 us
  Pallas kernels: 0 us -> 4.64 us
    all_to_all x3, blocking collectives: 61.5 us -> 47.5 us  [the longest x2 33.7 us: gram_times(): return total(lax.all_to_all(parts, 'y', 0, 0, tiled=True))]
    all_gather x3, blocking collectives: 38.9 us -> 46.1 us  [the longest x1 21 us: shards(): gathered = lax.all_gather(once.astype(jnp.bfloat16), 'z_lo', axis=0)]
    dot_general x3 -> x0, matrix products: 5.62 us -> none  [product(): lax.dot_general(lhs, rhs, ((contract[:1], contract[1:]), ((), ())), prefe...]
    pallas_call x0 -> x3, Pallas kernels: none -> 4.64 us  [the longest x2 3.06 us: gram_times(): parts = multiply(array).reshape(4, rows, cols)]
    convert_element_type x2 -> x0, local copies, waits for them, and re-layouts: 2.24 us -> none  [the longest x1 1.12 us: shards(): product(gram, right, (1, 0)).astype(jnp.bfloat16).reshape(4, rows, cols)]
    ppermute x0 -> x1, local copies, waits for them, and re-layouts: none -> 2.03 us  [shards(): right_other = lax.ppermute(right, 'core', SWAP)]
    ppermute x1 -> x2, starting transfers between devices: 8.38 us -> 8.07 us  [the longest x1 6.14 us: shards(): right_other = lax.ppermute(right, 'core', SWAP)]
  transfers between devices with their start and end apart: 2 -> 3, of which waited for: 2 -> 2; matrix products, arithmetic and copies ran while one was open for 0% -> 0% of each run, Pallas kernels for 0% -> 0%
where the time goes in v3:
time: 186 us; the launch traced here: 184 us
  blocking collectives  156 us (84%)
  starting transfers between devices  14.7 us (8%)
  Pallas kernels  4.64 us (2%)
  local copies, waits for them, and re-layouts  3.92 us (2%)
  waiting for transfers between devices  3.24 us (2%)
    all_gather x1, blocking collectives, shards(): piece = total(lax.all_gather(piece, 'z_hi', axis=0)).astype(jnp.bfloat16)  38.7 us
    all_to_all x2, blocking collectives, gram_times(): return total(lax.all_to_all(parts, 'y', 0, 0, tiled=True))  33.7 us
    all_gather x1, blocking collectives, shards(): right = lax.all_gather(iterate, 'z_lo', axis=0).reshape(4 * rows, cols)  23.5 us
    all_gather x1, blocking collectives, shards(): gathered = lax.all_gather(once.astype(jnp.bfloat16), 'z_lo', axis=0)  21 us
    all_to_all x1, blocking collectives, shards(): lax.all_to_all(tile, 'x', 0, 0, tiled=True)  13.8 us
    all_gather x1, blocking collectives, shards(): left = lax.all_gather(kept, 'y', axis=0)  13.6 us
    all_gather x1, blocking collectives, shards(): mine = lax.all_gather(piece, 'x', axis=0)  11.5 us
    ppermute x1, starting transfers between devices, shards(): other = lax.ppermute(mine, 'core', SWAP)  6.67 us
  transfers between devices with their start and end apart: 3, of which 2 were waited for; matrix products, arithmetic and copies ran while one was open for 0% of the time, Pallas kernels for 0%

profile of v3, /device:TPU:1, one launch (start us, length us, event | category | flops | bytes accessed | tf_op | source)
XLA Modules:
  0.0 184.0 jit_solution(10861280938322449110)
XLA Ops:
  0.0 23.5 %all-gather.1.right = bf16[896,576]{1,0:T(8,128)(2,1)S(1)} all-gather(bf16[224,576]{1,0:T(8,128)(2,1)} %param.1), channel_id=3, replica_groups=mesh['z_lo'=4,'y'=4,'z_hi'=4,'x'=4,'core'=2] {'z_lo'}, dimensions={0}, use_global_device_ids=true | all-gather | bytes 1290240 | tf_op jit(solution)/shard_map/all_gather | solution.py:69
  23.5 0.0 copy-start
  23.5 1.1 copy.4
  24.6 6.1 %collective-permute-start.1 = (bf16[896,576]{0,1:T(8,128)(2,1)S(1)}, bf16[896,576]{0,1:T(8,128)(2,1)}, u32[]{:S(2)}, u32[]{:S(2)}) collective-permute-start(bf16[896,576]{0,1:T(8,128)(2,1)S(1)} %copy.4), channel_id=1, source_target_pairs={{0,1},{1,0},{2,3},{3,2},{4,5},{5,4},{6,7},{7,6},{8,9},{9,8},{10,11... | collective-permute-start | bytes 3096584 | tf_op jit(solution)/shard_map/ppermute | solution.py:70
  30.8 0.0 copy-done
  30.8 1.9 %collective-permute-start = (bf16[112,576]{1,0:T(8,128)(2,1)S(1)}, bf16[112,576]{1,0:T(8,128)(2,1)S(1)}, u32[]{:S(2)}, u32[]{:S(2)}) collective-permute-start(bf16[112,576]{1,0:T(8,128)(2,1)S(1)} %get-tuple-element.6), channel_id=1, source_target_pairs={{0,1},{1,0},{2,3},{3,2},{4,5},{5,4},{6,7},{7,6},{8,9},{9,8},{10,11... | collective-permute-start | bytes 387080 | tf_op jit(solution)/shard_map/ppermute | solution.py:68
  32.8 1.3 collective-permute-done
  34.1 13.6 %all-gather = bf16[8,112,576]{2,1,0:T(8,128)(2,1)S(1)} all-gather(bf16[2,112,576]{2,1,0:T(8,128)(2,1)S(1)} %pad_maximum_fusion), channel_id=2, replica_groups=mesh['z_lo'=4,'y'=4,'z_hi'=4,'x'=4,'core'=2] {'y'}, dimensions={0}, use_global_device_ids=true | all-gather | bytes 1290240 | tf_op jit(solution)/shard_map/all_gather | solution.py:71
  47.7 0.0 collective-permute-done.1
  47.7 2.0 %copy.5.right_other = bf16[896,576]{1,0:T(8,128)(2,1)S(1)} copy(bf16[896,576]{0,1:T(8,128)(2,1)} %collective-permute-done.1) | data formatting | bytes 2064384 | tf_op jit(solution)/shard_map/ppermute | solution.py:70
  49.7 1.6 shard_map.17
  51.3 13.8 %all_to_all.15 = bf16[4,112,896]{2,1,0:T(8,128)(2,1)S(1)} all-to-all(bf16[4,112,896]{2,1,0:T(8,128)(2,1)S(1)} %shard_map.17), channel_id=1, replica_groups=mesh['z_lo'=4,'y'=4,'z_hi'=4,'x'=4,'core'=2] {'x'}, dimensions={0} | all-to-all | bytes 1605632 | tf_op jit(solution)/shard_map/all_to_all | solution.py:76
  65.1 0.1 reduce_sum.42
  65.2 38.7 %all-gather.2 = bf16[448,896]{1,0:T(8,128)(2,1)S(1)} all-gather(bf16[112,896]{1,0:T(8,128)(2,1)S(1)} %reduce_sum.42), channel_id=4, replica_groups=mesh['z_lo'=4,'y'=4,'z_hi'=4,'x'=4,'core'=2] {'z_hi'}, dimensions={0}, use_global_device_ids=true | all-gather | bytes 1003520 | tf_op jit(solution)/shard_map/all_gather | solution.py:77
  103.9 0.1 reduce_sum.43
  104.1 11.5 %all-gather.3 = bf16[448,896]{1,0:T(8,128)(2,1)S(1)} all-gather(bf16[112,896]{1,0:T(8,128)(2,1)S(1)} %reduce_sum.43), channel_id=5, replica_groups=mesh['z_lo'=4,'y'=4,'z_hi'=4,'x'=4,'core'=2] {'x'}, dimensions={0}, use_global_device_ids=true | all-gather | bytes 1003520 | tf_op jit(solution)/shard_map/all_gather | solution.py:78
  115.5 6.7 %collective-permute-start.2 = (bf16[4,112,896]{2,1,0:T(8,128)(2,1)S(1)}, bf16[4,112,896]{2,1,0:T(8,128)(2,1)S(1)}, u32[]{:S(2)}, u32[]{:S(2)}) collective-permute-start(bf16[4,112,896]{2,1,0:T(8,128)(2,1)S(1)} %bitcast.10), channel_id=1, source_target_pairs={{0,1},{1,0},{2,3},{3,2},{4,5},{5,4},{6,7},{7,6},{8,9},{9,8},{10,11... | collective-permute-start | bytes 2408456 | tf_op jit(solution)/shard_map/ppermute | solution.py:79
  122.2 1.9 %collective-permute-done.2.other = bf16[4,112,896]{2,1,0:T(8,128)(2,1)S(1)} collective-permute-done((bf16[4,112,896]{2,1,0:T(8,128)(2,1)S(1)}, bf16[4,112,896]{2,1,0:T(8,128)(2,1)S(1)}, u32[]{:S(2)}, u32[]{:S(2)}) %collective-permute-start.2) | collective-permute-done | bytes 802848 | tf_op jit(solution)/shard_map/ppermute | solution.py:79
  124.1 1.5 shard_map.18
  125.7 18.6 %all_to_all.16 = bf16[4,224,576]{2,1,0:T(8,128)(2,1)S(1)} all-to-all(bf16[4,224,576]{2,1,0:T(8,128)(2,1)S(1)} %bitcast.15), channel_id=1, replica_groups=mesh['z_lo'=4,'y'=4,'z_hi'=4,'x'=4,'core'=2] {'y'}, dimensions={0} | all-to-all | bytes 2064384 | tf_op jit(solution)/shard_map/all_to_all | solution.py:91
  144.2 0.2 convert_reduce_fusion.1
  144.5 21.0 %all-gather.4.right = bf16[896,576]{1,0:T(8,128)(2,1)S(1)} all-gather(bf16[224,576]{1,0:T(8,128)(2,1)S(1)} %convert_element_type.31), channel_id=6, replica_groups=mesh['z_lo'=4,'y'=4,'z_hi'=4,'x'=4,'core'=2] {'z_lo'}, dimensions={0}, use_global_device_ids=true | all-gather | bytes 1290240 | tf_op jit(solution)/shard_map/all_gather | solution.py:94
  165.5 1.5 shard_map.19
  167.0 15.1 %all_to_all.17 = bf16[4,224,576]{2,1,0:T(8,128)(2,1)S(1)} all-to-all(bf16[4,224,576]{2,1,0:T(8,128)(2,1)S(1)} %bitcast.14), channel_id=1, replica_groups=mesh['z_lo'=4,'y'=4,'z_hi'=4,'x'=4,'core'=2] {'y'}, dimensions={0} | all-to-all | bytes 2064384 | tf_op jit(solution)/shard_map/all_to_all | solution.py:91
  182.1 0.0 copy-start.1
  182.1 0.2 convert_reduce_fusion
  182.3 0.8 copy-done.1
  183.1 0.9 multiply_convert_fusion
  (3 shorter events, 0.1 us)
Async XLA Ops:
  23.5 7.2 %copy-start = (bf16[224,576]{1,0:T(8,128)(2,1)S(1)}, bf16[224,576]{1,0:T(8,128)(2,1)}, u32[]{:S(2)}) copy-start(bf16[224,576]{1,0:T(8,128)(2,1)} %param.1) | copy-start | bytes 774148
  24.6 23.1 %collective-permute-start.1 = (bf16[896,576]{0,1:T(8,128)(2,1)S(1)}, bf16[896,576]{0,1:T(8,128)(2,1)}, u32[]{:S(2)}, u32[]{:S(2)}) collective-permute-start(bf16[896,576]{0,1:T(8,128)(2,1)S(1)} %copy.4), channel_id=1, source_target_pairs={{0,1},{1,0},{2,3},{3,2},{4,5},{5,4},{6,7},{7,6},{8,9},{9,8},{10,11... | collective-permute-start | bytes 3096584 | tf_op jit(solution)/shard_map/ppermute | solution.py:70
  30.8 3.3 %collective-permute-start = (bf16[112,576]{1,0:T(8,128)(2,1)S(1)}, bf16[112,576]{1,0:T(8,128)(2,1)S(1)}, u32[]{:S(2)}, u32[]{:S(2)}) collective-permute-start(bf16[112,576]{1,0:T(8,128)(2,1)S(1)} %get-tuple-element.6), channel_id=1, source_target_pairs={{0,1},{1,0},{2,3},{3,2},{4,5},{5,4},{6,7},{7,6},{8,9},{9,8},{10,11... | collective-permute-start | bytes 387080 | tf_op jit(solution)/shard_map/ppermute | solution.py:68
  115.5 8.6 %collective-permute-start.2 = (bf16[4,112,896]{2,1,0:T(8,128)(2,1)S(1)}, bf16[4,112,896]{2,1,0:T(8,128)(2,1)S(1)}, u32[]{:S(2)}, u32[]{:S(2)}) collective-permute-start(bf16[4,112,896]{2,1,0:T(8,128)(2,1)S(1)} %bitcast.10), channel_id=1, source_target_pairs={{0,1},{1,0},{2,3},{3,2},{4,5},{5,4},{6,7},{7,6},{8,9},{9,8},{10,11... | collective-permute-start | bytes 2408456 | tf_op jit(solution)/shard_map/ppermute | solution.py:79
  182.1 1.0 copy-start.1

commit v4 on v1

v4 whole, which is shorter than its diff:
```python
import math

import jax
import jax.numpy as jnp
from jax import lax
from jax.experimental import pallas as pl
from jax.experimental.pallas import tpu as pltpu
from jax.sharding import Mesh
from jax.sharding import PartitionSpec as P

D = 3584
FF = 18432

coef_linear = 3.4445
coef_cubic = -4.775
coef_quintic = 2.0315

VMEM = pl.BlockSpec(memory_space=pltpu.VMEM)
SMEM = pl.BlockSpec(memory_space=pltpu.SMEM)


def call(kernel, shape, flops, *operands):
    return pl.pallas_call(
        kernel,
        out_shape=jax.ShapeDtypeStruct(shape, jnp.bfloat16),
        in_specs=[SMEM if operand.ndim == 1 else VMEM for operand in operands],
        out_specs=VMEM,
        compiler_params=pltpu.CompilerParams(vmem_limit_bytes=32 * 1024 * 1024),
        cost_estimate=pl.CostEstimate(
            flops=flops, bytes_accessed=8 * math.prod(shape), transcendentals=0
        ),
    )(*operands)


def dot(lhs, rhs, rhs_dim):
    return lax.dot_general(
        lhs, rhs, (((1,), (rhs_dim,)), ((), ())), preferred_element_type=jnp.float32
    )


def gram_kernel(core, left, right, out):
    blocks, cores, rows, cols = left.shape
    half = rows // 2
    start = pl.multiple_of(core[0] * half, 16)
    tile = jnp.zeros((blocks * half, blocks * rows), jnp.float32)
    for k in range(cores):
        lhs = left[:, k, pl.ds(start, half)].reshape(blocks * half, cols)
        tile += dot(lhs, right[:, k].reshape(blocks * rows, cols), 1)
    out[...] = tile.astype(out.dtype).reshape(out.shape)


def product_kernel(core, left, right, out):
    rhs = right[:, pl.ds(core[0], 1)].reshape(left.shape[1], out.shape[1])
    out[...] = dot(left[...], rhs, 0).astype(out.dtype)


def total(parts):
    return jnp.sum(parts.astype(jnp.float32), axis=0)


def gather(array, axes):
    return lax.all_gather(array.astype(jnp.float16), axes, axis=0).astype(jnp.bfloat16)


def shards(iterate):
    core = lax.axis_index("core").astype(jnp.int32).reshape(1)
    rows, cols = iterate.shape
    right = gather(iterate, ("z_lo", "core")).reshape(4, 2, rows, cols)
    left = gather(iterate, ("y", "core")).reshape(4, 2, rows, cols)

    tile = (4, rows // 2, 4 * rows)
    tile = call(gram_kernel, tile, 4 * math.prod(tile) * cols, core, left, right)
    piece = total(lax.all_to_all(tile, "x", 0, 0, tiled=True)).astype(jnp.bfloat16)
    piece = total(lax.all_gather(piece, "z_hi", axis=0)).astype(jnp.bfloat16)
    gram = gather(piece, ("x", "core")).reshape(4 * rows, 4 * rows)

    def gram_times(place, array):
        flops = 2 * gram.size * cols
        parts = call(product_kernel, (4 * rows, cols), flops, place, gram, array)
        return total(lax.all_to_all(parts.reshape(4, rows, cols), "y", 0, 0, tiled=True))

    once = gram_times(core, right)
    gathered = lax.all_gather(once.astype(jnp.bfloat16), "z_lo", axis=0)
    twice = gram_times(jnp.zeros_like(core), gathered.reshape(4, 1, rows, cols))

    step = coef_linear * iterate.astype(jnp.float32) + coef_cubic * once + coef_quintic * twice
    return (0.2 * math.sqrt(max(D, FF)) * step).astype(jnp.bfloat16)


def solution(mesh):
    axes = ("z_lo", "y", "z_hi", "x", "core")
    fine = Mesh(mesh.devices.reshape(4, 4, 4, 4, 2), axes)
    placed = P(axes[:2], axes[2:])
    return jax.shard_map(
        shards, mesh=fine, in_specs=(placed,), out_specs=placed, check_vma=False
    )
```

time: 196 us -> 185 us (0.944)
  starting transfers between devices: 14.2 us -> 0 us
  blocking collectives: 163 us -> 171 us
  matrix products: 5.62 us -> 0 us
  Pallas kernels: 0 us -> 4.66 us
  waiting for transfers between devices: 4.16 us -> 0 us
  local copies, waits for them, and re-layouts: 4.38 us -> 1.65 us
  other arithmetic: 3.02 us -> 5.06 us
    all_gather x4, blocking collectives: 62.6 us -> 81.5 us  [the longest x3 60.5 us: gather(): lax.all_gather(array.astype(jnp.float16), axes, axis=0).astype(jnp.bfloat16)]
    ppermute x2 -> x0, starting transfers between devices: 14.2 us -> none  [the longest x1 8.38 us: shards(): lax.ppermute(away, 'core', SWAP).astype(jnp.float32)]
    all_to_all x3, blocking collectives: 61.5 us -> 49 us  [the longest x2 33.8 us: gram_times(): lax.all_to_all(parts.reshape(4, rows, cols), 'y', 0, 0, tiled=True)]
    dot_general x3 -> x0, matrix products: 5.62 us -> none  [product(): lax.dot_general(lhs, rhs, ((contract[:1], contract[1:]), ((), ())), prefe...]
    pallas_call x0 -> x3, Pallas kernels: none -> 4.66 us  [call(): pl.pallas_call(kernel, out_shape=jax.ShapeDtypeStruct(shape, jnp.bfloat16...]
    ppermute x2 -> x0, waiting for transfers between devices: 4.16 us -> none  [the longest x1 2.26 us: shards(): lax.ppermute(away, 'core', SWAP).astype(jnp.float32)]
    convert_element_type x2 -> x0, local copies, waits for them, and re-layouts: 2.24 us -> none  [the longest x1 1.12 us: shards(): product(gram, right, (1, 0)).astype(jnp.bfloat16).reshape(4, rows, cols)]
    convert_element_type x2 -> x6, other arithmetic: 1.39 us -> 3.6 us  [the longest x3 2.52 us: gather(): lax.all_gather(array.astype(jnp.float16), axes, axis=0).astype(jnp.bfloat16)]
  transfers between devices with their start and end apart: 2 -> 0, of which waited for: 2 -> 0; matrix products, arithmetic and copies ran while one was open for 0% -> 0% of each run, Pallas kernels for 0% -> 0%
where the time goes in v4:
time: 185 us; the launch traced here: 183 us
  blocking collectives  171 us (92%)
  other arithmetic  5.06 us (3%)
  Pallas kernels  4.66 us (3%)
    all_gather x3, blocking collectives, gather(): lax.all_gather(array.astype(jnp.float16), axes, axis=0).astype(jnp.bfloat16)  60.5 us
    all_gather x1, blocking collectives, shards(): piece = total(lax.all_gather(piece, 'z_hi', axis=0)).astype(jnp.bfloat16)  40.6 us
    all_to_all x2, blocking collectives, gram_times(): lax.all_to_all(parts.reshape(4, rows, cols), 'y', 0, 0, tiled=True)  33.8 us
    all_gather x1, blocking collectives, shards(): gathered = lax.all_gather(once.astype(jnp.bfloat16), 'z_lo', axis=0)  21 us
    all_to_all x1, blocking collectives, shards(): lax.all_to_all(tile, 'x', 0, 0, tiled=True)  15.2 us
    pallas_call x3, Pallas kernels, call(): pl.pallas_call(kernel, out_shape=jax.ShapeDtypeStruct(shape, jnp.bfloat16...  4.66 us

profile of v4, /device:TPU:1, one launch (start us, length us, event | category | flops | bytes accessed | tf_op | source)
XLA Modules:
  0.0 182.5 jit_solution(3947521320609598255)
XLA Ops:
  0.0 1.0 convert_element_type.56
  1.0 28.6 %all-gather.8 = f16[1792,576]{1,0:T(8,128)(2,1)S(1)} all-gather(f16[224,576]{1,0:T(8,128)(2,1)S(1)} %convert_element_type.56), channel_id=3, replica_groups=mesh['z_lo'=4,'y'=4,'z_hi'=4,'x'=4,'core'=2] {'z_lo','core'}, dimensions={0}, use_global_device_ids=true | all-gather | bytes 2322432 | tf_op jit(solution)/shard_map/all_gather | solution.py:62
  29.6 16.6 %all-gather.9 = f16[1792,576]{1,0:T(8,128)(2,1)S(1)} all-gather(f16[224,576]{1,0:T(8,128)(2,1)S(1)} %convert_element_type.56), channel_id=2, replica_groups=mesh['z_lo'=4,'y'=4,'z_hi'=4,'x'=4,'core'=2] {'y','core'}, dimensions={0}, use_global_device_ids=true | all-gather | bytes 2322432 | tf_op jit(solution)/shard_map/all_gather | solution.py:62
  46.3 0.4 convert_element_type.68
  46.7 1.8 convert_element_type.67
  48.5 0.0 copy-start
  48.5 1.6 copy-done
  50.2 1.6 shard_map.17
  51.8 15.2 %all_to_all.15 = bf16[4,112,896]{2,1,0:T(8,128)(2,1)S(1)} all-to-all(bf16[4,112,896]{2,1,0:T(8,128)(2,1)S(1)} %shard_map.17), channel_id=1, replica_groups=mesh['z_lo'=4,'y'=4,'z_hi'=4,'x'=4,'core'=2] {'x'}, dimensions={0} | all-to-all | bytes 1605632 | tf_op jit(solution)/shard_map/all_to_all | solution.py:73
  66.9 0.1 reduce_sum.42
  67.1 40.6 %all-gather.2 = bf16[448,896]{1,0:T(8,128)(2,1)S(1)} all-gather(bf16[112,896]{1,0:T(8,128)(2,1)S(1)} %reduce_sum.42), channel_id=4, replica_groups=mesh['z_lo'=4,'y'=4,'z_hi'=4,'x'=4,'core'=2] {'z_hi'}, dimensions={0}, use_global_device_ids=true | all-gather | bytes 1003520 | tf_op jit(solution)/shard_map/all_gather | solution.py:74
  107.7 0.1 reduce_sum.43
  107.8 15.2 %all-gather.10 = f16[896,896]{1,0:T(8,128)(2,1)S(1)} all-gather(f16[112,896]{1,0:T(8,128)(2,1)S(1)} %convert_element_type.59), channel_id=5, replica_groups=mesh['z_lo'=4,'y'=4,'z_hi'=4,'x'=4,'core'=2] {'x','core'}, dimensions={0}, use_global_device_ids=true | all-gather | bytes 1806336 | tf_op jit(solution)/shard_map/all_gather | solution.py:62
  123.1 0.3 convert_element_type.69.left
  123.3 1.5 shard_map.18
  124.9 18.7 %all_to_all.16 = bf16[4,224,576]{2,1,0:T(8,128)(2,1)S(1)} all-to-all(bf16[4,224,576]{2,1,0:T(8,128)(2,1)S(1)} %bitcast.12), channel_id=1, replica_groups=mesh['z_lo'=4,'y'=4,'z_hi'=4,'x'=4,'core'=2] {'y'}, dimensions={0} | all-to-all | bytes 2064384 | tf_op jit(solution)/shard_map/all_to_all | solution.py:80
  143.6 0.2 convert_reduce_fusion.1
  143.8 21.0 %all-gather.4 = bf16[896,576]{1,0:T(8,128)(2,1)S(1)} all-gather(bf16[224,576]{1,0:T(8,128)(2,1)S(1)} %convert_element_type.63), channel_id=6, replica_groups=mesh['z_lo'=4,'y'=4,'z_hi'=4,'x'=4,'core'=2] {'z_lo'}, dimensions={0}, use_global_device_ids=true | all-gather | bytes 1290240 | tf_op jit(solution)/shard_map/all_gather | solution.py:83
  164.8 1.5 shard_map.19
  166.3 0.0 copy-start.1
  166.3 15.2 %all_to_all.17 = bf16[4,224,576]{2,1,0:T(8,128)(2,1)S(1)} all-to-all(bf16[4,224,576]{2,1,0:T(8,128)(2,1)S(1)} %bitcast.11), channel_id=1, replica_groups=mesh['z_lo'=4,'y'=4,'z_hi'=4,'x'=4,'core'=2] {'y'}, dimensions={0} | all-to-all | bytes 2064384 | tf_op jit(solution)/shard_map/all_to_all | solution.py:80
  181.5 0.2 convert_reduce_fusion
  181.7 0.0 copy-done.1
  181.7 0.9 multiply_convert_fusion
  (2 shorter events, 0.1 us)
Async XLA Ops:
  48.5 1.6 copy-start
  166.3 15.3 %copy-start.1 = (bf16[224,576]{1,0:T(8,128)(2,1)S(1)}, bf16[224,576]{1,0:T(8,128)(2,1)}, u32[]{:S(2)}) copy-start(bf16[224,576]{1,0:T(8,128)(2,1)} %param.1) | copy-start | bytes 774148

commit v5 on v4

v5 whole, which is shorter than its diff:
```python
import math

import jax
import jax.numpy as jnp
from jax import lax
from jax.experimental import pallas as pl
from jax.experimental.pallas import tpu as pltpu
from jax.sharding import Mesh
from jax.sharding import PartitionSpec as P

D = 3584
FF = 18432

coef_linear = 3.4445
coef_cubic = -4.775
coef_quintic = 2.0315

VMEM = pl.BlockSpec(memory_space=pltpu.VMEM)


def call(kernel, shape, flops, *operands):
    return pl.pallas_call(
        kernel,
        out_shape=jax.ShapeDtypeStruct(shape, jnp.bfloat16),
        in_specs=[VMEM] * len(operands),
        out_specs=VMEM,
        compiler_params=pltpu.CompilerParams(vmem_limit_bytes=32 * 1024 * 1024),
        cost_estimate=pl.CostEstimate(
            flops=flops, bytes_accessed=8 * math.prod(shape), transcendentals=0
        ),
    )(*operands)


def dot(lhs, rhs, rhs_dim):
    return lax.dot_general(
        lhs, rhs, (((1,), (rhs_dim,)), ((), ())), preferred_element_type=jnp.float32
    )


def copies_kernel(array, out, sems):
    copies = [
        pltpu.make_async_copy(array, out.at[i], sems.at[i]) for i in range(out.shape[0])
    ]
    for copy in copies:
        copy.start()
    for copy in copies:
        copy.wait()


def copies(array, count):
    return pl.pallas_call(
        copies_kernel,
        out_shape=jax.ShapeDtypeStruct((count,) + array.shape, array.dtype),
        in_specs=[pl.BlockSpec(memory_space=pl.ANY)],
        out_specs=pl.BlockSpec(memory_space=pltpu.HBM),
        scratch_shapes=[pltpu.SemaphoreType.DMA((count,))],
    )(array)


def gram_kernel(left, right, out):
    blocks, cores, rows, cols = left.shape
    tile = jnp.zeros((blocks * rows, out.shape[-1]), jnp.float32)
    for k in range(cores):
        lhs = left[:, k].reshape(blocks * rows, cols)
        tile += dot(lhs, right[:, k].reshape(out.shape[-1], cols), 1)
    out[...] = tile.astype(out.dtype).reshape(out.shape)


def product_kernel(left, right, out):
    out[...] = dot(left[...], right[...], 0).astype(out.dtype)


def total(parts):
    return jnp.sum(parts.astype(jnp.float32), axis=0)


def gather(array, axes):
    return lax.all_gather(array.astype(jnp.float16), axes, axis=0)


def shards(iterate):
    rows, cols = iterate.shape
    left = copies(iterate.reshape(2, rows // 2, cols), 4).reshape(8, rows // 2, cols)
    left = lax.all_to_all(left, ("y", "core"), 0, 0, tiled=True)
    left = left.reshape(4, 2, rows // 2, cols)
    right = gather(iterate, ("z_lo", "core")).reshape(4, 2, rows, cols)
    own = lax.dynamic_index_in_dim(right, lax.axis_index("core"), 1, keepdims=False)
    own = own.astype(jnp.bfloat16).reshape(4 * rows, cols)

    tile = (4, rows // 2, 4 * rows)
    flops = 4 * math.prod(tile) * cols
    tile = call(gram_kernel, tile, flops, left, right.astype(jnp.bfloat16))
    piece = total(lax.all_to_all(tile, "x", 0, 0, tiled=True)).astype(jnp.bfloat16)
    piece = total(lax.all_gather(piece, "z_hi", axis=0)).astype(jnp.bfloat16)
    gram = gather(piece, ("x", "core")).astype(jnp.bfloat16).reshape(4 * rows, 4 * rows)

    def gram_times(array):
        flops = 2 * gram.size * cols
        parts = call(product_kernel, array.shape, flops, gram, array)
        return total(lax.all_to_all(parts.reshape(4, rows, cols), "y", 0, 0, tiled=True))

    once = gram_times(own)
    gathered = lax.all_gather(once.astype(jnp.bfloat16), "z_lo", axis=0)
    twice = gram_times(gathered.reshape(4 * rows, cols))

    step = coef_linear * iterate.astype(jnp.float32) + coef_cubic * once + coef_quintic * twice
    return (0.2 * math.sqrt(max(D, FF)) * step).astype(jnp.bfloat16)


def solution(mesh):
    axes = ("z_lo", "y", "z_hi", "x", "core")
    fine = Mesh(mesh.devices.reshape(4, 4, 4, 4, 2), axes)
    placed = P(axes[:2], axes[2:])
    return jax.shard_map(
        shards, mesh=fine, in_specs=(placed,), out_specs=placed, check_vma=False
    )
```

time: 185 us -> 208 us (1.12)
  blocking collectives: 171 us -> 132 us
  Pallas kernels: 4.66 us -> 40.5 us
  starting transfers between devices: 0 us -> 14 us
  waiting for transfers between devices: 0 us -> 11 us
    pallas_call x0 -> x1, Pallas kernels: none -> 35.9 us  [copies(): pl.pallas_call(copies_kernel, out_shape=jax.ShapeDtypeStruct((count,) + a...]
    all_gather x3 -> x2, blocking collectives: 60.5 us -> 39.8 us  [gather(): return lax.all_gather(array.astype(jnp.float16), axes, axis=0)]
    all_to_all x1 -> x0, blocking collectives: 15.2 us -> none  [shards(): lax.all_to_all(tile, 'x', 0, 0, tiled=True)]
    all_to_all x0 -> x2, starting transfers between devices: none -> 14 us  [the longest x1 10.5 us: shards(): left = lax.all_to_all(left, ('y', 'core'), 0, 0, tiled=True)]
    all_to_all x0 -> x2, waiting for transfers between devices: none -> 11 us  [the longest x1 11 us: shards(): lax.all_to_all(tile, 'x', 0, 0, tiled=True)]
    all_gather x1, blocking collectives: 40.6 us -> 38.3 us  [shards(): piece = total(lax.all_gather(piece, 'z_hi', axis=0)).astype(jnp.bfloat16)]
  transfers between devices with their start and end apart: 0 -> 2, of which waited for: 0 -> 1; matrix products, arithmetic and copies ran while one was open for 0% -> 1% of each run, Pallas kernels for 0% -> 0%
where the time goes in v5:
time: 208 us; the launch traced here: 205 us
  blocking collectives  132 us (63%)
  Pallas kernels  40.5 us (19%)
  starting transfers between devices  14 us (7%)
  waiting for transfers between devices  11 us (5%)
  other arithmetic  3.71 us (2%)
  local copies, waits for them, and re-layouts  3.06 us (1%)
    all_gather x2, blocking collectives, gather(): return lax.all_gather(array.astype(jnp.float16), axes, axis=0)  39.8 us
    all_gather x1, blocking collectives, shards(): piece = total(lax.all_gather(piece, 'z_hi', axis=0)).astype(jnp.bfloat16)  38.3 us
    pallas_call x1, Pallas kernels, copies(): pl.pallas_call(copies_kernel, out_shape=jax.ShapeDtypeStruct((count,) + a...  35.9 us
    all_to_all x2, blocking collectives, gram_times(): lax.all_to_all(parts.reshape(4, rows, cols), 'y', 0, 0, tiled=True)  33.5 us
    all_gather x1, blocking collectives, shards(): gathered = lax.all_gather(once.astype(jnp.bfloat16), 'z_lo', axis=0)  20.6 us
    all_to_all x1, waiting for transfers between devices, shards(): lax.all_to_all(tile, 'x', 0, 0, tiled=True)  11 us
    all_to_all x1, starting transfers between devices, shards(): left = lax.all_to_all(left, ('y', 'core'), 0, 0, tiled=True)  10.5 us
    pallas_call x3, Pallas kernels, call(): pl.pallas_call(kernel, out_shape=jax.ShapeDtypeStruct(shape, jnp.bfloat16...  4.65 us
  transfers between devices with their start and end apart: 2, of which 1 were waited for; matrix products, arithmetic and copies ran while one was open for 1% of the time, Pallas kernels for 0%

profile of v5, /device:TPU:1, one launch (start us, length us, event | category | flops | bytes accessed | tf_op | source)
XLA Modules:
  0.0 204.6 jit_solution(16256642178722785154)
XLA Ops:
  0.0 35.9 %shard_map.17 = bf16[4,2,112,576]{3,2,1,0:T(8,128)(2,1)} custom-call(bf16[2,112,576]{2,1,0:T(8,128)(2,1)} %bitcast.16), custom_call_target="tpu_custom_call" | custom-call | tf_op jit(solution)/shard_map/pallas_call | solution.py:51
  35.9 0.0 copy-start.2
  35.9 10.5 %all-to-all-start = ((bf16[8,112,576]{2,1,0:T(8,128)(2,1)}), bf16[8,112,576]{2,1,0:T(8,128)(2,1)S(1)}, u32[]{:S(2)}, u32[]{:S(2)}) async-start(bf16[8,112,576]{2,1,0:T(8,128)(2,1)} %bitcast.14), calls=%async_computation | async-start | bytes 2293760 | tf_op jit(solution)/shard_map/all_to_all | solution.py:84
  46.4 0.0 copy-done.2
  46.4 0.1 convert_element_type.59
  46.4 24.4 %all-gather.6 = f16[1792,576]{1,0:T(8,128)(2,1)S(1)} all-gather(f16[224,576]{1,0:T(8,128)(2,1)S(1)} %convert_element_type.59), channel_id=2, replica_groups=mesh['z_lo'=4,'y'=4,'z_hi'=4,'x'=4,'core'=2] {'z_lo','core'}, dimensions={0}, use_global_device_ids=true | all-gather | bytes 2322432 | tf_op jit(solution)/shard_map/all_gather | solution.py:78
  70.8 0.0 copy-start.1
  70.8 1.4 copy-done.1
  72.2 0.4 convert_element_type.60.right
  72.6 0.0 all-to-all-done
  72.6 1.6 shard_map.18
  74.2 0.0 copy-start
  74.2 0.9 copy-done
  75.1 3.5 %all-to-all-start.1 = ((bf16[4,112,896]{2,1,0:T(8,128)(2,1)}), bf16[4,112,896]{2,1,0:T(8,128)(2,1)S(1)}, u32[]{:S(2)}, u32[]{:S(2)}) async-start(bf16[4,112,896]{2,1,0:T(8,128)(2,1)} %copy-done), calls=%async_computation.1 | async-start | bytes 1605632 | tf_op jit(solution)/shard_map/all_to_all | solution.py:93
  78.6 1.4 dynamic-slice_convert_fusion
  80.1 11.0 %all-to-all-done.1 = bf16[4,112,896]{2,1,0:T(8,128)(2,1)S(1)} async-done(((bf16[4,112,896]{2,1,0:T(8,128)(2,1)}), bf16[4,112,896]{2,1,0:T(8,128)(2,1)S(1)}, u32[]{:S(2)}, u32[]{:S(2)}) %all-to-all-start.1) | async-done | bytes 802848 | tf_op jit(solution)/shard_map/all_to_all | solution.py:93
  91.0 0.1 reduce_sum.42
  91.1 38.3 %all-gather.1 = bf16[448,896]{1,0:T(8,128)(2,1)S(1)} all-gather(bf16[112,896]{1,0:T(8,128)(2,1)S(1)} %reduce_sum.42), channel_id=3, replica_groups=mesh['z_lo'=4,'y'=4,'z_hi'=4,'x'=4,'core'=2] {'z_hi'}, dimensions={0}, use_global_device_ids=true | all-gather | bytes 1003520 | tf_op jit(solution)/shard_map/all_gather | solution.py:94
  129.4 0.1 reduce_sum.43
  129.6 15.4 %all-gather.7 = f16[896,896]{1,0:T(8,128)(2,1)S(1)} all-gather(f16[112,896]{1,0:T(8,128)(2,1)S(1)} %convert_element_type.61), channel_id=4, replica_groups=mesh['z_lo'=4,'y'=4,'z_hi'=4,'x'=4,'core'=2] {'x','core'}, dimensions={0}, use_global_device_ids=true | all-gather | bytes 1806336 | tf_op jit(solution)/shard_map/all_gather | solution.py:78
  145.0 0.3 convert_element_type.71.left
  145.3 1.5 shard_map.19
  146.8 19.3 %all_to_all.20 = bf16[4,224,576]{2,1,0:T(8,128)(2,1)S(1)} all-to-all(bf16[4,224,576]{2,1,0:T(8,128)(2,1)S(1)} %bitcast.11), channel_id=1, replica_groups=mesh['z_lo'=4,'y'=4,'z_hi'=4,'x'=4,'core'=2] {'y'}, dimensions={0} | all-to-all | bytes 2064384 | tf_op jit(solution)/shard_map/all_to_all | solution.py:100
  166.2 0.2 convert_reduce_fusion.1
  166.4 20.6 %all-gather.3.right = bf16[896,576]{1,0:T(8,128)(2,1)S(1)} all-gather(bf16[224,576]{1,0:T(8,128)(2,1)S(1)} %convert_element_type.67), channel_id=5, replica_groups=mesh['z_lo'=4,'y'=4,'z_hi'=4,'x'=4,'core'=2] {'z_lo'}, dimensions={0}, use_global_device_ids=true | all-gather | bytes 1290240 | tf_op jit(solution)/shard_map/all_gather | solution.py:103
  187.0 1.5 shard_map.20
  188.5 14.2 %all_to_all.21 = bf16[4,224,576]{2,1,0:T(8,128)(2,1)S(1)} all-to-all(bf16[4,224,576]{2,1,0:T(8,128)(2,1)S(1)} %bitcast.10), channel_id=1, replica_groups=mesh['z_lo'=4,'y'=4,'z_hi'=4,'x'=4,'core'=2] {'y'}, dimensions={0} | all-to-all | bytes 2064384 | tf_op jit(solution)/shard_map/all_to_all | solution.py:100
  202.8 0.0 copy-start.3
  202.8 0.2 convert_reduce_fusion
  203.0 0.8 copy-done.3
  203.7 0.9 multiply_convert_fusion
  (2 shorter events, 0.1 us)
Async XLA Ops:
  35.9 10.5 %copy-start.2 = (bf16[224,576]{1,0:T(8,128)(2,1)S(1)}, bf16[224,576]{1,0:T(8,128)(2,1)}, u32[]{:S(2)}) copy-start(bf16[224,576]{1,0:T(8,128)(2,1)} %param.1) | copy-start | bytes 774148
  35.9 36.7 %all-to-all-start = ((bf16[8,112,576]{2,1,0:T(8,128)(2,1)}), bf16[8,112,576]{2,1,0:T(8,128)(2,1)S(1)}, u32[]{:S(2)}, u32[]{:S(2)}) async-start(bf16[8,112,576]{2,1,0:T(8,128)(2,1)} %bitcast.14), calls=%async_computation | async-start | bytes 2293760 | tf_op jit(solution)/shard_map/all_to_all | solution.py:84
  70.8 1.4 copy-start.1
  74.2 0.9 copy-start
  75.1 15.9 %all-to-all-start.1 = ((bf16[4,112,896]{2,1,0:T(8,128)(2,1)}), bf16[4,112,896]{2,1,0:T(8,128)(2,1)S(1)}, u32[]{:S(2)}, u32[]{:S(2)}) async-start(bf16[4,112,896]{2,1,0:T(8,128)(2,1)} %copy-done), calls=%async_computation.1 | async-start | bytes 1605632 | tf_op jit(solution)/shard_map/all_to_all | solution.py:93
  202.8 1.0 copy-start.3

commit v6 on v5

--- a/solution.py
+++ b/solution.py
@@ -16,18 +16,19 @@
 coef_quintic = 2.0315
 
 VMEM = pl.BlockSpec(memory_space=pltpu.VMEM)
+SMEM = pl.BlockSpec(memory_space=pltpu.SMEM)
 
 
-def call(kernel, shape, flops, *operands):
+def call(kernel, shapes, flops, *operands):
+    shapes = [jax.ShapeDtypeStruct(shape, jnp.bfloat16) for shape in shapes]
+    size = sum(2 * math.prod(array.shape) for array in (*shapes, *operands))
     return pl.pallas_call(
         kernel,
-        out_shape=jax.ShapeDtypeStruct(shape, jnp.bfloat16),
-        in_specs=[VMEM] * len(operands),
-        out_specs=VMEM,
-        compiler_params=pltpu.CompilerParams(vmem_limit_bytes=32 * 1024 * 1024),
-        cost_estimate=pl.CostEstimate(
-            flops=flops, bytes_accessed=8 * math.prod(shape), transcendentals=0
-        ),
+        out_shape=shapes,
+        in_specs=[SMEM if operand.ndim == 1 else VMEM for operand in operands],
+        out_specs=[VMEM] * len(shapes),
+        compiler_params=pltpu.CompilerParams(vmem_limit_bytes=24 * 1024 * 1024),
+        cost_estimate=pl.CostEstimate(flops=flops, bytes_accessed=size, transcendentals=0),
     )(*operands)
 
 
@@ -37,10 +38,12 @@
     )
 
 
-def copies_kernel(array, out, sems):
-    copies = [
-        pltpu.make_async_copy(array, out.at[i], sems.at[i]) for i in range(out.shape[0])
-    ]
+def copies_kernel(array, out, held, sems):
+    count = out.shape[0]
+    fetch = pltpu.make_async_copy(array, held, sems.at[count])
+    fetch.start()
+    fetch.wait()
+    copies = [pltpu.make_async_copy(held, out.at[i], sems.at[i]) for i in range(count)]
     for copy in copies:
         copy.start()
     for copy in copies:
@@ -53,17 +56,22 @@
         out_shape=jax.ShapeDtypeStruct((count,) + array.shape, array.dtype),
         in_specs=[pl.BlockSpec(memory_space=pl.ANY)],
         out_specs=pl.BlockSpec(memory_space=pltpu.HBM),
-        scratch_shapes=[pltpu.SemaphoreType.DMA((count,))],
+        scratch_shapes=[
+            pltpu.VMEM(array.shape, array.dtype),
+            pltpu.SemaphoreType.DMA((count + 1,)),
+        ],
+        compiler_params=pltpu.CompilerParams(vmem_limit_bytes=8 * 1024 * 1024),
     )(array)
 
 
-def gram_kernel(left, right, out):
+def gram_kernel(core, left, right, out, own):
     blocks, cores, rows, cols = left.shape
     tile = jnp.zeros((blocks * rows, out.shape[-1]), jnp.float32)
     for k in range(cores):
         lhs = left[:, k].reshape(blocks * rows, cols)
         tile += dot(lhs, right[:, k].reshape(out.shape[-1], cols), 1)
     out[...] = tile.astype(out.dtype).reshape(out.shape)
+    own[...] = right[:, pl.ds(core[0], 1)].reshape(own.shape)
 
 
 def product_kernel(left, right, out):
@@ -84,19 +92,18 @@
     left = lax.all_to_all(left, ("y", "core"), 0, 0, tiled=True)
     left = left.reshape(4, 2, rows // 2, cols)
     right = gather(iterate, ("z_lo", "core")).reshape(4, 2, rows, cols)
-    own = lax.dynamic_index_in_dim(right, lax.axis_index("core"), 1, keepdims=False)
-    own = own.astype(jnp.bfloat16).reshape(4 * rows, cols)
 
-    tile = (4, rows // 2, 4 * rows)
-    flops = 4 * math.prod(tile) * cols
-    tile = call(gram_kernel, tile, flops, left, right.astype(jnp.bfloat16))
+    shapes = (4, rows // 2, 4 * rows), (4 * rows, cols)
+    flops = 4 * math.prod(shapes[0]) * cols
+    core = lax.axis_index("core").astype(jnp.int32).reshape(1)
+    tile, own = call(gram_kernel, shapes, flops, core, left, right.astype(jnp.bfloat16))
     piece = total(lax.all_to_all(tile, "x", 0, 0, tiled=True)).astype(jnp.bfloat16)
     piece = total(lax.all_gather(piece, "z_hi", axis=0)).astype(jnp.bfloat16)
     gram = gather(piece, ("x", "core")).astype(jnp.bfloat16).reshape(4 * rows, 4 * rows)
 
     def gram_times(array):
         flops = 2 * gram.size * cols
-        parts = call(product_kernel, array.shape, flops, gram, array)
+        (parts,) = call(product_kernel, [array.shape], flops, gram, array)
         return total(lax.all_to_all(parts.reshape(4, rows, cols), "y", 0, 0, tiled=True))
 
     once = gram_times(own)

time: 208 us -> 174 us (0.84)
  Pallas kernels: 40.5 us -> 5.79 us
  blocking collectives: 132 us -> 148 us
  waiting for transfers between devices: 11 us -> 0.01 us
  starting transfers between devices: 14 us -> 10.5 us
    pallas_call x1, Pallas kernels: 35.9 us -> 1.09 us  [copies(): pl.pallas_call(copies_kernel, out_shape=jax.ShapeDtypeStruct((count,) + a...]
    all_to_all x0 -> x1, blocking collectives: none -> 14.5 us  [shards(): lax.all_to_all(tile, 'x', 0, 0, tiled=True)]
    all_to_all x1 -> x0, waiting for transfers between devices: 11 us -> none  [shards(): lax.all_to_all(tile, 'x', 0, 0, tiled=True)]
    all_to_all x1 -> x0, starting transfers between devices: 3.49 us -> none  [shards(): lax.all_to_all(tile, 'x', 0, 0, tiled=True)]
  transfers between devices with their start and end apart: 2 -> 1, of which waited for: 1 -> 0; matrix products, arithmetic and copies ran while one was open for 1% -> 0% of each run, Pallas kernels for 0% -> 0%
where the time goes in v6:
time: 174 us; the launch traced here: 171 us
  blocking collectives  148 us (85%)
  starting transfers between devices  10.5 us (6%)
  Pallas kernels  5.79 us (3%)
  local copies, waits for them, and re-layouts  3.76 us (2%)
  other arithmetic  2.26 us (1%)
    all_gather x2, blocking collectives, gather(): return lax.all_gather(array.astype(jnp.float16), axes, axis=0)  39.6 us
    all_gather x1, blocking collectives, shards(): piece = total(lax.all_gather(piece, 'z_hi', axis=0)).astype(jnp.bfloat16)  39.5 us
    all_to_all x2, blocking collectives, gram_times(): lax.all_to_all(parts.reshape(4, rows, cols), 'y', 0, 0, tiled=True)  34.1 us
    all_gather x1, blocking collectives, shards(): gathered = lax.all_gather(once.astype(jnp.bfloat16), 'z_lo', axis=0)  20.4 us
    all_to_all x1, blocking collectives, shards(): lax.all_to_all(tile, 'x', 0, 0, tiled=True)  14.5 us
    all_to_all x1, starting transfers between devices, shards(): left = lax.all_to_all(left, ('y', 'core'), 0, 0, tiled=True)  10.5 us
    pallas_call x3, Pallas kernels, call(): pl.pallas_call(kernel, out_shape=shapes, in_specs=[SMEM if operand.ndim =...  4.7 us
    unnamed x10, local copies, waits for them, and re-layouts  3.76 us
  transfers between devices with their start and end apart: 1, of which 0 were waited for; matrix products, arithmetic and copies ran while one was open for 0% of the time, Pallas kernels for 0%

profile of v6, /device:TPU:1, one launch (start us, length us, event | category | flops | bytes accessed | tf_op | source)
XLA Modules:
  0.0 170.6 jit_solution(8200935977785918789)
XLA Ops:
  0.0 0.0 copy-start
  0.0 1.0 copy-done
  1.0 1.1 shard_map.17
  2.1 0.0 copy-start.1
  2.1 10.5 %all-to-all-start = ((bf16[8,112,576]{2,1,0:T(8,128)(2,1)}), bf16[8,112,576]{2,1,0:T(8,128)(2,1)S(1)}, u32[]{:S(2)}, u32[]{:S(2)}) async-start(bf16[8,112,576]{2,1,0:T(8,128)(2,1)} %bitcast.2), calls=%async_computation | async-start | bytes 2293760 | tf_op jit(solution)/shard_map/all_to_all | solution.py:92
  12.6 0.0 copy-done.1
  12.6 0.1 convert_element_type.54
  12.6 24.4 %all-gather.6 = f16[1792,576]{1,0:T(8,128)(2,1)S(1)} all-gather(f16[224,576]{1,0:T(8,128)(2,1)S(1)} %convert_element_type.54), channel_id=2, replica_groups=mesh['z_lo'=4,'y'=4,'z_hi'=4,'x'=4,'core'=2] {'z_lo','core'}, dimensions={0}, use_global_device_ids=true | all-gather | bytes 2322432 | tf_op jit(solution)/shard_map/all_gather | solution.py:86
  37.0 0.4 convert_element_type.65
  37.4 0.0 all-to-all-done
  37.4 1.6 shard_map.18
  39.1 0.0 copy-start.3
  39.1 1.0 copy-done.3
  40.1 14.5 %all_to_all.20 = bf16[4,112,896]{2,1,0:T(8,128)(2,1)S(1)} all-to-all(bf16[4,112,896]{2,1,0:T(8,128)(2,1)S(1)} %get-tuple-element.7), channel_id=1, replica_groups=mesh['z_lo'=4,'y'=4,'z_hi'=4,'x'=4,'core'=2] {'x'}, dimensions={0} | all-to-all | bytes 1605632 | tf_op jit(solution)/shard_map/all_to_all | solution.py:100
  54.6 0.1 reduce_sum.42
  54.7 39.5 %all-gather.1 = bf16[448,896]{1,0:T(8,128)(2,1)S(1)} all-gather(bf16[112,896]{1,0:T(8,128)(2,1)S(1)} %reduce_sum.42), channel_id=3, replica_groups=mesh['z_lo'=4,'y'=4,'z_hi'=4,'x'=4,'core'=2] {'z_hi'}, dimensions={0}, use_global_device_ids=true | all-gather | bytes 1003520 | tf_op jit(solution)/shard_map/all_gather | solution.py:101
  94.3 0.1 reduce_sum.43
  94.4 15.2 %all-gather.7 = f16[896,896]{1,0:T(8,128)(2,1)S(1)} all-gather(f16[112,896]{1,0:T(8,128)(2,1)S(1)} %convert_element_type.57), channel_id=4, replica_groups=mesh['z_lo'=4,'y'=4,'z_hi'=4,'x'=4,'core'=2] {'x','core'}, dimensions={0}, use_global_device_ids=true | all-gather | bytes 1806336 | tf_op jit(solution)/shard_map/all_gather | solution.py:86
  109.7 0.0 copy-start.4
  109.7 0.2 convert_element_type.66.left
  109.9 1.0 copy-done.4
  110.9 1.5 shard_map.19
  112.5 19.7 %all_to_all.21 = bf16[4,224,576]{2,1,0:T(8,128)(2,1)S(1)} all-to-all(bf16[4,224,576]{2,1,0:T(8,128)(2,1)S(1)} %bitcast.11), channel_id=1, replica_groups=mesh['z_lo'=4,'y'=4,'z_hi'=4,'x'=4,'core'=2] {'y'}, dimensions={0} | all-to-all | bytes 2064384 | tf_op jit(solution)/shard_map/all_to_all | solution.py:107
  132.2 0.2 convert_reduce_fusion.1
  132.4 20.4 %all-gather.3.right = bf16[896,576]{1,0:T(8,128)(2,1)S(1)} all-gather(bf16[224,576]{1,0:T(8,128)(2,1)S(1)} %convert_element_type.61), channel_id=5, replica_groups=mesh['z_lo'=4,'y'=4,'z_hi'=4,'x'=4,'core'=2] {'z_lo'}, dimensions={0}, use_global_device_ids=true | all-gather | bytes 1290240 | tf_op jit(solution)/shard_map/all_gather | solution.py:110
  152.8 1.5 shard_map.20
  154.4 14.4 %all_to_all.22 = bf16[4,224,576]{2,1,0:T(8,128)(2,1)S(1)} all-to-all(bf16[4,224,576]{2,1,0:T(8,128)(2,1)S(1)} %bitcast.10), channel_id=1, replica_groups=mesh['z_lo'=4,'y'=4,'z_hi'=4,'x'=4,'core'=2] {'y'}, dimensions={0} | all-to-all | bytes 2064384 | tf_op jit(solution)/shard_map/all_to_all | solution.py:107
  168.8 0.0 copy-start.2
  168.8 0.2 convert_reduce_fusion
  169.0 0.8 copy-done.2
  169.7 0.9 multiply_convert_fusion
  (2 shorter events, 0.1 us)
Async XLA Ops:
  0.0 1.0 copy-start
  2.1 10.5 %copy-start.1 = (bf16[224,576]{1,0:T(8,128)(2,1)S(1)}, bf16[224,576]{1,0:T(8,128)(2,1)}, u32[]{:S(2)}) copy-start(bf16[224,576]{1,0:T(8,128)(2,1)} %param.1) | copy-start | bytes 774148
  2.1 35.4 %all-to-all-start = ((bf16[8,112,576]{2,1,0:T(8,128)(2,1)}), bf16[8,112,576]{2,1,0:T(8,128)(2,1)S(1)}, u32[]{:S(2)}, u32[]{:S(2)}) async-start(bf16[8,112,576]{2,1,0:T(8,128)(2,1)} %bitcast.2), calls=%async_computation | async-start | bytes 2293760 | tf_op jit(solution)/shard_map/all_to_all | solution.py:92
  39.1 1.0 copy-start.3
  109.7 1.3 copy-start.4
  168.8 1.0 copy-start.2

commit v7 on v2

v7 whole, which is shorter than its diff:
```python
import math

import jax
import jax.numpy as jnp
from jax import lax
from jax.experimental import pallas as pl
from jax.experimental.pallas import tpu as pltpu
from jax.sharding import Mesh
from jax.sharding import PartitionSpec as P

D = 3584
FF = 18432

coef_linear = 3.4445
coef_cubic = -4.775
coef_quintic = 2.0315

VMEM = pl.BlockSpec(memory_space=pltpu.VMEM)
SMEM = pl.BlockSpec(memory_space=pltpu.SMEM)
HBM = pl.BlockSpec(memory_space=pltpu.HBM)
ANY = pl.BlockSpec(memory_space=pl.ANY)

SAME_Y = [[4 * y + (s - y) % 4 for s in range(4)] for y in range(4)]
SAME_X = [[4 * ((s - x) % 4) + x for s in range(4)] for x in range(4)]
SAME_S = [[4 * y + (s - y) % 4 for y in range(4)] for s in range(4)]


def with_cores(groups):
    return [[2 * chip + core for chip in group for core in range(2)] for group in groups]


def call(kernel, operands, outputs, scratch=(), flops=0):
    arrays, in_specs = zip(*operands)
    shapes, out_specs = zip(*outputs)
    shapes = [jax.ShapeDtypeStruct(shape, jnp.bfloat16) for shape in shapes]
    size = sum(2 * math.prod(array.shape) for array in (*shapes, *arrays))
    return pl.pallas_call(
        kernel,
        out_shape=shapes,
        in_specs=in_specs,
        out_specs=out_specs,
        scratch_shapes=scratch,
        compiler_params=pltpu.CompilerParams(vmem_limit_bytes=24 * 1024 * 1024),
        cost_estimate=pl.CostEstimate(flops=flops, bytes_accessed=size, transcendentals=0),
    )(*arrays)


def dot(lhs, rhs, contract=(1, 0)):
    return lax.dot_general(
        lhs, rhs, ((contract[:1], contract[1:]), ((), ())), preferred_element_type=jnp.float32
    )


def start_copies(source, out, sems):
    copies = [pltpu.make_async_copy(source, out.at[i], sems.at[i]) for i in range(out.shape[0])]
    for copy in copies:
        copy.start()
    return copies


def wait(copies):
    for copy in copies:
        copy.wait()


def copies_kernel(array, out, sems):
    wait(start_copies(array, out, sems))


def gram_kernel(core, left, right, tile, spread, sems):
    copies = start_copies(right.at[:, core[0]], spread, sems)
    blocks, cores, rows, cols = left.shape
    sums = jnp.zeros((blocks * rows, tile.shape[-1]), jnp.float32)
    for k in range(cores):
        lhs = left[:, k].reshape(blocks * rows, cols)
        sums += dot(lhs, right[:, k].reshape(tile.shape[-1], cols), (1, 1))
    tile[...] = sums.astype(tile.dtype).reshape(tile.shape)
    wait(copies)


def piece_kernel(parts, piece, spread, sems):
    piece[...] = jnp.sum(parts[...].astype(jnp.float32), axis=0).astype(piece.dtype)
    wait(start_copies(piece, spread, sems))


def first_kernel(band, whole, out, held, sems):
    blocks, cores, rows, inner = band.shape
    copies = [pltpu.make_async_copy(whole.at[y], held.at[y], sems.at[y]) for y in range(blocks)]
    for copy in copies:
        copy.start()
    sums = jnp.zeros((cores * rows, out.shape[-1]), jnp.float32)
    for y in range(blocks):
        copies[y].wait()
        sums += dot(band[y].reshape(cores * rows, inner), held[y])
    out[...] = sums.astype(out.dtype)


def second_kernel(tile, once, out):
    out[...] = dot(tile[...], once[...], (0, 0)).astype(out.dtype)


def total(parts):
    return jnp.sum(parts.astype(jnp.float32), axis=0)


def gather(array, axes, groups=None):
    array = array.astype(jnp.float16)
    array = lax.all_gather(array, axes, axis=0, axis_index_groups=groups)
    return array.astype(jnp.bfloat16)


def exchange(array, axes, groups=None):
    return lax.all_to_all(array, axes, 0, 0, tiled=True, axis_index_groups=groups)


def shards(iterate):
    rows, cols = iterate.shape
    half, plane = rows // 2, ("y", "x", "core")
    core = lax.axis_index("core").astype(jnp.int32).reshape(1)
    sems = pltpu.SemaphoreType.DMA

    halves = iterate.reshape(2, half, cols)
    (left,) = call(
        copies_kernel, [(halves, VMEM)], [((4, 2, half, cols), HBM)], [sems((4,))]
    )
    left = exchange(left.reshape(8, half, cols), ("y", "core")).reshape(4, 2, half, cols)
    right = gather(iterate, ("z_lo", "core")).reshape(4, 2, rows, cols)

    tile, spread = call(
        gram_kernel,
        [(core, SMEM), (left, VMEM), (right, VMEM)],
        [((4, half, 4 * rows), VMEM), ((4, 4, rows, cols), HBM)],
        [sems((4,))],
        flops=4 * 4 * half * 4 * rows * cols,
    )
    whole = exchange(spread, "y").reshape(4, 4 * rows, cols)
    piece = total(exchange(tile, ("y", "x"), SAME_Y)).astype(jnp.bfloat16)
    piece, spread = call(
        piece_kernel,
        [(lax.all_gather(piece, "z_hi", axis=0), VMEM)],
        [((half, 4 * rows), VMEM), ((8, half, 4 * rows), HBM)],
        [sems((8,))],
    )

    tile = exchange(spread, plane, with_cores(SAME_Y)).reshape(4 * rows, 4 * rows)
    band = gather(piece, plane, with_cores(SAME_S)).reshape(4, 2, half, 4 * rows)
    (once,) = call(
        first_kernel,
        [(band, VMEM), (whole, ANY)],
        [((rows, cols), VMEM)],
        [pltpu.VMEM(whole.shape, whole.dtype), sems((4,))],
        flops=2 * rows * 16 * rows * cols,
    )
    once = lax.all_gather(once, ("y", "x"), axis=0, axis_index_groups=SAME_X)
    (parts,) = call(
        second_kernel,
        [(tile, VMEM), (once.reshape(4 * rows, cols), VMEM)],
        [((4 * rows, cols), VMEM)],
        flops=2 * tile.size * cols,
    )
    twice = total(exchange(parts.reshape(4, rows, cols), "z_lo"))
    once = lax.dynamic_index_in_dim(once, lax.axis_index("y"), 0, keepdims=False)

    step = coef_linear * iterate.astype(jnp.float32) + coef_cubic * once.astype(jnp.float32)
    step = step + coef_quintic * twice
    return (0.2 * math.sqrt(max(D, FF)) * step).astype(jnp.bfloat16)


def solution(mesh):
    axes = ("z_lo", "y", "z_hi", "x", "core")
    fine = Mesh(mesh.devices.reshape(4, 4, 4, 4, 2), axes)
    placed = P(axes[:2], axes[2:])
    return jax.shard_map(
        shards, mesh=fine, in_specs=(placed,), out_specs=placed, check_vma=False
    )
```

time: 200 us -> 206 us (1.030)
  between operations: 13.5 us -> 0.13 us
  Pallas kernels: 0 us -> 10.5 us
  matrix products: 8.14 us -> 0 us
  starting transfers between devices: 17.1 us -> 24.6 us
  waiting for transfers between devices: 31.4 us -> 36.2 us
  blocking collectives: 124 us -> 127 us
    all_to_all x1 -> x4, starting transfers between devices: 6.22 us -> 24.6 us  [exchange(): lax.all_to_all(array, axes, 0, 0, tiled=True, axis_index_groups=groups)]
    ppermute x2 -> x0, starting transfers between devices: 10.8 us -> none  [the longest x1 6.63 us: shards(): lax.ppermute(away, 'core', SWAP).astype(jnp.float32)]
    pallas_call x0 -> x5, Pallas kernels: none -> 10.5 us  [call(): pl.pallas_call(kernel, out_shape=shapes, in_specs=in_specs, out_specs=out...]
    all_to_all x1 -> x4, waiting for transfers between devices: 27.3 us -> 36.2 us  [exchange(): lax.all_to_all(array, axes, 0, 0, tiled=True, axis_index_groups=groups)]
    dot_general x3 -> x0, matrix products: 8.14 us -> none  [product(): lax.dot_general(lhs, rhs, ((contract[:1], contract[1:]), ((), ())), prefe...]
    unnamed x5 -> x12, local copies, waits for them, and re-layouts: 0.21 us -> 5.25 us
    ppermute x2 -> x0, waiting for transfers between devices: 4.03 us -> none  [the longest x1 2.12 us: shards(): lax.ppermute(away, 'core', SWAP).astype(jnp.float32)]
    all_gather x4 -> x3, blocking collectives: 92.2 us -> 94.5 us  [the longest x2 55.1 us: gather(): array = lax.all_gather(array, axes, axis=0, axis_index_groups=groups)]
  transfers between devices with their start and end apart: 5 -> 4, of which waited for: 3 -> 2; matrix products, arithmetic and copies ran while one was open for 4% -> 0% of each run, Pallas kernels for 0% -> 3%
where the time goes in v7:
time: 206 us; the launch traced here: 205 us
  blocking collectives  127 us (62%)
  waiting for transfers between devices  36.2 us (18%)
  starting transfers between devices  24.6 us (12%)
  Pallas kernels  10.5 us (5%)
  local copies, waits for them, and re-layouts  5.25 us (3%)
    all_gather x2, blocking collectives, gather(): array = lax.all_gather(array, axes, axis=0, axis_index_groups=groups)  55.1 us
    all_gather x1, blocking collectives, shards(): lax.all_gather(piece, 'z_hi', axis=0)  39.4 us
    all_to_all x4, waiting for transfers between devices, exchange(): lax.all_to_all(array, axes, 0, 0, tiled=True, axis_index_groups=groups)  36.2 us
    all_to_all x4, starting transfers between devices, exchange(): lax.all_to_all(array, axes, 0, 0, tiled=True, axis_index_groups=groups)  24.6 us
    all_gather x1, blocking collectives, shards(): once = lax.all_gather(once, ('y', 'x'), axis=0, axis_index_groups=SAME_X)  17.5 us
    all_to_all x1, blocking collectives, exchange(): lax.all_to_all(array, axes, 0, 0, tiled=True, axis_index_groups=groups)  14.5 us
    pallas_call x5, Pallas kernels, call(): pl.pallas_call(kernel, out_shape=shapes, in_specs=in_specs, out_specs=out...  10.5 us
    unnamed x12, local copies, waits for them, and re-layouts  5.25 us
  transfers between devices with their start and end apart: 4, of which 2 were waited for; matrix products, arithmetic and copies ran while one was open for 0% of the time, Pallas kernels for 3%

profile of v7, /device:TPU:1, one launch (start us, length us, event | category | flops | bytes accessed | tf_op | source)
XLA Modules:
  0.0 205.2 jit_solution(5603441896626035547)
XLA Ops:
  0.0 1.0 copy-done.2
  1.0 1.1 shard_map.17
  2.0 10.4 %all-to-all-start = ((bf16[8,112,576]{2,1,0:T(8,128)(2,1)}), bf16[8,112,576]{2,1,0:T(8,128)(2,1)S(1)}, u32[]{:S(2)}, u32[]{:S(2)}) async-start(bf16[8,112,576]{2,1,0:T(8,128)(2,1)} %bitcast.2), calls=%async_computation | async-start | bytes 2293760 | tf_op jit(solution)/shard_map/all_to_all | solution.py:113
  12.4 0.0 copy-done.3
  12.4 0.1 convert_element_type.28
  12.4 24.4 %all-gather.6 = f16[1792,576]{1,0:T(8,128)(2,1)S(1)} all-gather(f16[224,576]{1,0:T(8,128)(2,1)S(1)} %convert_element_type.28), channel_id=2, replica_groups=mesh['z_lo'=4,'y'=4,'z_hi'=4,'x'=4,'core'=2] {'z_lo','core'}, dimensions={0}, use_global_device_ids=true | all-gather | bytes 2322432 | tf_op jit(solution)/shard_map/all_gather | solution.py:108
  36.8 0.4 convert_element_type.35
  37.2 0.0 all-to-all-done
  37.2 2.0 shard_map.18
  39.3 0.0 copy-start
  39.3 2.1 %copy-done = bf16[4,4,224,576]{3,2,1,0:T(8,128)(2,1)} copy-done((bf16[4,4,224,576]{3,2,1,0:T(8,128)(2,1)}, bf16[4,4,224,576]{3,2,1,0:T(8,128)(2,1)S(1)}, u32[]{:S(2)}) %copy-start) | copy-done | bytes 4128792
  41.4 14.5 %all_to_all.25 = bf16[4,112,896]{2,1,0:T(8,128)(2,1)S(1)} all-to-all(bf16[4,112,896]{2,1,0:T(8,128)(2,1)S(1)} %get-tuple-element.9), channel_id=1, replica_groups={{0,2,4,6},{38,32,34,36},{68,70,64,66},{98,100,102,96},{1,3,5,7},{39,33,..., dimensions={0} | all-to-all | bytes 1605632 | tf_op jit(solution)/shard_map/all_to_all | solution.py:113
  55.9 4.9 %all-to-all-start.2 = ((bf16[4,4,224,576]{3,2,1,0:T(8,128)(2,1)}), bf16[4,4,224,576]{3,2,1,0:T(8,128)(2,1)}, u32[]{:S(2)}, u32[]{:S(2)}) async-start(bf16[4,4,224,576]{3,2,1,0:T(8,128)(2,1)} %copy-done), calls=%async_computation.2 | async-start | bytes 9175040 | tf_op jit(solution)/shard_map/all_to_all | solution.py:113
  60.9 0.1 reduce_sum.21
  61.0 39.4 %all-gather.1 = bf16[448,896]{1,0:T(8,128)(2,1)S(1)} all-gather(bf16[112,896]{1,0:T(8,128)(2,1)S(1)} %reduce_sum.21), channel_id=3, replica_groups=mesh['z_lo'=4,'y'=4,'z_hi'=4,'x'=4,'core'=2] {'z_hi'}, dimensions={0}, use_global_device_ids=true | all-gather | bytes 1003520 | tf_op jit(solution)/shard_map/all_gather | solution.py:140
  100.4 2.2 %shard_map.19 = (bf16[112,896]{1,0:T(8,128)(2,1)S(1)}, bf16[8,112,896]{2,1,0:T(8,128)(2,1)S(1)}) custom-call(bf16[4,112,896]{2,1,0:T(8,128)(2,1)S(1)} %bitcast.25), custom_call_target="tpu_custom_call" | custom-call | bytes 2609152 | tf_op jit(solution)/shard_map/pallas_call | solution.py:37
  102.7 0.0 copy-start.5
  102.7 1.2 copy-done.5
  103.8 8.9 %all-to-all-done.2 = bf16[4,4,224,576]{3,2,1,0:T(8,128)(2,1)} async-done(((bf16[4,4,224,576]{3,2,1,0:T(8,128)(2,1)}), bf16[4,4,224,576]{3,2,1,0:T(8,128)(2,1)}, u32[]{:S(2)}, u32[]{:S(2)}) %all-to-all-start.2) | async-done | bytes 4128800 | tf_op jit(solution)/shard_map/all_to_all | solution.py:113
  112.7 5.7 %all-to-all-start.3 = ((bf16[8,112,896]{2,1,0:T(8,128)(2,1)}), bf16[8,112,896]{2,1,0:T(8,128)(2,1)S(1)}, u32[]{:S(2)}, u32[]{:S(2)}) async-start(bf16[8,112,896]{2,1,0:T(8,128)(2,1)} %copy-done.5), calls=%async_computation.3 | async-start | bytes 3211264 | tf_op jit(solution)/shard_map/all_to_all | solution.py:113
  118.4 30.8 %all-gather.7 = f16[896,896]{1,0:T(8,128)(2,1)S(1)} all-gather(f16[112,896]{1,0:T(8,128)(2,1)S(1)} %convert_element_type.30), channel_id=4, replica_groups={{0,1,38,39,68,69,98,99},{2,3,32,33,70,71,100,101},{4,5,34,35,64,65,102,..., dimensions={0}, use_global_device_ids=true | all-gather | bytes 1806336 | tf_op jit(solution)/shard_map/all_gather | solution.py:108
  149.2 0.3 convert_element_type.36
  149.5 3.5 %shard_map.20 = bf16[224,576]{1,0:T(8,128)(2,1)S(1)} custom-call(bf16[4,2,112,896]{3,2,1,0:T(8,128)(2,1)S(1)} %bitcast.20, bf16[4,896,576]{2,1,0:T(8,128)(2,1)} %bitcast.7.whole), custom_call_target="tpu_custom_call" | custom-call | flops 924844032 | bytes 5992448 | tf_op jit(solution)/shard_map/pallas_call | solution.py:37
  153.0 17.5 %all-gather.3.once = bf16[896,576]{1,0:T(8,128)(2,1)S(1)} all-gather(bf16[224,576]{1,0:T(8,128)(2,1)S(1)} %shard_map.20), channel_id=5, replica_groups={{0,32,64,96},{98,2,34,66},{68,100,4,36},{38,70,102,6},{1,33,65,97},{99,..., dimensions={0}, use_global_device_ids=true | all-gather | bytes 1290240 | tf_op jit(solution)/shard_map/all_gather | solution.py:154
  170.6 0.0 all-to-all-done.3
  170.6 1.6 shard_map.21
  172.1 0.0 copy-start.1
  172.2 1.0 copy-done.1
  173.2 3.7 %all-to-all-start.4 = ((bf16[4,224,576]{2,1,0:T(8,128)(2,1)}), bf16[4,224,576]{2,1,0:T(8,128)(2,1)S(1)}, u32[]{:S(2)}, u32[]{:S(2)}) async-start(bf16[4,224,576]{2,1,0:T(8,128)(2,1)} %bitcast.24), calls=%async_computation.4 | async-start | bytes 2293760 | tf_op jit(solution)/shard_map/all_to_all | solution.py:113
  176.8 27.3 %all-to-all-done.4 = bf16[4,224,576]{2,1,0:T(8,128)(2,1)S(1)} async-done(((bf16[4,224,576]{2,1,0:T(8,128)(2,1)}), bf16[4,224,576]{2,1,0:T(8,128)(2,1)S(1)}, u32[]{:S(2)}, u32[]{:S(2)}) %all-to-all-start.4) | async-done | bytes 1032224 | tf_op jit(solution)/shard_map/all_to_all | solution.py:113
  204.1 0.2 convert_reduce_fusion
  204.3 0.9 fusion.2
  (5 shorter events, 0.0 us)
Async XLA Ops:
  0.0 1.0 copy-start.2
  1.0 11.4 %copy-start.3 = (bf16[224,576]{1,0:T(8,128)(2,1)S(1)}, bf16[224,576]{1,0:T(8,128)(2,1)}, u32[]{:S(2)}) copy-start(bf16[224,576]{1,0:T(8,128)(2,1)} %param.1) | copy-start | bytes 774148
  2.0 35.2 %all-to-all-start = ((bf16[8,112,576]{2,1,0:T(8,128)(2,1)}), bf16[8,112,576]{2,1,0:T(8,128)(2,1)S(1)}, u32[]{:S(2)}, u32[]{:S(2)}) async-start(bf16[8,112,576]{2,1,0:T(8,128)(2,1)} %bitcast.2), calls=%async_computation | async-start | bytes 2293760 | tf_op jit(solution)/shard_map/all_to_all | solution.py:113
  39.3 2.1 %copy-start = (bf16[4,4,224,576]{3,2,1,0:T(8,128)(2,1)}, bf16[4,4,224,576]{3,2,1,0:T(8,128)(2,1)S(1)}, u32[]{:S(2)}) copy-start(bf16[4,4,224,576]{3,2,1,0:T(8,128)(2,1)S(1)} %get-tuple-element.11) | copy-start | bytes 12386308
  55.9 56.8 %all-to-all-start.2 = ((bf16[4,4,224,576]{3,2,1,0:T(8,128)(2,1)}), bf16[4,4,224,576]{3,2,1,0:T(8,128)(2,1)}, u32[]{:S(2)}, u32[]{:S(2)}) async-start(bf16[4,4,224,576]{3,2,1,0:T(8,128)(2,1)} %copy-done), calls=%async_computation.2 | async-start | bytes 9175040 | tf_op jit(solution)/shard_map/all_to_all | solution.py:113
  102.7 1.2 copy-start.5
  112.7 57.8 %all-to-all-start.3 = ((bf16[8,112,896]{2,1,0:T(8,128)(2,1)}), bf16[8,112,896]{2,1,0:T(8,128)(2,1)S(1)}, u32[]{:S(2)}, u32[]{:S(2)}) async-start(bf16[8,112,896]{2,1,0:T(8,128)(2,1)} %copy-done.5), calls=%async_computation.3 | async-start | bytes 3211264 | tf_op jit(solution)/shard_map/all_to_all | solution.py:113
  172.1 1.0 copy-start.1
  173.2 31.1 %copy-start.4 = (bf16[224,576]{1,0:T(8,128)(2,1)S(1)}, bf16[224,576]{1,0:T(8,128)(2,1)}, u32[]{:S(2)}) copy-start(bf16[224,576]{1,0:T(8,128)(2,1)} %param.1) | copy-start | bytes 774148
  173.2 31.0 %all-to-all-start.4 = ((bf16[4,224,576]{2,1,0:T(8,128)(2,1)}), bf16[4,224,576]{2,1,0:T(8,128)(2,1)S(1)}, u32[]{:S(2)}, u32[]{:S(2)}) async-start(bf16[4,224,576]{2,1,0:T(8,128)(2,1)} %bitcast.24), calls=%async_computation.4 | async-start | bytes 2293760 | tf_op jit(solution)/shard_map/all_to_all | solution.py:113

commit v8 on v1

v8 whole, which is shorter than its diff:
```python
import math

import jax
import jax.numpy as jnp
from jax import lax
from jax.experimental import pallas as pl
from jax.experimental.pallas import tpu as pltpu
from jax.sharding import Mesh
from jax.sharding import PartitionSpec as P

D = 3584
FF = 18432

coef_linear = 3.4445
coef_cubic = -4.775
coef_quintic = 2.0315

SWAP = [(0, 1), (1, 0)]
VMEM = pl.BlockSpec(memory_space=pltpu.VMEM)
SMEM = pl.BlockSpec(memory_space=pltpu.SMEM)
HBM = pl.BlockSpec(memory_space=pltpu.HBM)
ANY = pl.BlockSpec(memory_space=pl.ANY)


def call(kernel, operands, output, spec=VMEM, scratch=(), flops=0):
    arrays, in_specs = zip(*operands)
    return pl.pallas_call(
        kernel,
        out_shape=output,
        in_specs=in_specs,
        out_specs=spec,
        scratch_shapes=scratch,
        compiler_params=pltpu.CompilerParams(vmem_limit_bytes=24 * 1024 * 1024),
        cost_estimate=pl.CostEstimate(
            flops=flops,
            bytes_accessed=2 * sum(math.prod(array.shape) for array in (output, *arrays)),
            transcendentals=0,
        ),
    )(*arrays)


def bf16(*shape):
    return jax.ShapeDtypeStruct(shape, jnp.bfloat16)


def f32(*shape):
    return jax.ShapeDtypeStruct(shape, jnp.float32)


def dot(lhs, rhs, rhs_dim):
    return lax.dot_general(
        lhs, rhs, (((1,), (rhs_dim,)), ((), ())), preferred_element_type=jnp.float32
    )


def copies_kernel(array, out, held, sems):
    count = out.shape[0]
    fetch = pltpu.make_async_copy(array, held, sems.at[count])
    fetch.start()
    fetch.wait()
    copies = [pltpu.make_async_copy(held, out.at[i], sems.at[i]) for i in range(count)]
    for copy in copies:
        copy.start()
    for copy in copies:
        copy.wait()


def gram_kernel(which, left, right, out):
    blocks, rows, cols = left.shape
    half = rows // 2
    start = pl.multiple_of(which[0] * half, 16)
    lhs = left[:, pl.ds(start, half)].reshape(blocks * half, cols)
    tile = dot(lhs, right[...].reshape(out.shape[-1], cols), 1)
    out[...] = tile.astype(out.dtype).reshape(out.shape)


def product_kernel(left, right, out, held, sems):
    blocks, rows, cols = right.shape
    copies = [pltpu.make_async_copy(right.at[i], held.at[i], sems.at[i]) for i in range(blocks)]
    for copy in copies:
        copy.start()
    sums = jnp.zeros(out.shape, jnp.float32)
    for i in range(blocks):
        copies[i].wait()
        sums += dot(left[:, i * rows : (i + 1) * rows], held[i], 0)
    out[...] = sums.astype(out.dtype)


def update_kernel(iterate, once, parts, out, held, sem):
    fetch = pltpu.make_async_copy(iterate, held, sem)
    fetch.start()
    step = coef_cubic * once[...]
    step += coef_quintic * jnp.sum(parts[...].astype(jnp.float32), axis=0)
    fetch.wait()
    step += coef_linear * held[...].astype(jnp.float32)
    out[...] = (0.2 * math.sqrt(max(D, FF)) * step).astype(out.dtype)


def total(parts):
    return jnp.sum(parts.astype(jnp.float32), axis=0)


def exchange(array, axes):
    return lax.all_to_all(array, axes, 0, 0, tiled=True)


def shards(iterate):
    rows, cols = iterate.shape
    half = rows // 2
    core = lax.axis_index("core").astype(jnp.int32).reshape(1)
    sems = pltpu.SemaphoreType.DMA

    left = call(
        copies_kernel,
        [(iterate, ANY)],
        bf16(4, rows, cols),
        spec=HBM,
        scratch=[pltpu.VMEM(iterate.shape, iterate.dtype), sems((5,))],
    )
    left = exchange(left, "y")
    right = lax.all_gather(iterate, "z_lo", axis=0)

    def half_tile(which, output):
        operands = [(which, SMEM), (left, VMEM), (right, VMEM)]
        return call(gram_kernel, operands, output, flops=2 * 4 * half * 4 * rows * cols)

    shape = (4, half, 4 * rows)
    away = lax.ppermute(half_tile(1 - core, bf16(*shape)), "core", SWAP)
    tile = (half_tile(core, f32(*shape)) + away.astype(jnp.float32)).astype(jnp.bfloat16)
    piece = total(exchange(tile, "x")).astype(jnp.bfloat16)
    piece = total(lax.all_gather(piece, "z_hi", axis=0)).astype(jnp.bfloat16)
    gram = lax.all_gather(piece.astype(jnp.float16), ("x", "core"), axis=0)
    gram = gram.astype(jnp.bfloat16).reshape(4 * rows, 4 * rows)

    def gram_times(array):
        parts = call(
            product_kernel,
            [(gram, VMEM), (array, ANY)],
            bf16(4 * rows, cols),
            scratch=[pltpu.VMEM(array.shape, array.dtype), sems((4,))],
            flops=2 * gram.size * cols,
        )
        return exchange(parts.reshape(4, rows, cols), "y")

    once = total(gram_times(right))
    twice = gram_times(lax.all_gather(once.astype(jnp.bfloat16), "z_lo", axis=0))
    return call(
        update_kernel,
        [(iterate, ANY), (once, VMEM), (twice, VMEM)],
        bf16(rows, cols),
        scratch=[pltpu.VMEM(iterate.shape, iterate.dtype), sems],
    )


def solution(mesh):
    axes = ("z_lo", "y", "z_hi", "x", "core")
    fine = Mesh(mesh.devices.reshape(4, 4, 4, 4, 2), axes)
    placed = P(axes[:2], axes[2:])
    return jax.shard_map(
        shards, mesh=fine, in_specs=(placed,), out_specs=placed, check_vma=False
    )
```

time: 196 us -> 176 us (0.90)
  blocking collectives: 163 us -> 150 us
  Pallas kernels: 0 us -> 9.4 us
  matrix products: 5.62 us -> 0 us
  local copies, waits for them, and re-layouts: 4.38 us -> 0.96 us
  starting transfers between devices: 14.2 us -> 10.9 us
  waiting for transfers between devices: 4.16 us -> 1.03 us
  other arithmetic: 3.02 us -> 0.91 us
    all_to_all x3, blocking collectives: 61.5 us -> 51.5 us  [exchange(): return lax.all_to_all(array, axes, 0, 0, tiled=True)]
    pallas_call x0 -> x6, Pallas kernels: none -> 9.4 us  [call(): pl.pallas_call(kernel, out_shape=output, in_specs=in_specs, out_specs=spe...]
    ppermute x2 -> x1, starting transfers between devices: 14.2 us -> 5.77 us  [shards(): away = lax.ppermute(half_tile(1 - core, bf16(*shape)), 'core', SWAP)]
    dot_general x3 -> x0, matrix products: 5.62 us -> none  [product(): lax.dot_general(lhs, rhs, ((contract[:1], contract[1:]), ((), ())), prefe...]
    all_to_all x0 -> x1, starting transfers between devices: none -> 5.16 us  [exchange(): return lax.all_to_all(array, axes, 0, 0, tiled=True)]
    all_gather x4 -> x3, blocking collectives: 62.6 us -> 58.7 us  [the longest x1 22.5 us: shards(): right = lax.all_gather(iterate, 'z_lo', axis=0)]
    ppermute x2 -> x1, waiting for transfers between devices: 4.16 us -> 1.03 us  [shards(): away = lax.ppermute(half_tile(1 - core, bf16(*shape)), 'core', SWAP)]
    convert_element_type x2 -> x0, local copies, waits for them, and re-layouts: 2.24 us -> none  [the longest x1 1.12 us: shards(): product(gram, right, (1, 0)).astype(jnp.bfloat16).reshape(4, rows, cols)]
  transfers between devices with their start and end apart: 2 -> 2, of which waited for: 2 -> 1; matrix products, arithmetic and copies ran while one was open for 0% -> 0% of each run, Pallas kernels for 0% -> 1%
where the time goes in v8:
time: 176 us; the launch traced here: 173 us
  blocking collectives  150 us (85%)
  starting transfers between devices  10.9 us (6%)
  Pallas kernels  9.4 us (5%)
    all_to_all x3, blocking collectives, exchange(): return lax.all_to_all(array, axes, 0, 0, tiled=True)  51.5 us
    all_gather x1, blocking collectives, shards(): piece = total(lax.all_gather(piece, 'z_hi', axis=0)).astype(jnp.bfloat16)  40 us
    all_gather x1, blocking collectives, shards(): right = lax.all_gather(iterate, 'z_lo', axis=0)  22.5 us
    all_gather x1, blocking collectives, shards(): lax.all_gather(once.astype(jnp.bfloat16), 'z_lo', axis=0)  20.4 us
    all_gather x1, blocking collectives, shards(): gram = lax.all_gather(piece.astype(jnp.float16), ('x', 'core'), axis=0)  15.7 us
    pallas_call x6, Pallas kernels, call(): pl.pallas_call(kernel, out_shape=output, in_specs=in_specs, out_specs=spe...  9.4 us
    ppermute x1, starting transfers between devices, shards(): away = lax.ppermute(half_tile(1 - core, bf16(*shape)), 'core', SWAP)  5.77 us
    all_to_all x1, starting transfers between devices, exchange(): return lax.all_to_all(array, axes, 0, 0, tiled=True)  5.16 us
  transfers between devices with their start and end apart: 2, of which 1 were waited for; matrix products, arithmetic and copies ran while one was open for 0% of the time, Pallas kernels for 1%

profile of v8, /device:TPU:1, one launch (start us, length us, event | category | flops | bytes accessed | tf_op | source)
XLA Modules:
  0.0 173.5 jit_solution(6439735046676844639)
XLA Ops:
  0.0 0.0 copy-start
  0.0 1.0 copy-done
  1.0 1.1 shard_map.17
  2.1 0.0 copy-start.1
  2.1 5.2 %all-to-all-start = ((bf16[4,224,576]{2,1,0:T(8,128)(2,1)}), bf16[4,224,576]{2,1,0:T(8,128)(2,1)S(1)}, u32[]{:S(2)}, u32[]{:S(2)}) async-start(bf16[4,224,576]{2,1,0:T(8,128)(2,1)} %shard_map.17), calls=%async_computation | async-start | bytes 2293760 | tf_op jit(solution)/shard_map/all_to_all | solution.py:104
  7.2 0.0 copy-done.1
  7.2 22.5 %all-gather = bf16[896,576]{1,0:T(8,128)(2,1)S(1)} all-gather(bf16[224,576]{1,0:T(8,128)(2,1)S(1)} %copy-done.1), channel_id=2, replica_groups=mesh['z_lo'=4,'y'=4,'z_hi'=4,'x'=4,'core'=2] {'z_lo'}, dimensions={0}, use_global_device_ids=true | all-gather | bytes 1290240 | tf_op jit(solution)/shard_map/all_gather | solution.py:121
  29.8 0.0 all-to-all-done.left
  29.8 0.9 shard_map.19
  30.6 5.8 %collective-permute-start = (bf16[4,112,896]{2,1,0:T(8,128)(2,1)S(1)}, bf16[4,112,896]{2,1,0:T(8,128)(2,1)S(1)}, u32[]{:S(2)}, u32[]{:S(2)}) collective-permute-start(bf16[4,112,896]{2,1,0:T(8,128)(2,1)S(1)} %shard_map.19), channel_id=1, source_target_pairs={{0,1},{1,0},{2,3},{3,2},{4,5},{5,4},{6,7},{7,6},{8,9},{9,8},{10,11... | collective-permute-start | bytes 2408456 | tf_op jit(solution)/shard_map/ppermute | solution.py:128
  36.4 0.9 shard_map.18
  37.3 1.0 collective-permute-done
  38.3 0.2 add_convert_fusion
  38.5 15.2 %all_to_all.20 = bf16[4,112,896]{2,1,0:T(8,128)(2,1)S(1)} all-to-all(bf16[4,112,896]{2,1,0:T(8,128)(2,1)S(1)} %add_convert_fusion), channel_id=1, replica_groups=mesh['z_lo'=4,'y'=4,'z_hi'=4,'x'=4,'core'=2] {'x'}, dimensions={0} | all-to-all | bytes 1605632 | tf_op jit(solution)/shard_map/all_to_all | solution.py:104
  53.7 0.1 reduce_sum.33
  53.9 40.0 %all-gather.1 = bf16[448,896]{1,0:T(8,128)(2,1)S(1)} all-gather(bf16[112,896]{1,0:T(8,128)(2,1)S(1)} %reduce_sum.33), channel_id=3, replica_groups=mesh['z_lo'=4,'y'=4,'z_hi'=4,'x'=4,'core'=2] {'z_hi'}, dimensions={0}, use_global_device_ids=true | all-gather | bytes 1003520 | tf_op jit(solution)/shard_map/all_gather | solution.py:131
  93.9 0.1 reduce_sum.34
  94.1 15.7 %all-gather.5 = f16[896,896]{1,0:T(8,128)(2,1)S(1)} all-gather(f16[112,896]{1,0:T(8,128)(2,1)S(1)} %convert_element_type.44), channel_id=4, replica_groups=mesh['z_lo'=4,'y'=4,'z_hi'=4,'x'=4,'core'=2] {'x','core'}, dimensions={0}, use_global_device_ids=true | all-gather | bytes 1806336 | tf_op jit(solution)/shard_map/all_gather | solution.py:132
  109.8 0.3 convert_element_type.50.left
  110.0 2.7 %shard_map.20 = bf16[896,576]{1,0:T(8,128)(2,1)S(1)} custom-call(bf16[896,896]{1,0:T(8,128)(2,1)S(1)} %convert_element_type.50.left, bf16[4,224,576]{2,1,0:T(8,128)(2,1)S(1)} %bitcast.8), custom_call_target="tpu_custom_call" | custom-call | flops 924844032 | bytes 3670016 | tf_op jit(solution)/shard_map/pallas_call | solution.py:27
  112.7 21.1 %all_to_all.21 = bf16[4,224,576]{2,1,0:T(8,128)(2,1)S(1)} all-to-all(bf16[4,224,576]{2,1,0:T(8,128)(2,1)S(1)} %bitcast.11), channel_id=1, replica_groups=mesh['z_lo'=4,'y'=4,'z_hi'=4,'x'=4,'core'=2] {'y'}, dimensions={0} | all-to-all | bytes 2064384 | tf_op jit(solution)/shard_map/all_to_all | solution.py:104
  133.8 0.2 convert_reduce_fusion.once
  134.1 20.4 %all-gather.3 = bf16[896,576]{1,0:T(8,128)(2,1)S(1)} all-gather(bf16[224,576]{1,0:T(8,128)(2,1)S(1)} %convert_element_type.48), channel_id=5, replica_groups=mesh['z_lo'=4,'y'=4,'z_hi'=4,'x'=4,'core'=2] {'z_lo'}, dimensions={0}, use_global_device_ids=true | all-gather | bytes 1290240 | tf_op jit(solution)/shard_map/all_gather | solution.py:146
  154.5 2.7 %shard_map.21 = bf16[896,576]{1,0:T(8,128)(2,1)S(1)} custom-call(bf16[896,896]{1,0:T(8,128)(2,1)S(1)} %convert_element_type.50.left, bf16[4,224,576]{2,1,0:T(8,128)(2,1)S(1)} %bitcast.9), custom_call_target="tpu_custom_call" | custom-call | flops 924844032 | bytes 3670016 | tf_op jit(solution)/shard_map/pallas_call | solution.py:27
  157.2 15.1 %all_to_all.22.parts = bf16[4,224,576]{2,1,0:T(8,128)(2,1)S(1)} all-to-all(bf16[4,224,576]{2,1,0:T(8,128)(2,1)S(1)} %bitcast.10), channel_id=1, replica_groups=mesh['z_lo'=4,'y'=4,'z_hi'=4,'x'=4,'core'=2] {'y'}, dimensions={0} | all-to-all | bytes 2064384 | tf_op jit(solution)/shard_map/all_to_all | solution.py:104
  172.3 1.2 shard_map.22
  (2 shorter events, 0.1 us)
Async XLA Ops:
  0.0 1.0 copy-start
  2.1 5.2 %copy-start.1 = (bf16[224,576]{1,0:T(8,128)(2,1)S(1)}, bf16[224,576]{1,0:T(8,128)(2,1)}, u32[]{:S(2)}) copy-start(bf16[224,576]{1,0:T(8,128)(2,1)} %iterate.1) | copy-start | bytes 774148
  2.1 27.7 %all-to-all-start = ((bf16[4,224,576]{2,1,0:T(8,128)(2,1)}), bf16[4,224,576]{2,1,0:T(8,128)(2,1)S(1)}, u32[]{:S(2)}, u32[]{:S(2)}) async-start(bf16[4,224,576]{2,1,0:T(8,128)(2,1)} %shard_map.17), calls=%async_computation | async-start | bytes 2293760 | tf_op jit(solution)/shard_map/all_to_all | solution.py:104
  30.6 7.7 %collective-permute-start = (bf16[4,112,896]{2,1,0:T(8,128)(2,1)S(1)}, bf16[4,112,896]{2,1,0:T(8,128)(2,1)S(1)}, u32[]{:S(2)}, u32[]{:S(2)}) collective-permute-start(bf16[4,112,896]{2,1,0:T(8,128)(2,1)S(1)} %shard_map.19), channel_id=1, source_target_pairs={{0,1},{1,0},{2,3},{3,2},{4,5},{5,4},{6,7},{7,6},{8,9},{9,8},{10,11... | collective-permute-start | bytes 2408456 | tf_op jit(solution)/shard_map/ppermute | solution.py:128

commit v9 on v8

v9 whole, which is shorter than its diff:
```python
import math

import jax
import jax.numpy as jnp
from jax import lax
from jax.experimental import pallas as pl
from jax.experimental.pallas import tpu as pltpu
from jax.sharding import Mesh
from jax.sharding import PartitionSpec as P

D = 3584
FF = 18432

coef_linear = 3.4445
coef_cubic = -4.775
coef_quintic = 2.0315

VMEM = pl.BlockSpec(memory_space=pltpu.VMEM)
SMEM = pl.BlockSpec(memory_space=pltpu.SMEM)
HBM = pl.BlockSpec(memory_space=pltpu.HBM)
ANY = pl.BlockSpec(memory_space=pl.ANY)


def call(kernel, operands, output, spec=VMEM, scratch=(), flops=0):
    arrays, in_specs = zip(*operands)
    return pl.pallas_call(
        kernel,
        out_shape=output,
        in_specs=in_specs,
        out_specs=spec,
        scratch_shapes=scratch,
        compiler_params=pltpu.CompilerParams(vmem_limit_bytes=24 * 1024 * 1024),
        cost_estimate=pl.CostEstimate(
            flops=flops,
            bytes_accessed=2 * sum(math.prod(array.shape) for array in (output, *arrays)),
            transcendentals=0,
        ),
    )(*arrays)


def bf16(*shape):
    return jax.ShapeDtypeStruct(shape, jnp.bfloat16)


def dot(lhs, rhs, rhs_dim):
    return lax.dot_general(
        lhs, rhs, (((1,), (rhs_dim,)), ((), ())), preferred_element_type=jnp.float32
    )


def copies_kernel(array, out, sems):
    copies = [pltpu.make_async_copy(array, out.at[i], sems.at[i]) for i in range(out.shape[0])]
    for copy in copies:
        copy.start()
    for copy in copies:
        copy.wait()


def gram_kernel(left, right, out):
    blocks, cores, rows, cols = left.shape
    tile = jnp.zeros((blocks * rows, out.shape[-1]), jnp.float32)
    for k in range(cores):
        lhs = left[:, k].reshape(blocks * rows, cols)
        tile += dot(lhs, right[:, k].reshape(out.shape[-1], cols), 1)
    out[...] = tile.astype(out.dtype).reshape(out.shape)


def own_kernel(core, right, out):
    out[...] = right[:, pl.ds(core[0], 1)].reshape(out.shape)


def product_kernel(left, right, out):
    out[...] = dot(left[...], right[...], 0).astype(out.dtype)


def update_kernel(iterate, once, parts, out, held, sem):
    fetch = pltpu.make_async_copy(iterate, held, sem)
    fetch.start()
    step = coef_cubic * once[...]
    step += coef_quintic * jnp.sum(parts[...].astype(jnp.float32), axis=0)
    fetch.wait()
    step += coef_linear * held[...].astype(jnp.float32)
    out[...] = (0.2 * math.sqrt(max(D, FF)) * step).astype(out.dtype)


def total(parts):
    return jnp.sum(parts.astype(jnp.float32), axis=0)


def gather(array, axes):
    return lax.all_gather(array.astype(jnp.float16), axes, axis=0).astype(jnp.bfloat16)


def exchange(array, axes):
    return lax.all_to_all(array, axes, 0, 0, tiled=True)


def shards(iterate):
    rows, cols = iterate.shape
    half = rows // 2
    core = lax.axis_index("core").astype(jnp.int32).reshape(1)
    sems = pltpu.SemaphoreType.DMA

    left = call(
        copies_kernel,
        [(iterate.reshape(2, half, cols), VMEM)],
        bf16(4, 2, half, cols),
        spec=HBM,
        scratch=[sems((4,))],
    )
    left = exchange(left.reshape(8, half, cols), ("y", "core")).reshape(4, 2, half, cols)
    right = gather(iterate, ("z_lo", "core")).reshape(4, 2, rows, cols)
    own = call(own_kernel, [(core, SMEM), (right, VMEM)], bf16(4 * rows, cols))

    tile = call(
        gram_kernel,
        [(left, VMEM), (right, VMEM)],
        bf16(4, half, 4 * rows),
        flops=4 * 4 * half * 4 * rows * cols,
    )
    piece = total(exchange(tile, "x")).astype(jnp.bfloat16)
    piece = total(lax.all_gather(piece, "z_hi", axis=0)).astype(jnp.bfloat16)
    gram = gather(piece, ("x", "core")).reshape(4 * rows, 4 * rows)

    def gram_times(array):
        parts = call(
            product_kernel,
            [(gram, VMEM), (array, VMEM)],
            bf16(4 * rows, cols),
            flops=2 * gram.size * cols,
        )
        return exchange(parts.reshape(4, rows, cols), "y")

    once = total(gram_times(own))
    gathered = lax.all_gather(once.astype(jnp.bfloat16), "z_lo", axis=0)
    twice = gram_times(gathered.reshape(4 * rows, cols))
    return call(
        update_kernel,
        [(iterate, ANY), (once, VMEM), (twice, VMEM)],
        bf16(rows, cols),
        scratch=[pltpu.VMEM(iterate.shape, iterate.dtype), sems],
    )


def solution(mesh):
    axes = ("z_lo", "y", "z_hi", "x", "core")
    fine = Mesh(mesh.devices.reshape(4, 4, 4, 4, 2), axes)
    placed = P(axes[:2], axes[2:])
    return jax.shard_map(
        shards, mesh=fine, in_specs=(placed,), out_specs=placed, check_vma=False
    )
```

time: 176 us -> 174 us (0.989)
  blocking collectives: 150 us -> 133 us
  waiting for transfers between devices: 1.03 us -> 12.4 us
  starting transfers between devices: 10.9 us -> 14.7 us
  Pallas kernels: 9.4 us -> 6.97 us
    all_to_all x3 -> x2, blocking collectives: 51.5 us -> 34.5 us  [exchange(): return lax.all_to_all(array, axes, 0, 0, tiled=True)]
    all_to_all x1 -> x2, waiting for transfers between devices: 0.01 us -> 12.4 us  [exchange(): return lax.all_to_all(array, axes, 0, 0, tiled=True)]
    all_to_all x1 -> x2, starting transfers between devices: 5.16 us -> 14.7 us  [exchange(): return lax.all_to_all(array, axes, 0, 0, tiled=True)]
    ppermute x1 -> x0, starting transfers between devices: 5.77 us -> none  [shards(): away = lax.ppermute(half_tile(1 - core, bf16(*shape)), 'core', SWAP)]
    pallas_call x6, Pallas kernels: 9.4 us -> 6.97 us  [call(): pl.pallas_call(kernel, out_shape=output, in_specs=in_specs, out_specs=spe...]
    all_gather x1, blocking collectives: 40 us -> 38.1 us  [shards(): piece = total(lax.all_gather(piece, 'z_hi', axis=0)).astype(jnp.bfloat16)]
  transfers between devices with their start and end apart: 2 -> 2, of which waited for: 1 -> 1; matrix products, arithmetic and copies ran while one was open for 0% -> 0% of each run, Pallas kernels for 1% -> 0%
where the time goes in v9:
time: 174 us; the launch traced here: 171 us
  blocking collectives  133 us (76%)
  starting transfers between devices  14.7 us (8%)
  waiting for transfers between devices  12.4 us (7%)
  Pallas kernels  6.97 us (4%)
  other arithmetic  2.39 us (1%)
  local copies, waits for them, and re-layouts  1.86 us (1%)
    all_gather x2, blocking collectives, gather(): lax.all_gather(array.astype(jnp.float16), axes, axis=0).astype(jnp.bfloat16)  39.7 us
    all_gather x1, blocking collectives, shards(): piece = total(lax.all_gather(piece, 'z_hi', axis=0)).astype(jnp.bfloat16)  38.1 us
    all_to_all x2, blocking collectives, exchange(): return lax.all_to_all(array, axes, 0, 0, tiled=True)  34.5 us
    all_gather x1, blocking collectives, shards(): gathered = lax.all_gather(once.astype(jnp.bfloat16), 'z_lo', axis=0)  20.4 us
    all_to_all x2, starting transfers between devices, exchange(): return lax.all_to_all(array, axes, 0, 0, tiled=True)  14.7 us
    all_to_all x2, waiting for transfers between devices, exchange(): return lax.all_to_all(array, axes, 0, 0, tiled=True)  12.4 us
    pallas_call x6, Pallas kernels, call(): pl.pallas_call(kernel, out_shape=output, in_specs=in_specs, out_specs=spe...  6.97 us
  transfers between devices with their start and end apart: 2, of which 1 were waited for; matrix products, arithmetic and copies ran while one was open for 0% of the time, Pallas kernels for 0%

profile of v9, /device:TPU:1, one launch (start us, length us, event | category | flops | bytes accessed | tf_op | source)
XLA Modules:
  0.0 171.1 jit_solution(5340659677926911872)
XLA Ops:
  0.0 0.0 copy-start.1
  0.0 1.0 copy-done.1
  1.0 1.0 shard_map.17
  2.0 0.0 copy-start.2
  2.0 10.5 %all-to-all-start = ((bf16[8,112,576]{2,1,0:T(8,128)(2,1)}), bf16[8,112,576]{2,1,0:T(8,128)(2,1)S(1)}, u32[]{:S(2)}, u32[]{:S(2)}) async-start(bf16[8,112,576]{2,1,0:T(8,128)(2,1)} %bitcast.1), calls=%async_computation | async-start | bytes 2293760 | tf_op jit(solution)/shard_map/all_to_all | solution.py:95
  12.5 0.0 copy-done.2
  12.5 0.1 convert_element_type.42
  12.6 24.4 %all-gather.6 = f16[1792,576]{1,0:T(8,128)(2,1)S(1)} all-gather(f16[224,576]{1,0:T(8,128)(2,1)S(1)} %convert_element_type.42), channel_id=2, replica_groups=mesh['z_lo'=4,'y'=4,'z_hi'=4,'x'=4,'core'=2] {'z_lo','core'}, dimensions={0}, use_global_device_ids=true | all-gather | bytes 2322432 | tf_op jit(solution)/shard_map/all_gather | solution.py:91
  36.9 0.4 convert_element_type.50
  37.4 0.0 all-to-all-done
  37.4 1.6 shard_map.18
  39.0 0.0 copy-start
  39.0 0.9 copy-done
  39.9 4.2 %all-to-all-start.1 = ((bf16[4,112,896]{2,1,0:T(8,128)(2,1)}), bf16[4,112,896]{2,1,0:T(8,128)(2,1)}, u32[]{:S(2)}, u32[]{:S(2)}) async-start(bf16[4,112,896]{2,1,0:T(8,128)(2,1)} %copy-done), calls=%async_computation.1 | async-start | bytes 1605632 | tf_op jit(solution)/shard_map/all_to_all | solution.py:95
  44.1 0.1 shard_map.19.right
  44.2 12.4 %all-to-all-done.1 = bf16[4,112,896]{2,1,0:T(8,128)(2,1)} async-done(((bf16[4,112,896]{2,1,0:T(8,128)(2,1)}), bf16[4,112,896]{2,1,0:T(8,128)(2,1)}, u32[]{:S(2)}, u32[]{:S(2)}) %all-to-all-start.1) | async-done | bytes 802848 | tf_op jit(solution)/shard_map/all_to_all | solution.py:95
  56.6 1.3 reduce_sum.33
  57.8 38.1 %all-gather.1 = bf16[448,896]{1,0:T(8,128)(2,1)S(1)} all-gather(bf16[112,896]{1,0:T(8,128)(2,1)S(1)} %reduce_sum.33), channel_id=3, replica_groups=mesh['z_lo'=4,'y'=4,'z_hi'=4,'x'=4,'core'=2] {'z_hi'}, dimensions={0}, use_global_device_ids=true | all-gather | bytes 1003520 | tf_op jit(solution)/shard_map/all_gather | solution.py:122
  95.9 0.1 reduce_sum.34
  96.1 15.3 %all-gather.7 = f16[896,896]{1,0:T(8,128)(2,1)S(1)} all-gather(f16[112,896]{1,0:T(8,128)(2,1)S(1)} %convert_element_type.44), channel_id=4, replica_groups=mesh['z_lo'=4,'y'=4,'z_hi'=4,'x'=4,'core'=2] {'x','core'}, dimensions={0}, use_global_device_ids=true | all-gather | bytes 1806336 | tf_op jit(solution)/shard_map/all_gather | solution.py:91
  111.4 0.3 convert_element_type.51.left
  111.6 1.5 shard_map.20
  113.2 19.6 %all_to_all.20 = bf16[4,224,576]{2,1,0:T(8,128)(2,1)S(1)} all-to-all(bf16[4,224,576]{2,1,0:T(8,128)(2,1)S(1)} %bitcast.12), channel_id=1, replica_groups=mesh['z_lo'=4,'y'=4,'z_hi'=4,'x'=4,'core'=2] {'y'}, dimensions={0} | all-to-all | bytes 2064384 | tf_op jit(solution)/shard_map/all_to_all | solution.py:95
  132.8 0.2 convert_reduce_fusion.once
  133.0 20.4 %all-gather.3.right = bf16[896,576]{1,0:T(8,128)(2,1)S(1)} all-gather(bf16[224,576]{1,0:T(8,128)(2,1)S(1)} %convert_element_type.48), channel_id=5, replica_groups=mesh['z_lo'=4,'y'=4,'z_hi'=4,'x'=4,'core'=2] {'z_lo'}, dimensions={0}, use_global_device_ids=true | all-gather | bytes 1290240 | tf_op jit(solution)/shard_map/all_gather | solution.py:135
  153.4 1.5 shard_map.21
  155.0 0.0 copy-start.3
  155.0 14.9 %all_to_all.21.parts = bf16[4,224,576]{2,1,0:T(8,128)(2,1)S(1)} all-to-all(bf16[4,224,576]{2,1,0:T(8,128)(2,1)S(1)} %bitcast.11), channel_id=1, replica_groups=mesh['z_lo'=4,'y'=4,'z_hi'=4,'x'=4,'core'=2] {'y'}, dimensions={0} | all-to-all | bytes 2064384 | tf_op jit(solution)/shard_map/all_to_all | solution.py:95
  169.9 0.0 copy-done.3
  169.9 1.2 shard_map.22
  (2 shorter events, 0.1 us)
Async XLA Ops:
  0.0 1.0 copy-start.1
  2.0 10.5 %copy-start.2 = (bf16[224,576]{1,0:T(8,128)(2,1)S(1)}, bf16[224,576]{1,0:T(8,128)(2,1)}, u32[]{:S(2)}) copy-start(bf16[224,576]{1,0:T(8,128)(2,1)} %iterate.1) | copy-start | bytes 774148
  2.0 35.3 %all-to-all-start = ((bf16[8,112,576]{2,1,0:T(8,128)(2,1)}), bf16[8,112,576]{2,1,0:T(8,128)(2,1)S(1)}, u32[]{:S(2)}, u32[]{:S(2)}) async-start(bf16[8,112,576]{2,1,0:T(8,128)(2,1)} %bitcast.1), calls=%async_computation | async-start | bytes 2293760 | tf_op jit(solution)/shard_map/all_to_all | solution.py:95
  39.0 0.9 copy-start
  39.9 16.7 %all-to-all-start.1 = ((bf16[4,112,896]{2,1,0:T(8,128)(2,1)}), bf16[4,112,896]{2,1,0:T(8,128)(2,1)}, u32[]{:S(2)}, u32[]{:S(2)}) async-start(bf16[4,112,896]{2,1,0:T(8,128)(2,1)} %copy-done), calls=%async_computation.1 | async-start | bytes 1605632 | tf_op jit(solution)/shard_map/all_to_all | solution.py:95
  155.0 14.9 %copy-start.3 = (bf16[224,576]{1,0:T(8,128)(2,1)S(1)}, bf16[224,576]{1,0:T(8,128)(2,1)}, u32[]{:S(2)}) copy-start(bf16[224,576]{1,0:T(8,128)(2,1)} %iterate.1) | copy-start | bytes 774148

commit v10 on v9

--- a/solution.py
+++ b/solution.py
@@ -15,6 +15,7 @@
 coef_cubic = -4.775
 coef_quintic = 2.0315
 
+LANES = 128
 VMEM = pl.BlockSpec(memory_space=pltpu.VMEM)
 SMEM = pl.BlockSpec(memory_space=pltpu.SMEM)
 HBM = pl.BlockSpec(memory_space=pltpu.HBM)
@@ -69,18 +70,43 @@
     out[...] = right[:, pl.ds(core[0], 1)].reshape(out.shape)
 
 
-def product_kernel(left, right, out):
-    out[...] = dot(left[...], right[...], 0).astype(out.dtype)
+def pieces(rows, cols):
+    whole, rest = cols // LANES, cols % LANES
+    for k in range(whole):
+        yield slice(0, rows), slice(k * LANES, (k + 1) * LANES), slice(k * rows, (k + 1) * rows), slice(0, LANES)
+    each = rows * rest // LANES
+    for k in range(LANES // rest if rest else 0):
+        columns = slice(k * rest, (k + 1) * rest)
+        yield slice(k * each, (k + 1) * each), slice(whole * LANES, cols), slice(whole * rows, whole * rows + each), columns
+
+
+def first_kernel(left, right, out):
+    product = dot(left[...], right[...], 0).astype(out.dtype)
+    rows = product.shape[0] // out.shape[0]
+    for i in range(out.shape[0]):
+        block = product[i * rows : (i + 1) * rows]
+        for row, col, packed_row, packed_col in pieces(rows, product.shape[1]):
+            out[i, packed_row, packed_col] = block[row, col]
+
+
+def second_kernel(left, right, out, held):
+    rows = held.shape[0] // right.shape[0]
+    for i in range(right.shape[0]):
+        for row, col, packed_row, packed_col in pieces(rows, held.shape[1]):
+            row = slice(i * rows + row.start, i * rows + row.stop)
+            held[row, col] = right[i, packed_row, packed_col]
+    first_kernel(left, held, out)
 
 
 def update_kernel(iterate, once, parts, out, held, sem):
     fetch = pltpu.make_async_copy(iterate, held, sem)
     fetch.start()
-    step = coef_cubic * once[...]
-    step += coef_quintic * jnp.sum(parts[...].astype(jnp.float32), axis=0)
+    packed = coef_cubic * once[...]
+    packed += coef_quintic * jnp.sum(parts[...].astype(jnp.float32), axis=0)
     fetch.wait()
-    step += coef_linear * held[...].astype(jnp.float32)
-    out[...] = (0.2 * math.sqrt(max(D, FF)) * step).astype(out.dtype)
+    for row, col, packed_row, packed_col in pieces(*out.shape):
+        step = coef_linear * held[row, col].astype(jnp.float32) + packed[packed_row, packed_col]
+        out[row, col] = (0.2 * math.sqrt(max(D, FF)) * step).astype(out.dtype)
 
 
 def total(parts):
@@ -111,6 +137,7 @@
     left = exchange(left.reshape(8, half, cols), ("y", "core")).reshape(4, 2, half, cols)
     right = gather(iterate, ("z_lo", "core")).reshape(4, 2, rows, cols)
     own = call(own_kernel, [(core, SMEM), (right, VMEM)], bf16(4 * rows, cols))
+    right, own = lax.optimization_barrier((right, own))
 
     tile = call(
         gram_kernel,
@@ -122,21 +149,20 @@
     piece = total(lax.all_gather(piece, "z_hi", axis=0)).astype(jnp.bfloat16)
     gram = gather(piece, ("x", "core")).reshape(4 * rows, 4 * rows)
 
-    def gram_times(array):
-        parts = call(
-            product_kernel,
-            [(gram, VMEM), (array, VMEM)],
-            bf16(4 * rows, cols),
-            flops=2 * gram.size * cols,
-        )
-        return exchange(parts.reshape(4, rows, cols), "y")
-
-    once = total(gram_times(own))
-    gathered = lax.all_gather(once.astype(jnp.bfloat16), "z_lo", axis=0)
-    twice = gram_times(gathered.reshape(4 * rows, cols))
+    packed = bf16(4, rows * cols // LANES, LANES)
+    flops = 2 * gram.size * cols
+    once = call(first_kernel, [(gram, VMEM), (own, VMEM)], packed, flops=flops)
+    once = total(exchange(once, "y"))
+    twice = call(
+        second_kernel,
+        [(gram, VMEM), (lax.all_gather(once.astype(jnp.bfloat16), "z_lo", axis=0), VMEM)],
+        packed,
+        scratch=[pltpu.VMEM(own.shape, own.dtype)],
+        flops=flops,
+    )
     return call(
         update_kernel,
-        [(iterate, ANY), (once, VMEM), (twice, VMEM)],
+        [(iterate, ANY), (once, VMEM), (exchange(twice, "y"), VMEM)],
         bf16(rows, cols),
         scratch=[pltpu.VMEM(iterate.shape, iterate.dtype), sems],
     )

time: 174 us -> 170 us (0.977)
  the two profiles are of different devices: /device:TPU:1 before, /device:TPU:32 now
where the time goes in v10:
time: 170 us; the launch traced here: 169 us
  blocking collectives  153 us (90%)
  Pallas kernels  7.18 us (4%)
  starting transfers between devices  4.48 us (3%)
  local copies, waits for them, and re-layouts  3.02 us (2%)
    all_to_all x3, blocking collectives, exchange(): return lax.all_to_all(array, axes, 0, 0, tiled=True)  52.5 us
    all_gather x2, blocking collectives, gather(): lax.all_gather(array.astype(jnp.float16), axes, axis=0).astype(jnp.bfloat16)  40.4 us
    all_gather x1, blocking collectives, shards(): piece = total(lax.all_gather(piece, 'z_hi', axis=0)).astype(jnp.bfloat16)  30.6 us
    all_gather x1, blocking collectives, shards(): lax.all_gather(once.astype(jnp.bfloat16), 'z_lo', axis=0)  29.8 us
    pallas_call x6, Pallas kernels, call(): pl.pallas_call(kernel, out_shape=output, in_specs=in_specs, out_specs=spe...  7.18 us
    all_to_all x1, starting transfers between devices, exchange(): return lax.all_to_all(array, axes, 0, 0, tiled=True)  4.48 us
  transfers between devices with their start and end apart: 1, of which 0 were waited for; matrix products, arithmetic and copies ran while one was open for 0% of the time, Pallas kernels for 0%

profile of v10, /device:TPU:32, one launch (start us, length us, event | category | flops | bytes accessed | tf_op | source)
XLA Modules:
  0.0 169.3 jit_solution(13014506619189762164)
XLA Ops:
  0.0 0.0 copy-start.2
  0.0 1.0 copy-done.2
  1.0 0.0 copy-start.3
  1.0 1.0 shard_map.17
  2.0 4.5 %all-to-all-start = ((bf16[8,112,576]{2,1,0:T(8,128)(2,1)}), bf16[8,112,576]{2,1,0:T(8,128)(2,1)S(1)}, u32[]{:S(2)}, u32[]{:S(2)}) async-start(bf16[8,112,576]{2,1,0:T(8,128)(2,1)} %bitcast.1), calls=%async_computation | async-start | bytes 2293760 | tf_op jit(solution)/shard_map/all_to_all | solution.py:121
  6.5 0.0 copy-done.3
  6.5 0.1 convert_element_type.42
  6.6 25.6 %all-gather.6 = f16[1792,576]{1,0:T(8,128)(2,1)S(1)} all-gather(f16[224,576]{1,0:T(8,128)(2,1)S(1)} %convert_element_type.42), channel_id=2, replica_groups=mesh['z_lo'=4,'y'=4,'z_hi'=4,'x'=4,'core'=2] {'z_lo','core'}, dimensions={0}, use_global_device_ids=true | all-gather | bytes 2322432 | tf_op jit(solution)/shard_map/all_gather | solution.py:117
  32.1 0.4 convert_element_type.50
  32.6 0.1 shard_map.18.right
  32.7 0.0 copy-start
  32.7 1.0 copy-done
  33.7 0.0 all-to-all-done
  33.7 1.6 shard_map.19
  35.3 16.9 %all_to_all.20 = bf16[4,112,896]{2,1,0:T(8,128)(2,1)S(1)} all-to-all(bf16[4,112,896]{2,1,0:T(8,128)(2,1)S(1)} %shard_map.19), channel_id=1, replica_groups=mesh['z_lo'=4,'y'=4,'z_hi'=4,'x'=4,'core'=2] {'x'}, dimensions={0} | all-to-all | bytes 1605632 | tf_op jit(solution)/shard_map/all_to_all | solution.py:121
  52.2 0.1 reduce_sum.33
  52.3 30.6 %all-gather.1 = bf16[448,896]{1,0:T(8,128)(2,1)S(1)} all-gather(bf16[112,896]{1,0:T(8,128)(2,1)S(1)} %reduce_sum.33), channel_id=3, replica_groups=mesh['z_lo'=4,'y'=4,'z_hi'=4,'x'=4,'core'=2] {'z_hi'}, dimensions={0}, use_global_device_ids=true | all-gather | bytes 1003520 | tf_op jit(solution)/shard_map/all_gather | solution.py:149
  83.0 0.1 reduce_sum.34
  83.1 14.9 %all-gather.7 = f16[896,896]{1,0:T(8,128)(2,1)S(1)} all-gather(f16[112,896]{1,0:T(8,128)(2,1)S(1)} %convert_element_type.44), channel_id=4, replica_groups=mesh['z_lo'=4,'y'=4,'z_hi'=4,'x'=4,'core'=2] {'x','core'}, dimensions={0}, use_global_device_ids=true | all-gather | bytes 1806336 | tf_op jit(solution)/shard_map/all_gather | solution.py:117
  98.0 0.0 copy-start.1
  98.0 0.2 convert_element_type.51.left
  98.2 1.0 copy-done.1
  99.3 1.6 shard_map.20
  100.9 19.7 %all_to_all.21 = bf16[4,1008,128]{2,1,0:T(8,128)(2,1)S(1)} all-to-all(bf16[4,1008,128]{2,1,0:T(8,128)(2,1)S(1)} %shard_map.20), channel_id=1, replica_groups=mesh['z_lo'=4,'y'=4,'z_hi'=4,'x'=4,'core'=2] {'y'}, dimensions={0} | all-to-all | bytes 2064384 | tf_op jit(solution)/shard_map/all_to_all | solution.py:121
  120.5 0.1 convert_reduce_fusion.once
  120.7 29.8 %all-gather.3 = bf16[4032,128]{1,0:T(8,128)(2,1)S(1)} all-gather(bf16[1008,128]{1,0:T(8,128)(2,1)S(1)} %convert_element_type.48), channel_id=5, replica_groups=mesh['z_lo'=4,'y'=4,'z_hi'=4,'x'=4,'core'=2] {'z_lo'}, dimensions={0}, use_global_device_ids=true | all-gather | bytes 1290240 | tf_op jit(solution)/shard_map/all_gather | solution.py:158
  150.5 1.7 %shard_map.21 = bf16[4,1008,128]{2,1,0:T(8,128)(2,1)S(1)} custom-call(bf16[896,896]{1,0:T(8,128)(2,1)S(1)} %convert_element_type.51.left, bf16[4,1008,128]{2,1,0:T(8,128)(2,1)S(1)} %bitcast.10), custom_call_target="tpu_custom_call" | custom-call | flops 924844032 | bytes 3670016 | tf_op jit(solution)/shard_map/pallas_call | solution.py:27
  152.2 0.0 copy-start.4
  152.2 15.9 %all_to_all.22.parts = bf16[4,1008,128]{2,1,0:T(8,128)(2,1)S(1)} all-to-all(bf16[4,1008,128]{2,1,0:T(8,128)(2,1)S(1)} %shard_map.21), channel_id=1, replica_groups=mesh['z_lo'=4,'y'=4,'z_hi'=4,'x'=4,'core'=2] {'y'}, dimensions={0} | all-to-all | bytes 2064384 | tf_op jit(solution)/shard_map/all_to_all | solution.py:121
  168.1 0.0 copy-done.4
  168.1 1.2 shard_map.22
  (2 shorter events, 0.1 us)
Async XLA Ops:
  0.0 1.0 copy-start.2
  1.0 5.5 %copy-start.3 = (bf16[224,576]{1,0:T(8,128)(2,1)S(1)}, bf16[224,576]{1,0:T(8,128)(2,1)}, u32[]{:S(2)}) copy-start(bf16[224,576]{1,0:T(8,128)(2,1)} %iterate.1) | copy-start | bytes 774148
  2.0 31.7 %all-to-all-start = ((bf16[8,112,576]{2,1,0:T(8,128)(2,1)}), bf16[8,112,576]{2,1,0:T(8,128)(2,1)S(1)}, u32[]{:S(2)}, u32[]{:S(2)}) async-start(bf16[8,112,576]{2,1,0:T(8,128)(2,1)} %bitcast.1), calls=%async_computation | async-start | bytes 2293760 | tf_op jit(solution)/shard_map/all_to_all | solution.py:121
  32.7 1.0 copy-start
  98.0 1.3 copy-start.1
  152.2 15.9 %copy-start.4 = (bf16[224,576]{1,0:T(8,128)(2,1)S(1)}, bf16[224,576]{1,0:T(8,128)(2,1)}, u32[]{:S(2)}) copy-start(bf16[224,576]{1,0:T(8,128)(2,1)} %iterate.1) | copy-start | bytes 774148

commit v11 on v10

--- a/solution.py
+++ b/solution.py
@@ -30,7 +30,7 @@
         in_specs=in_specs,
         out_specs=spec,
         scratch_shapes=scratch,
-        compiler_params=pltpu.CompilerParams(vmem_limit_bytes=24 * 1024 * 1024),
+        compiler_params=pltpu.CompilerParams(vmem_limit_bytes=16 * 1024 * 1024),
         cost_estimate=pl.CostEstimate(
             flops=flops,
             bytes_accessed=2 * sum(math.prod(array.shape) for array in (output, *arrays)),
@@ -136,8 +136,6 @@
     )
     left = exchange(left.reshape(8, half, cols), ("y", "core")).reshape(4, 2, half, cols)
     right = gather(iterate, ("z_lo", "core")).reshape(4, 2, rows, cols)
-    own = call(own_kernel, [(core, SMEM), (right, VMEM)], bf16(4 * rows, cols))
-    right, own = lax.optimization_barrier((right, own))
 
     tile = call(
         gram_kernel,
@@ -145,6 +143,9 @@
         bf16(4, half, 4 * rows),
         flops=4 * 4 * half * 4 * rows * cols,
     )
+    tile, right = lax.optimization_barrier((tile, right))
+    own = call(own_kernel, [(core, SMEM), (right, VMEM)], bf16(4 * rows, cols))
+    tile, own = lax.optimization_barrier((tile, own))
     piece = total(exchange(tile, "x")).astype(jnp.bfloat16)
     piece = total(lax.all_gather(piece, "z_hi", axis=0)).astype(jnp.bfloat16)
     gram = gather(piece, ("x", "core")).reshape(4 * rows, 4 * rows)

time: 170 us -> 168 us (0.988)
  local copies, waits for them, and re-layouts: 3.02 us -> 0.97 us
    unnamed x10 -> x6, local copies, waits for them, and re-layouts: 3.02 us -> 0.97 us
where the time goes in v11:
time: 168 us; the launch traced here: 167 us
  blocking collectives  153 us (91%)
  Pallas kernels  7.23 us (4%)
  starting transfers between devices  4.48 us (3%)
    all_to_all x3, blocking collectives, exchange(): return lax.all_to_all(array, axes, 0, 0, tiled=True)  52.8 us
    all_gather x2, blocking collectives, gather(): lax.all_gather(array.astype(jnp.float16), axes, axis=0).astype(jnp.bfloat16)  40.4 us
    all_gather x1, blocking collectives, shards(): piece = total(lax.all_gather(piece, 'z_hi', axis=0)).astype(jnp.bfloat16)  30.2 us
    all_gather x1, blocking collectives, shards(): lax.all_gather(once.astype(jnp.bfloat16), 'z_lo', axis=0)  29.9 us
    pallas_call x6, Pallas kernels, call(): pl.pallas_call(kernel, out_shape=output, in_specs=in_specs, out_specs=spe...  7.23 us
    all_to_all x1, starting transfers between devices, exchange(): return lax.all_to_all(array, axes, 0, 0, tiled=True)  4.48 us
  transfers between devices with their start and end apart: 1, of which 0 were waited for; matrix products, arithmetic and copies ran while one was open for 0% of the time, Pallas kernels for 0%

profile of v11, /device:TPU:32, one launch (start us, length us, event | category | flops | bytes accessed | tf_op | source)
XLA Modules:
  0.0 167.3 jit_solution(2349700120845952348)
XLA Ops:
  0.0 0.0 copy-start
  0.0 1.0 copy-done
  1.0 0.0 copy-start.1
  1.0 1.0 shard_map.17
  2.0 4.5 %all-to-all-start = ((bf16[8,112,576]{2,1,0:T(8,128)(2,1)}), bf16[8,112,576]{2,1,0:T(8,128)(2,1)S(1)}, u32[]{:S(2)}, u32[]{:S(2)}) async-start(bf16[8,112,576]{2,1,0:T(8,128)(2,1)} %bitcast.1), calls=%async_computation | async-start | bytes 2293760 | tf_op jit(solution)/shard_map/all_to_all | solution.py:121
  6.5 0.0 copy-done.1
  6.5 0.1 convert_element_type.42
  6.6 25.6 %all-gather.6 = f16[1792,576]{1,0:T(8,128)(2,1)S(1)} all-gather(f16[224,576]{1,0:T(8,128)(2,1)S(1)} %convert_element_type.42), channel_id=2, replica_groups=mesh['z_lo'=4,'y'=4,'z_hi'=4,'x'=4,'core'=2] {'z_lo','core'}, dimensions={0}, use_global_device_ids=true | all-gather | bytes 2322432 | tf_op jit(solution)/shard_map/all_gather | solution.py:117
  32.1 0.4 convert_element_type.50
  32.6 0.0 all-to-all-done
  32.6 1.6 shard_map.18
  34.2 0.1 shard_map.19.right
  34.3 16.9 %all_to_all.20 = bf16[4,112,896]{2,1,0:T(8,128)(2,1)S(1)} all-to-all(bf16[4,112,896]{2,1,0:T(8,128)(2,1)S(1)} %shard_map.18), channel_id=1, replica_groups=mesh['z_lo'=4,'y'=4,'z_hi'=4,'x'=4,'core'=2] {'x'}, dimensions={0} | all-to-all | bytes 1605632 | tf_op jit(solution)/shard_map/all_to_all | solution.py:121
  51.2 0.1 reduce_sum.33
  51.3 30.2 %all-gather.1 = bf16[448,896]{1,0:T(8,128)(2,1)S(1)} all-gather(bf16[112,896]{1,0:T(8,128)(2,1)S(1)} %reduce_sum.33), channel_id=3, replica_groups=mesh['z_lo'=4,'y'=4,'z_hi'=4,'x'=4,'core'=2] {'z_hi'}, dimensions={0}, use_global_device_ids=true | all-gather | bytes 1003520 | tf_op jit(solution)/shard_map/all_gather | solution.py:150
  81.5 0.1 reduce_sum.34
  81.6 14.9 %all-gather.7 = f16[896,896]{1,0:T(8,128)(2,1)S(1)} all-gather(f16[112,896]{1,0:T(8,128)(2,1)S(1)} %convert_element_type.44), channel_id=4, replica_groups=mesh['z_lo'=4,'y'=4,'z_hi'=4,'x'=4,'core'=2] {'x','core'}, dimensions={0}, use_global_device_ids=true | all-gather | bytes 1806336 | tf_op jit(solution)/shard_map/all_gather | solution.py:117
  96.5 0.3 convert_element_type.51.left
  96.7 1.6 shard_map.20
  98.4 20.0 %all_to_all.21 = bf16[4,1008,128]{2,1,0:T(8,128)(2,1)S(1)} all-to-all(bf16[4,1008,128]{2,1,0:T(8,128)(2,1)S(1)} %shard_map.20), channel_id=1, replica_groups=mesh['z_lo'=4,'y'=4,'z_hi'=4,'x'=4,'core'=2] {'y'}, dimensions={0} | all-to-all | bytes 2064384 | tf_op jit(solution)/shard_map/all_to_all | solution.py:121
  118.3 0.1 convert_reduce_fusion.once
  118.5 29.9 %all-gather.3 = bf16[4032,128]{1,0:T(8,128)(2,1)S(1)} all-gather(bf16[1008,128]{1,0:T(8,128)(2,1)S(1)} %convert_element_type.48), channel_id=5, replica_groups=mesh['z_lo'=4,'y'=4,'z_hi'=4,'x'=4,'core'=2] {'z_lo'}, dimensions={0}, use_global_device_ids=true | all-gather | bytes 1290240 | tf_op jit(solution)/shard_map/all_gather | solution.py:159
  148.5 1.7 %shard_map.21 = bf16[4,1008,128]{2,1,0:T(8,128)(2,1)S(1)} custom-call(bf16[896,896]{1,0:T(8,128)(2,1)S(1)} %convert_element_type.51.left, bf16[4,1008,128]{2,1,0:T(8,128)(2,1)S(1)} %bitcast.10), custom_call_target="tpu_custom_call" | custom-call | flops 924844032 | bytes 3670016 | tf_op jit(solution)/shard_map/pallas_call | solution.py:27
  150.2 0.0 copy-start.2
  150.2 15.9 %all_to_all.22.parts = bf16[4,1008,128]{2,1,0:T(8,128)(2,1)S(1)} all-to-all(bf16[4,1008,128]{2,1,0:T(8,128)(2,1)S(1)} %shard_map.21), channel_id=1, replica_groups=mesh['z_lo'=4,'y'=4,'z_hi'=4,'x'=4,'core'=2] {'y'}, dimensions={0} | all-to-all | bytes 2064384 | tf_op jit(solution)/shard_map/all_to_all | solution.py:121
  166.1 0.0 copy-done.2
  166.1 1.2 shard_map.22
  (2 shorter events, 0.1 us)
Async XLA Ops:
  0.0 1.0 copy-start
  1.0 5.5 %copy-start.1 = (bf16[224,576]{1,0:T(8,128)(2,1)S(1)}, bf16[224,576]{1,0:T(8,128)(2,1)}, u32[]{:S(2)}) copy-start(bf16[224,576]{1,0:T(8,128)(2,1)} %iterate.1) | copy-start | bytes 774148
  2.0 30.6 %all-to-all-start = ((bf16[8,112,576]{2,1,0:T(8,128)(2,1)}), bf16[8,112,576]{2,1,0:T(8,128)(2,1)S(1)}, u32[]{:S(2)}, u32[]{:S(2)}) async-start(bf16[8,112,576]{2,1,0:T(8,128)(2,1)} %bitcast.1), calls=%async_computation | async-start | bytes 2293760 | tf_op jit(solution)/shard_map/all_to_all | solution.py:121
  150.2 15.9 %copy-start.2 = (bf16[224,576]{1,0:T(8,128)(2,1)S(1)}, bf16[224,576]{1,0:T(8,128)(2,1)}, u32[]{:S(2)}) copy-start(bf16[224,576]{1,0:T(8,128)(2,1)} %iterate.1) | copy-start | bytes 774148

commit v12 on v11

--- a/solution.py
+++ b/solution.py
@@ -16,6 +16,7 @@
 coef_quintic = 2.0315
 
 LANES = 128
+PAIRS = [[0, 2], [4, 6], [3, 5], [7, 1]], [[2, 4], [6, 0], [1, 3], [5, 7]]
 VMEM = pl.BlockSpec(memory_space=pltpu.VMEM)
 SMEM = pl.BlockSpec(memory_space=pltpu.SMEM)
 HBM = pl.BlockSpec(memory_space=pltpu.HBM)
@@ -146,8 +147,10 @@
     tile, right = lax.optimization_barrier((tile, right))
     own = call(own_kernel, [(core, SMEM), (right, VMEM)], bf16(4 * rows, cols))
     tile, own = lax.optimization_barrier((tile, own))
-    piece = total(exchange(tile, "x")).astype(jnp.bfloat16)
-    piece = total(lax.all_gather(piece, "z_hi", axis=0)).astype(jnp.bfloat16)
+    piece = total(exchange(tile, "x"))
+    for groups in PAIRS:
+        piece = piece.astype(jnp.float16)
+        piece = total(lax.all_gather(piece, ("z_hi", "core"), axis=0, axis_index_groups=groups))
     gram = gather(piece, ("x", "core")).reshape(4 * rows, 4 * rows)
 
     packed = bf16(4, rows * cols // LANES, LANES)

time: 168 us -> 161 us (0.958)
  blocking collectives: 153 us -> 146 us
    all_gather x1, blocking collectives: 29.9 us -> 25.3 us  [shards(): lax.all_gather(once.astype(jnp.bfloat16), 'z_lo', axis=0)]
    all_gather x1 -> x2, blocking collectives: 30.2 us -> 28 us  [shards(): lax.all_gather(piece, ('z_hi', 'core'), axis=0, axis_index_groups=groups)]
where the time goes in v12:
time: 161 us; the launch traced here: 160 us
  blocking collectives  146 us (91%)
  Pallas kernels  7.22 us (4%)
  starting transfers between devices  4.48 us (3%)
    all_to_all x3, blocking collectives, exchange(): return lax.all_to_all(array, axes, 0, 0, tiled=True)  52.4 us
    all_gather x2, blocking collectives, gather(): lax.all_gather(array.astype(jnp.float16), axes, axis=0).astype(jnp.bfloat16)  40.4 us
    all_gather x2, blocking collectives, shards(): lax.all_gather(piece, ('z_hi', 'core'), axis=0, axis_index_groups=groups)  28 us
    all_gather x1, blocking collectives, shards(): lax.all_gather(once.astype(jnp.bfloat16), 'z_lo', axis=0)  25.3 us
    pallas_call x6, Pallas kernels, call(): pl.pallas_call(kernel, out_shape=output, in_specs=in_specs, out_specs=spe...  7.22 us
    all_to_all x1, starting transfers between devices, exchange(): return lax.all_to_all(array, axes, 0, 0, tiled=True)  4.48 us
  transfers between devices with their start and end apart: 1, of which 0 were waited for; matrix products, arithmetic and copies ran while one was open for 0% of the time, Pallas kernels for 0%

profile of v12, /device:TPU:32, one launch (start us, length us, event | category | flops | bytes accessed | tf_op | source)
XLA Modules:
  0.0 160.2 jit_solution(9742391990304355144)
XLA Ops:
  0.0 0.0 copy-start
  0.0 1.0 copy-done
  1.0 0.0 copy-start.1
  1.0 1.0 shard_map.17
  2.0 4.5 %all-to-all-start = ((bf16[8,112,576]{2,1,0:T(8,128)(2,1)}), bf16[8,112,576]{2,1,0:T(8,128)(2,1)S(1)}, u32[]{:S(2)}, u32[]{:S(2)}) async-start(bf16[8,112,576]{2,1,0:T(8,128)(2,1)} %bitcast.1), calls=%async_computation | async-start | bytes 2293760 | tf_op jit(solution)/shard_map/all_to_all | solution.py:122
  6.5 0.0 copy-done.1
  6.5 0.1 convert_element_type.73
  6.6 25.6 %all-gather.7 = f16[1792,576]{1,0:T(8,128)(2,1)S(1)} all-gather(f16[224,576]{1,0:T(8,128)(2,1)S(1)} %convert_element_type.73), channel_id=2, replica_groups=mesh['z_lo'=4,'y'=4,'z_hi'=4,'x'=4,'core'=2] {'z_lo','core'}, dimensions={0}, use_global_device_ids=true | all-gather | bytes 2322432 | tf_op jit(solution)/shard_map/all_gather | solution.py:118
  32.1 0.4 convert_element_type.88
  32.6 0.0 all-to-all-done
  32.6 1.6 shard_map.18
  34.2 0.1 shard_map.19.right
  34.3 16.9 %all_to_all.20 = bf16[4,112,896]{2,1,0:T(8,128)(2,1)S(1)} all-to-all(bf16[4,112,896]{2,1,0:T(8,128)(2,1)S(1)} %shard_map.18), channel_id=1, replica_groups=mesh['z_lo'=4,'y'=4,'z_hi'=4,'x'=4,'core'=2] {'x'}, dimensions={0} | all-to-all | bytes 1605632 | tf_op jit(solution)/shard_map/all_to_all | solution.py:122
  51.2 0.1 convert_reduce_fusion.1
  51.3 17.4 %all-gather.1 = f16[224,896]{1,0:T(8,128)(2,1)S(1)} all-gather(f16[112,896]{1,0:T(8,128)(2,1)S(1)} %convert_element_type.76), channel_id=3, replica_groups={{0,8},{16,24},{9,17},{25,1},{2,10},{18,26},{11,19},{27,3},{4,12},{20,28..., dimensions={0}, use_global_device_ids=true | all-gather | bytes 602112 | tf_op jit(solution)/shard_map/all_gather | solution.py:153
  68.7 0.1 convert_reduce_fusion.3
  68.8 10.6 %all-gather.2 = f16[224,896]{1,0:T(8,128)(2,1)S(1)} all-gather(f16[112,896]{1,0:T(8,128)(2,1)S(1)} %convert_element_type.79), channel_id=4, replica_groups={{8,16},{24,0},{1,9},{17,25},{10,18},{26,2},{3,11},{19,27},{12,20},{28,4..., dimensions={0}, use_global_device_ids=true | all-gather | bytes 602112 | tf_op jit(solution)/shard_map/all_gather | solution.py:153
  79.4 0.1 convert_reduce_fusion.2
  79.5 14.9 %all-gather.8 = f16[896,896]{1,0:T(8,128)(2,1)S(1)} all-gather(f16[112,896]{1,0:T(8,128)(2,1)S(1)} %convert_element_type.82), channel_id=5, replica_groups=mesh['z_lo'=4,'y'=4,'z_hi'=4,'x'=4,'core'=2] {'x','core'}, dimensions={0}, use_global_device_ids=true | all-gather | bytes 1806336 | tf_op jit(solution)/shard_map/all_gather | solution.py:118
  94.4 0.3 convert_element_type.91.left
  94.7 1.6 %shard_map.20 = bf16[4,1008,128]{2,1,0:T(8,128)(2,1)S(1)} custom-call(bf16[896,896]{1,0:T(8,128)(2,1)S(1)} %convert_element_type.91.left, bf16[896,576]{1,0:T(8,128)(2,1)S(1)} %shard_map.19.right), custom_call_target="tpu_custom_call" | custom-call | flops 924844032 | bytes 3670016 | tf_op jit(solution)/shard_map/pallas_call | solution.py:28
  96.3 19.6 %all_to_all.21 = bf16[4,1008,128]{2,1,0:T(8,128)(2,1)S(1)} all-to-all(bf16[4,1008,128]{2,1,0:T(8,128)(2,1)S(1)} %shard_map.20), channel_id=1, replica_groups=mesh['z_lo'=4,'y'=4,'z_hi'=4,'x'=4,'core'=2] {'y'}, dimensions={0} | all-to-all | bytes 2064384 | tf_op jit(solution)/shard_map/all_to_all | solution.py:122
  115.9 0.1 convert_reduce_fusion.once
  116.1 25.3 %all-gather.4 = bf16[4032,128]{1,0:T(8,128)(2,1)S(1)} all-gather(bf16[1008,128]{1,0:T(8,128)(2,1)S(1)} %convert_element_type.86), channel_id=6, replica_groups=mesh['z_lo'=4,'y'=4,'z_hi'=4,'x'=4,'core'=2] {'z_lo'}, dimensions={0}, use_global_device_ids=true | all-gather | bytes 1290240 | tf_op jit(solution)/shard_map/all_gather | solution.py:162
  141.4 1.7 %shard_map.21 = bf16[4,1008,128]{2,1,0:T(8,128)(2,1)S(1)} custom-call(bf16[896,896]{1,0:T(8,128)(2,1)S(1)} %convert_element_type.91.left, bf16[4,1008,128]{2,1,0:T(8,128)(2,1)S(1)} %bitcast.13), custom_call_target="tpu_custom_call" | custom-call | flops 924844032 | bytes 3670016 | tf_op jit(solution)/shard_map/pallas_call | solution.py:28
  143.1 0.0 copy-start.2
  143.1 15.9 %all_to_all.22.parts = bf16[4,1008,128]{2,1,0:T(8,128)(2,1)S(1)} all-to-all(bf16[4,1008,128]{2,1,0:T(8,128)(2,1)S(1)} %shard_map.21), channel_id=1, replica_groups=mesh['z_lo'=4,'y'=4,'z_hi'=4,'x'=4,'core'=2] {'y'}, dimensions={0} | all-to-all | bytes 2064384 | tf_op jit(solution)/shard_map/all_to_all | solution.py:122
  159.0 0.0 copy-done.2
  159.0 1.2 shard_map.22
  (4 shorter events, 0.1 us)
Async XLA Ops:
  0.0 1.0 copy-start
  1.0 5.5 %copy-start.1 = (bf16[224,576]{1,0:T(8,128)(2,1)S(1)}, bf16[224,576]{1,0:T(8,128)(2,1)}, u32[]{:S(2)}) copy-start(bf16[224,576]{1,0:T(8,128)(2,1)} %iterate.1) | copy-start | bytes 774148
  2.0 30.6 %all-to-all-start = ((bf16[8,112,576]{2,1,0:T(8,128)(2,1)}), bf16[8,112,576]{2,1,0:T(8,128)(2,1)S(1)}, u32[]{:S(2)}, u32[]{:S(2)}) async-start(bf16[8,112,576]{2,1,0:T(8,128)(2,1)} %bitcast.1), calls=%async_computation | async-start | bytes 2293760 | tf_op jit(solution)/shard_map/all_to_all | solution.py:122
  143.1 15.9 %copy-start.2 = (bf16[224,576]{1,0:T(8,128)(2,1)S(1)}, bf16[224,576]{1,0:T(8,128)(2,1)}, u32[]{:S(2)}) copy-start(bf16[224,576]{1,0:T(8,128)(2,1)} %iterate.1) | copy-start | bytes 774148

commit v13 on v12

--- a/solution.py
+++ b/solution.py
@@ -44,9 +44,9 @@
     return jax.ShapeDtypeStruct(shape, jnp.bfloat16)
 
 
-def dot(lhs, rhs, rhs_dim):
+def dot(lhs, rhs, contract):
     return lax.dot_general(
-        lhs, rhs, (((1,), (rhs_dim,)), ((), ())), preferred_element_type=jnp.float32
+        lhs, rhs, ((contract[:1], contract[1:]), ((), ())), preferred_element_type=jnp.float32
     )
 
 
@@ -63,12 +63,12 @@
     tile = jnp.zeros((blocks * rows, out.shape[-1]), jnp.float32)
     for k in range(cores):
         lhs = left[:, k].reshape(blocks * rows, cols)
-        tile += dot(lhs, right[:, k].reshape(out.shape[-1], cols), 1)
+        tile += dot(lhs, right[:, k].reshape(out.shape[-1], cols), (1, 1))
     out[...] = tile.astype(out.dtype).reshape(out.shape)
 
 
-def own_kernel(core, right, out):
-    out[...] = right[:, pl.ds(core[0], 1)].reshape(out.shape)
+def columns_kernel(core, array, out):
+    out[...] = array[:, pl.ds(core[0], 1)].reshape(out.shape)
 
 
 def pieces(rows, cols):
@@ -81,13 +81,22 @@
         yield slice(k * each, (k + 1) * each), slice(whole * LANES, cols), slice(whole * rows, whole * rows + each), columns
 
 
-def first_kernel(left, right, out):
-    product = dot(left[...], right[...], 0).astype(out.dtype)
-    rows = product.shape[0] // out.shape[0]
+def product(left, right, out):
+    sums = dot(left[...], right[...], (0, 0)).astype(out.dtype)
+    rows = sums.shape[0] // out.shape[0]
     for i in range(out.shape[0]):
-        block = product[i * rows : (i + 1) * rows]
-        for row, col, packed_row, packed_col in pieces(rows, product.shape[1]):
+        block = sums[i * rows : (i + 1) * rows]
+        for row, col, packed_row, packed_col in pieces(rows, sums.shape[1]):
             out[i, packed_row, packed_col] = block[row, col]
+
+
+def first_kernel(core, left, mine, other, out, held):
+    blocks, half, _ = mine.shape
+    for array, place in ((mine, core[0]), (other, 1 - core[0])):
+        for i in range(blocks):
+            start = pl.multiple_of(2 * half * i + half * place, 16)
+            held[pl.ds(start, half)] = array[i]
+    product(left, held, out)
 
 
 def second_kernel(left, right, out, held):
@@ -96,7 +105,7 @@
         for row, col, packed_row, packed_col in pieces(rows, held.shape[1]):
             row = slice(i * rows + row.start, i * rows + row.stop)
             held[row, col] = right[i, packed_row, packed_col]
-    first_kernel(left, held, out)
+    product(left, held, out)
 
 
 def update_kernel(iterate, once, parts, out, held, sem):
@@ -128,26 +137,30 @@
     core = lax.axis_index("core").astype(jnp.int32).reshape(1)
     sems = pltpu.SemaphoreType.DMA
 
-    left = call(
+    right = call(
         copies_kernel,
         [(iterate.reshape(2, half, cols), VMEM)],
         bf16(4, 2, half, cols),
         spec=HBM,
         scratch=[sems((4,))],
     )
-    left = exchange(left.reshape(8, half, cols), ("y", "core")).reshape(4, 2, half, cols)
-    right = gather(iterate, ("z_lo", "core")).reshape(4, 2, rows, cols)
+    right = exchange(right.reshape(8, half, cols), ("z_lo", "core")).reshape(4, 2, half, cols)
+    left = gather(iterate, ("y", "core")).reshape(4, 2, rows, cols)
 
     tile = call(
         gram_kernel,
-        [(left, VMEM), (right, VMEM)],
+        [(right, VMEM), (left, VMEM)],
         bf16(4, half, 4 * rows),
         flops=4 * 4 * half * 4 * rows * cols,
     )
     tile, right = lax.optimization_barrier((tile, right))
-    own = call(own_kernel, [(core, SMEM), (right, VMEM)], bf16(4 * rows, cols))
-    tile, own = lax.optimization_barrier((tile, own))
-    piece = total(exchange(tile, "x"))
+    mine, away = (
+        call(columns_kernel, [(which, SMEM), (right, VMEM)], bf16(4, half, cols))
+        for which in (core, 1 - core)
+    )
+    tile, mine, away = lax.optimization_barrier((tile, mine, away))
+    piece, away = lax.optimization_barrier((total(exchange(tile, "x")), away))
+    other = lax.ppermute(away, "core", [(0, 1), (1, 0)])
     for groups in PAIRS:
         piece = piece.astype(jnp.float16)
         piece = total(lax.all_gather(piece, ("z_hi", "core"), axis=0, axis_index_groups=groups))
@@ -155,13 +168,20 @@
 
     packed = bf16(4, rows * cols // LANES, LANES)
     flops = 2 * gram.size * cols
-    once = call(first_kernel, [(gram, VMEM), (own, VMEM)], packed, flops=flops)
+    held = pltpu.VMEM((4 * rows, cols), jnp.bfloat16)
+    once = call(
+        first_kernel,
+        [(core, SMEM), (gram, VMEM), (mine, VMEM), (other, VMEM)],
+        packed,
+        scratch=[held],
+        flops=flops,
+    )
     once = total(exchange(once, "y"))
     twice = call(
         second_kernel,
         [(gram, VMEM), (lax.all_gather(once.astype(jnp.bfloat16), "z_lo", axis=0), VMEM)],
         packed,
-        scratch=[pltpu.VMEM(own.shape, own.dtype)],
+        scratch=[held],
         flops=flops,
     )
     return call(

time: 161 us -> 164 us (1.019)
  the two profiles are of different devices: /device:TPU:32 before, /device:TPU:1 now
where the time goes in v13:
time: 164 us; the launch traced here: 162 us
  blocking collectives  128 us (78%)
  starting transfers between devices  14.4 us (9%)
  waiting for transfers between devices  10.7 us (7%)
  Pallas kernels  7.35 us (4%)
    all_to_all x3, blocking collectives, exchange(): return lax.all_to_all(array, axes, 0, 0, tiled=True)  49 us
    all_gather x2, blocking collectives, gather(): lax.all_gather(array.astype(jnp.float16), axes, axis=0).astype(jnp.bfloat16)  31.8 us
    all_gather x2, blocking collectives, shards(): lax.all_gather(piece, ('z_hi', 'core'), axis=0, axis_index_groups=groups)  28 us
    all_gather x1, blocking collectives, shards(): lax.all_gather(once.astype(jnp.bfloat16), 'z_lo', axis=0)  18.9 us
    all_to_all x1, waiting for transfers between devices, exchange(): return lax.all_to_all(array, axes, 0, 0, tiled=True)  10.7 us
    all_to_all x1, starting transfers between devices, exchange(): return lax.all_to_all(array, axes, 0, 0, tiled=True)  10.4 us
    pallas_call x7, Pallas kernels, call(): pl.pallas_call(kernel, out_shape=output, in_specs=in_specs, out_specs=spe...  7.35 us
    ppermute x1, starting transfers between devices, shards(): other = lax.ppermute(away, 'core', [(0, 1), (1, 0)])  4.02 us
  transfers between devices with their start and end apart: 2, of which 1 were waited for; matrix products, arithmetic and copies ran while one was open for 0% of the time, Pallas kernels for 0%

profile of v13, /device:TPU:1, one launch (start us, length us, event | category | flops | bytes accessed | tf_op | source)
XLA Modules:
  0.0 162.5 jit_solution(3202023032530013901)
XLA Ops:
  0.0 0.0 copy-start
  0.0 1.0 copy-done
  1.0 0.0 copy-start.1
  1.0 1.0 shard_map.17
  2.0 10.4 %all-to-all-start = ((bf16[8,112,576]{2,1,0:T(8,128)(2,1)}), bf16[8,112,576]{2,1,0:T(8,128)(2,1)S(1)}, u32[]{:S(2)}, u32[]{:S(2)}) async-start(bf16[8,112,576]{2,1,0:T(8,128)(2,1)} %bitcast.2), calls=%async_computation | async-start | bytes 2293760 | tf_op jit(solution)/shard_map/all_to_all | solution.py:131
  12.4 0.0 copy-done.1
  12.4 0.1 convert_element_type.63
  12.4 16.7 %all-gather.7 = f16[1792,576]{1,0:T(8,128)(2,1)S(1)} all-gather(f16[224,576]{1,0:T(8,128)(2,1)S(1)} %convert_element_type.63), channel_id=2, replica_groups=mesh['z_lo'=4,'y'=4,'z_hi'=4,'x'=4,'core'=2] {'y','core'}, dimensions={0}, use_global_device_ids=true | all-gather | bytes 2322432 | tf_op jit(solution)/shard_map/all_gather | solution.py:127
  29.1 0.4 convert_element_type.77
  29.5 10.7 %all-to-all-done = bf16[8,112,576]{2,1,0:T(8,128)(2,1)S(1)} async-done(((bf16[8,112,576]{2,1,0:T(8,128)(2,1)}), bf16[8,112,576]{2,1,0:T(8,128)(2,1)S(1)}, u32[]{:S(2)}, u32[]{:S(2)}) %all-to-all-start) | async-done | bytes 1032224 | tf_op jit(solution)/shard_map/all_to_all | solution.py:131
  40.2 1.6 shard_map.18
  41.8 0.1 shard_map.19.mine
  41.9 0.1 shard_map.20
  41.9 13.8 %all_to_all.20 = bf16[4,112,896]{2,1,0:T(8,128)(2,1)S(1)} all-to-all(bf16[4,112,896]{2,1,0:T(8,128)(2,1)S(1)} %shard_map.18), channel_id=1, replica_groups=mesh['z_lo'=4,'y'=4,'z_hi'=4,'x'=4,'core'=2] {'x'}, dimensions={0} | all-to-all | bytes 1605632 | tf_op jit(solution)/shard_map/all_to_all | solution.py:131
  55.7 0.1 convert_reduce_fusion.1
  55.9 12.9 %all-gather.1 = f16[224,896]{1,0:T(8,128)(2,1)S(1)} all-gather(f16[112,896]{1,0:T(8,128)(2,1)S(1)} %convert_element_type.66), channel_id=3, replica_groups={{0,8},{16,24},{9,17},{25,1},{2,10},{18,26},{11,19},{27,3},{4,12},{20,28..., dimensions={0}, use_global_device_ids=true | all-gather | bytes 602112 | tf_op jit(solution)/shard_map/all_gather | solution.py:166
  68.8 0.1 convert_reduce_fusion.3
  68.9 15.1 %all-gather.2 = f16[224,896]{1,0:T(8,128)(2,1)S(1)} all-gather(f16[112,896]{1,0:T(8,128)(2,1)S(1)} %convert_element_type.68), channel_id=4, replica_groups={{8,16},{24,0},{1,9},{17,25},{10,18},{26,2},{3,11},{19,27},{12,20},{28,4..., dimensions={0}, use_global_device_ids=true | all-gather | bytes 602112 | tf_op jit(solution)/shard_map/all_gather | solution.py:166
  84.0 0.1 convert_reduce_fusion.2
  84.1 4.0 %collective-permute-start = (bf16[4,112,576]{2,1,0:T(8,128)(2,1)S(1)}, bf16[4,112,576]{2,1,0:T(8,128)(2,1)S(1)}, u32[]{:S(2)}, u32[]{:S(2)}) collective-permute-start(bf16[4,112,576]{2,1,0:T(8,128)(2,1)S(1)} %shard_map.20), channel_id=1, source_target_pairs={{0,1},{1,0},{2,3},{3,2},{4,5},{5,4},{6,7},{7,6},{8,9},{9,8},{10,11... | collective-permute-start | bytes 1548296 | tf_op jit(solution)/shard_map/ppermute | solution.py:163
  88.1 15.1 %all-gather.8 = f16[896,896]{1,0:T(8,128)(2,1)S(1)} all-gather(f16[112,896]{1,0:T(8,128)(2,1)S(1)} %convert_element_type.71), channel_id=5, replica_groups=mesh['z_lo'=4,'y'=4,'z_hi'=4,'x'=4,'core'=2] {'x','core'}, dimensions={0}, use_global_device_ids=true | all-gather | bytes 1806336 | tf_op jit(solution)/shard_map/all_gather | solution.py:127
  103.2 0.3 convert_element_type.80.left
  103.5 0.0 collective-permute-done.other
  103.5 1.7 %shard_map.21 = bf16[4,1008,128]{2,1,0:T(8,128)(2,1)S(1)} custom-call(s32[1]{0:T(128)} %bitcast.core, bf16[896,896]{1,0:T(8,128)(2,1)S(1)} %convert_element_type.80.left, bf16[4,112,576]{2,1,0:T(8,128)(2,1)S(1)} %shard_map.19.mine, bf16[4,112,576]{2,1,0:T(8,128)(2,1)S(1)} %collective-permute-done.other), custom_call_target="tpu_custom_call" | custom-call | flops 924844032 | bytes 3670018 | tf_op jit(solution)/shard_map/pallas_call | solution.py:28
  105.2 20.6 %all_to_all.21 = bf16[4,1008,128]{2,1,0:T(8,128)(2,1)S(1)} all-to-all(bf16[4,1008,128]{2,1,0:T(8,128)(2,1)S(1)} %shard_map.21), channel_id=1, replica_groups=mesh['z_lo'=4,'y'=4,'z_hi'=4,'x'=4,'core'=2] {'y'}, dimensions={0} | all-to-all | bytes 2064384 | tf_op jit(solution)/shard_map/all_to_all | solution.py:131
  125.9 0.1 convert_reduce_fusion.once
  126.0 18.9 %all-gather.4 = bf16[4032,128]{1,0:T(8,128)(2,1)S(1)} all-gather(bf16[1008,128]{1,0:T(8,128)(2,1)S(1)} %convert_element_type.75), channel_id=6, replica_groups=mesh['z_lo'=4,'y'=4,'z_hi'=4,'x'=4,'core'=2] {'z_lo'}, dimensions={0}, use_global_device_ids=true | all-gather | bytes 1290240 | tf_op jit(solution)/shard_map/all_gather | solution.py:182
  145.0 1.8 %shard_map.22 = bf16[4,1008,128]{2,1,0:T(8,128)(2,1)S(1)} custom-call(bf16[896,896]{1,0:T(8,128)(2,1)S(1)} %convert_element_type.80.left, bf16[4,1008,128]{2,1,0:T(8,128)(2,1)S(1)} %bitcast.14), custom_call_target="tpu_custom_call" | custom-call | flops 924844032 | bytes 3670016 | tf_op jit(solution)/shard_map/pallas_call | solution.py:28
  146.7 0.0 copy-start.2
  146.8 14.5 %all_to_all.22.parts = bf16[4,1008,128]{2,1,0:T(8,128)(2,1)S(1)} all-to-all(bf16[4,1008,128]{2,1,0:T(8,128)(2,1)S(1)} %shard_map.22), channel_id=1, replica_groups=mesh['z_lo'=4,'y'=4,'z_hi'=4,'x'=4,'core'=2] {'y'}, dimensions={0} | all-to-all | bytes 2064384 | tf_op jit(solution)/shard_map/all_to_all | solution.py:131
  161.3 0.0 copy-done.2
  161.3 1.2 shard_map.23
  (4 shorter events, 0.1 us)
Async XLA Ops:
  0.0 1.0 copy-start
  1.0 11.4 %copy-start.1 = (bf16[224,576]{1,0:T(8,128)(2,1)S(1)}, bf16[224,576]{1,0:T(8,128)(2,1)}, u32[]{:S(2)}) copy-start(bf16[224,576]{1,0:T(8,128)(2,1)} %iterate.1) | copy-start | bytes 774148
  2.0 38.2 %all-to-all-start = ((bf16[8,112,576]{2,1,0:T(8,128)(2,1)}), bf16[8,112,576]{2,1,0:T(8,128)(2,1)S(1)}, u32[]{:S(2)}, u32[]{:S(2)}) async-start(bf16[8,112,576]{2,1,0:T(8,128)(2,1)} %bitcast.2), calls=%async_computation | async-start | bytes 2293760 | tf_op jit(solution)/shard_map/all_to_all | solution.py:131
  84.1 19.4 %collective-permute-start = (bf16[4,112,576]{2,1,0:T(8,128)(2,1)S(1)}, bf16[4,112,576]{2,1,0:T(8,128)(2,1)S(1)}, u32[]{:S(2)}, u32[]{:S(2)}) collective-permute-start(bf16[4,112,576]{2,1,0:T(8,128)(2,1)S(1)} %shard_map.20), channel_id=1, source_target_pairs={{0,1},{1,0},{2,3},{3,2},{4,5},{5,4},{6,7},{7,6},{8,9},{9,8},{10,11... | collective-permute-start | bytes 1548296 | tf_op jit(solution)/shard_map/ppermute | solution.py:163
  146.7 14.6 %copy-start.2 = (bf16[224,576]{1,0:T(8,128)(2,1)S(1)}, bf16[224,576]{1,0:T(8,128)(2,1)}, u32[]{:S(2)}) copy-start(bf16[224,576]{1,0:T(8,128)(2,1)} %iterate.1) | copy-start | bytes 774148

commit v14 on v12

--- a/solution.py
+++ b/solution.py
@@ -17,6 +17,8 @@
 
 LANES = 128
 PAIRS = [[0, 2], [4, 6], [3, 5], [7, 1]], [[2, 4], [6, 0], [1, 3], [5, 7]]
+GATHERS = [[0, 2], [4, 6], [3, 5], [1, 7]], [[2, 4], [0, 6], [1, 3], [7, 5]]
+ORDER = (0, 1, 2, 3), (0, 3, 1, 2)
 VMEM = pl.BlockSpec(memory_space=pltpu.VMEM)
 SMEM = pl.BlockSpec(memory_space=pltpu.SMEM)
 HBM = pl.BlockSpec(memory_space=pltpu.HBM)
@@ -81,13 +83,24 @@
         yield slice(k * each, (k + 1) * each), slice(whole * LANES, cols), slice(whole * rows, whole * rows + each), columns
 
 
+def half_pieces(half, rows, cols):
+    size = rows // 2
+    for row, col, packed_row, packed_col in pieces(rows, cols):
+        if row.stop - row.start == rows:
+            start = packed_row.start + half * size
+            yield col, slice(start, start + size), packed_col
+        elif row.start == half * size:
+            yield col, packed_row, packed_col
+
+
 def first_kernel(left, right, out):
-    product = dot(left[...], right[...], 0).astype(out.dtype)
-    rows = product.shape[0] // out.shape[0]
-    for i in range(out.shape[0]):
-        block = product[i * rows : (i + 1) * rows]
-        for row, col, packed_row, packed_col in pieces(rows, product.shape[1]):
-            out[i, packed_row, packed_col] = block[row, col]
+    halves, blocks, size, inner = left.shape
+    for half in range(halves):
+        product = dot(left[half].reshape(blocks * size, inner), right[...], 0).astype(out.dtype)
+        for i in range(blocks):
+            block = product[i * size : (i + 1) * size]
+            for col, packed_row, packed_col in half_pieces(half, 2 * size, product.shape[1]):
+                out[ORDER[half][i], packed_row, packed_col] = block[:, col]
 
 
 def second_kernel(left, right, out, held):
@@ -151,7 +164,12 @@
     for groups in PAIRS:
         piece = piece.astype(jnp.float16)
         piece = total(lax.all_gather(piece, ("z_hi", "core"), axis=0, axis_index_groups=groups))
-    gram = gather(piece, ("x", "core")).reshape(4 * rows, 4 * rows)
+    piece = piece.astype(jnp.float16)[None]
+    for groups in GATHERS:
+        piece = lax.all_gather(
+            piece, ("x", "core"), axis=0, tiled=True, axis_index_groups=groups
+        )
+    gram = lax.all_gather(piece, "core", axis=0).astype(jnp.bfloat16)
 
     packed = bf16(4, rows * cols // LANES, LANES)
     flops = 2 * gram.size * cols

time: 161 us -> 165 us (1.025)
  blocking collectives: 146 us -> 151 us
    all_gather x0 -> x3, blocking collectives: none -> 20.4 us  [the longest x2 17.5 us: shards(): lax.all_gather(piece, ('x', 'core'), axis=0, tiled=True, axis_index_group...]
    all_gather x2 -> x1, blocking collectives: 40.4 us -> 25.6 us  [gather(): lax.all_gather(array.astype(jnp.float16), axes, axis=0).astype(jnp.bfloat16)]
where the time goes in v14:
time: 165 us
  blocking collectives  151 us (92%)
  Pallas kernels  7.16 us (4%)
  starting transfers between devices  4.48 us (3%)
    all_to_all x3, blocking collectives, exchange(): return lax.all_to_all(array, axes, 0, 0, tiled=True)  51.4 us
    all_gather x2, blocking collectives, shards(): lax.all_gather(piece, ('z_hi', 'core'), axis=0, axis_index_groups=groups)  28 us
    all_gather x1, blocking collectives, shards(): lax.all_gather(once.astype(jnp.bfloat16), 'z_lo', axis=0)  25.7 us
    all_gather x1, blocking collectives, gather(): lax.all_gather(array.astype(jnp.float16), axes, axis=0).astype(jnp.bfloat16)  25.6 us
    all_gather x2, blocking collectives, shards(): lax.all_gather(piece, ('x', 'core'), axis=0, tiled=True, axis_index_group...  17.5 us
    pallas_call x6, Pallas kernels, call(): pl.pallas_call(kernel, out_shape=output, in_specs=in_specs, out_specs=spe...  7.16 us
    all_to_all x1, starting transfers between devices, exchange(): return lax.all_to_all(array, axes, 0, 0, tiled=True)  4.48 us
  transfers between devices with their start and end apart: 1, of which 0 were waited for; matrix products, arithmetic and copies ran while one was open for 0% of the time, Pallas kernels for 0%

profile of v14, /device:TPU:32, one launch (start us, length us, event | category | flops | bytes accessed | tf_op | source)
XLA Modules:
  0.0 165.1 jit_solution(7326645048593730612)
XLA Ops:
  0.0 0.0 copy-start
  0.0 1.0 copy-done
  1.0 0.0 copy-start.1
  1.0 1.0 shard_map.17
  2.0 4.5 %all-to-all-start = ((bf16[8,112,576]{2,1,0:T(8,128)(2,1)}), bf16[8,112,576]{2,1,0:T(8,128)(2,1)S(1)}, u32[]{:S(2)}, u32[]{:S(2)}) async-start(bf16[8,112,576]{2,1,0:T(8,128)(2,1)} %bitcast.1), calls=%async_computation | async-start | bytes 2293760 | tf_op jit(solution)/shard_map/all_to_all | solution.py:135
  6.5 0.0 copy-done.1
  6.5 0.1 convert_element_type.73
  6.6 25.6 %all-gather.8 = f16[1792,576]{1,0:T(8,128)(2,1)S(1)} all-gather(f16[224,576]{1,0:T(8,128)(2,1)S(1)} %convert_element_type.73), channel_id=2, replica_groups=mesh['z_lo'=4,'y'=4,'z_hi'=4,'x'=4,'core'=2] {'z_lo','core'}, dimensions={0}, use_global_device_ids=true | all-gather | bytes 2322432 | tf_op jit(solution)/shard_map/all_gather | solution.py:131
  32.1 0.4 convert_element_type.88
  32.6 0.0 all-to-all-done
  32.6 1.6 shard_map.18
  34.2 0.1 shard_map.19.right
  34.3 16.9 %all_to_all.20 = bf16[4,112,896]{2,1,0:T(8,128)(2,1)S(1)} all-to-all(bf16[4,112,896]{2,1,0:T(8,128)(2,1)S(1)} %shard_map.18), channel_id=1, replica_groups=mesh['z_lo'=4,'y'=4,'z_hi'=4,'x'=4,'core'=2] {'x'}, dimensions={0} | all-to-all | bytes 1605632 | tf_op jit(solution)/shard_map/all_to_all | solution.py:135
  51.2 0.1 convert_reduce_fusion.1
  51.3 17.4 %all-gather.1 = f16[224,896]{1,0:T(8,128)(2,1)S(1)} all-gather(f16[112,896]{1,0:T(8,128)(2,1)S(1)} %convert_element_type.76), channel_id=3, replica_groups={{0,8},{16,24},{9,17},{25,1},{2,10},{18,26},{11,19},{27,3},{4,12},{20,28..., dimensions={0}, use_global_device_ids=true | all-gather | bytes 602112 | tf_op jit(solution)/shard_map/all_gather | solution.py:166
  68.7 0.1 convert_reduce_fusion.3
  68.8 10.6 %all-gather.2 = f16[224,896]{1,0:T(8,128)(2,1)S(1)} all-gather(f16[112,896]{1,0:T(8,128)(2,1)S(1)} %convert_element_type.79), channel_id=4, replica_groups={{8,16},{24,0},{1,9},{17,25},{10,18},{26,2},{3,11},{19,27},{12,20},{28,4..., dimensions={0}, use_global_device_ids=true | all-gather | bytes 602112 | tf_op jit(solution)/shard_map/all_gather | solution.py:166
  79.4 0.1 convert_reduce_fusion.2
  79.5 7.7 %all-gather.3 = f16[224,896]{1,0:T(8,128)(2,1)S(1)} all-gather(f16[112,896]{1,0:T(8,128)(2,1)S(1)} %convert_element_type.82), channel_id=5, replica_groups={{0,2},{4,6},{3,5},{1,7},{8,10},{12,14},{11,13},{9,15},{16,18},{20,22},{..., dimensions={0}, use_global_device_ids=true | all-gather | bytes 602112 | tf_op jit(solution)/shard_map/all_gather | solution.py:169
  87.3 9.7 %all_gather.35 = f16[4,112,896]{2,1,0:T(8,128)(2,1)S(1)} all-gather(f16[2,112,896]{2,1,0:T(8,128)(2,1)S(1)} %bitcast.21), channel_id=1, replica_groups={{2,4},{0,6},{1,3},{7,5},{10,12},{8,14},{9,11},{15,13},{18,20},{16,22},{..., dimensions={0}, use_global_device_ids=true | all-gather | bytes 1204224 | tf_op jit(solution)/shard_map/all_gather | solution.py:169
  97.0 2.9 %all-gather.9 = f16[8,112,896]{2,1,0:T(8,128)(2,1)S(1)} all-gather(f16[4,112,896]{2,1,0:T(8,128)(2,1)S(1)} %all_gather.35), channel_id=6, replica_groups=mesh['z_lo'=4,'y'=4,'z_hi'=4,'x'=4,'core'=2] {'core'}, dimensions={0}, use_global_device_ids=true | all-gather | bytes 2408448 | tf_op jit(solution)/shard_map/all_gather | solution.py:172
  100.0 0.3 convert_element_type.91
  100.2 1.6 shard_map.20
  101.8 19.2 %all_to_all.21 = bf16[4,1008,128]{2,1,0:T(8,128)(2,1)S(1)} all-to-all(bf16[4,1008,128]{2,1,0:T(8,128)(2,1)S(1)} %shard_map.20), channel_id=1, replica_groups=mesh['z_lo'=4,'y'=4,'z_hi'=4,'x'=4,'core'=2] {'y'}, dimensions={0} | all-to-all | bytes 2064384 | tf_op jit(solution)/shard_map/all_to_all | solution.py:135
  121.0 0.1 convert_reduce_fusion.once
  121.2 25.7 %all-gather.5 = bf16[4032,128]{1,0:T(8,128)(2,1)S(1)} all-gather(bf16[1008,128]{1,0:T(8,128)(2,1)S(1)} %convert_element_type.86), channel_id=7, replica_groups=mesh['z_lo'=4,'y'=4,'z_hi'=4,'x'=4,'core'=2] {'z_lo'}, dimensions={0}, use_global_device_ids=true | all-gather | bytes 1290240 | tf_op jit(solution)/shard_map/all_gather | solution.py:180
  146.9 1.7 %shard_map.21 = bf16[4,1008,128]{2,1,0:T(8,128)(2,1)S(1)} custom-call(bf16[2,4,112,896]{3,2,1,0:T(8,128)(2,1)S(1)} %bitcast.15, bf16[4,1008,128]{2,1,0:T(8,128)(2,1)S(1)} %bitcast.17), custom_call_target="tpu_custom_call" | custom-call | flops 924844032 | bytes 3670016 | tf_op jit(solution)/shard_map/pallas_call | solution.py:30
  148.6 0.0 copy-start.2
  148.6 15.3 %all_to_all.22.parts = bf16[4,1008,128]{2,1,0:T(8,128)(2,1)S(1)} all-to-all(bf16[4,1008,128]{2,1,0:T(8,128)(2,1)S(1)} %shard_map.21), channel_id=1, replica_groups=mesh['z_lo'=4,'y'=4,'z_hi'=4,'x'=4,'core'=2] {'y'}, dimensions={0} | all-to-all | bytes 2064384 | tf_op jit(solution)/shard_map/all_to_all | solution.py:135
  164.0 0.0 copy-done.2
  164.0 1.2 shard_map.22
  (4 shorter events, 0.1 us)
Async XLA Ops:
  0.0 1.0 copy-start
  1.0 5.5 %copy-start.1 = (bf16[224,576]{1,0:T(8,128)(2,1)S(1)}, bf16[224,576]{1,0:T(8,128)(2,1)}, u32[]{:S(2)}) copy-start(bf16[224,576]{1,0:T(8,128)(2,1)} %iterate.1) | copy-start | bytes 774148
  2.0 30.6 %all-to-all-start = ((bf16[8,112,576]{2,1,0:T(8,128)(2,1)}), bf16[8,112,576]{2,1,0:T(8,128)(2,1)S(1)}, u32[]{:S(2)}, u32[]{:S(2)}) async-start(bf16[8,112,576]{2,1,0:T(8,128)(2,1)} %bitcast.1), calls=%async_computation | async-start | bytes 2293760 | tf_op jit(solution)/shard_map/all_to_all | solution.py:135
  148.6 15.4 %copy-start.2 = (bf16[224,576]{1,0:T(8,128)(2,1)S(1)}, bf16[224,576]{1,0:T(8,128)(2,1)}, u32[]{:S(2)}) copy-start(bf16[224,576]{1,0:T(8,128)(2,1)} %iterate.1) | copy-start | bytes 774148

commit v15 on v9

v15 whole, which is shorter than its diff:
```python
import math

import jax
import jax.numpy as jnp
from jax import lax
from jax.experimental import pallas as pl
from jax.experimental.pallas import tpu as pltpu
from jax.sharding import Mesh
from jax.sharding import PartitionSpec as P

D = 3584
FF = 18432

coef_linear = 3.4445
coef_cubic = -4.775
coef_quintic = 2.0315

LANES = 128
PAIRS = [[0, 2], [4, 6], [3, 5], [7, 1]], [[2, 4], [6, 0], [1, 3], [5, 7]]
VMEM = pl.BlockSpec(memory_space=pltpu.VMEM)
SMEM = pl.BlockSpec(memory_space=pltpu.SMEM)
HBM = pl.BlockSpec(memory_space=pltpu.HBM)
ANY = pl.BlockSpec(memory_space=pl.ANY)


def call(kernel, operands, output, spec=VMEM, scratch=(), flops=0):
    arrays, in_specs = zip(*operands)
    return pl.pallas_call(
        kernel,
        out_shape=output,
        in_specs=in_specs,
        out_specs=spec,
        scratch_shapes=scratch,
        compiler_params=pltpu.CompilerParams(vmem_limit_bytes=16 * 1024 * 1024),
        cost_estimate=pl.CostEstimate(
            flops=flops,
            bytes_accessed=2 * sum(math.prod(array.shape) for array in arrays),
            transcendentals=0,
        ),
    )(*arrays)


def bf16(*shape):
    return jax.ShapeDtypeStruct(shape, jnp.bfloat16)


def dot(lhs, rhs, rhs_dim):
    return lax.dot_general(
        lhs, rhs, (((1,), (rhs_dim,)), ((), ())), preferred_element_type=jnp.float32
    )


def pieces(rows, cols):
    whole, rest = cols // LANES, cols % LANES
    for k in range(whole):
        yield slice(0, rows), slice(k * LANES, (k + 1) * LANES), slice(k * rows, (k + 1) * rows), slice(0, LANES)
    each = rows * rest // LANES
    for k in range(LANES // rest if rest else 0):
        columns = slice(k * rest, (k + 1) * rest)
        yield slice(k * each, (k + 1) * each), slice(whole * LANES, cols), slice(whole * rows, whole * rows + each), columns


def unpack(packed, out):
    rows = out.shape[0] // packed.shape[0]
    for i in range(packed.shape[0]):
        for row, col, packed_row, packed_col in pieces(rows, out.shape[1]):
            row = slice(i * rows + row.start, i * rows + row.stop)
            out[row, col] = packed[i, packed_row, packed_col]


def first_kernel(array, out, packed, sems):
    copies = [pltpu.make_async_copy(array, out.at[i], sems.at[i]) for i in range(out.shape[0])]
    for copy in copies:
        copy.start()
    for row, col, packed_row, packed_col in pieces(*array.shape):
        packed[packed_row, packed_col] = array[row, col]
    for copy in copies:
        copy.wait()


def gram_kernel(left, right, out, held):
    blocks, cores, rows, cols = left.shape
    tile = jnp.zeros((blocks * rows, out.shape[-1]), jnp.float32)
    for k in range(cores):
        unpack(right.at[:, k], held.at[k])
        tile += dot(left[:, k].reshape(blocks * rows, cols), held[k], 1)
    out[...] = tile.astype(out.dtype).reshape(out.shape)


def own_kernel(core, right, out):
    out[...] = right[:, pl.ds(core[0], 1)].reshape(out.shape)


def product_kernel(left, right, out, held):
    unpack(right, held)
    product = dot(left[...], held[...], 0).astype(out.dtype)
    rows = product.shape[0] // out.shape[0]
    for i in range(out.shape[0]):
        block = product[i * rows : (i + 1) * rows]
        for row, col, packed_row, packed_col in pieces(rows, product.shape[1]):
            out[i, packed_row, packed_col] = block[row, col]


def update_kernel(iterate, once, parts, out, held, sem):
    fetch = pltpu.make_async_copy(iterate, held, sem)
    fetch.start()
    packed = coef_cubic * once[...]
    packed += coef_quintic * jnp.sum(parts[...].astype(jnp.float32), axis=0)
    fetch.wait()
    for row, col, packed_row, packed_col in pieces(*out.shape):
        step = coef_linear * held[row, col].astype(jnp.float32) + packed[packed_row, packed_col]
        out[row, col] = (0.2 * math.sqrt(max(D, FF)) * step).astype(out.dtype)


def total(parts):
    return jnp.sum(parts.astype(jnp.float32), axis=0)


def gather(array, axes):
    return lax.all_gather(array.astype(jnp.float16), axes, axis=0).astype(jnp.bfloat16)


def exchange(array, axes):
    return lax.all_to_all(array, axes, 0, 0, tiled=True)


def shards(iterate):
    rows, cols = iterate.shape
    half = rows // 2
    core = lax.axis_index("core").astype(jnp.int32).reshape(1)
    sems = pltpu.SemaphoreType.DMA

    packed = rows * cols // LANES
    left, right = call(
        first_kernel,
        [(iterate, VMEM)],
        (bf16(4, rows, cols), bf16(packed, LANES)),
        spec=(HBM, VMEM),
        scratch=[sems((4,))],
    )
    left = exchange(left.reshape(8, half, cols), ("y", "core")).reshape(4, 2, half, cols)
    right = gather(right, ("z_lo", "core")).reshape(4, 2, packed, LANES)

    tile = call(
        gram_kernel,
        [(left, VMEM), (right, VMEM)],
        bf16(4, half, 4 * rows),
        scratch=[pltpu.VMEM((2, 4 * rows, cols), jnp.bfloat16)],
        flops=4 * 4 * half * 4 * rows * cols,
    )
    tile, right = lax.optimization_barrier((tile, right))
    own = call(own_kernel, [(core, SMEM), (right, VMEM)], bf16(4, packed, LANES))
    tile, own = lax.optimization_barrier((tile, own))
    piece = total(exchange(tile, "x"))
    for groups in PAIRS:
        piece = piece.astype(jnp.float16)
        piece = total(lax.all_gather(piece, ("z_hi", "core"), axis=0, axis_index_groups=groups))
    gram = gather(piece, ("x", "core")).reshape(4 * rows, 4 * rows)

    def gram_times(array):
        parts = call(
            product_kernel,
            [(gram, VMEM), (array, VMEM)],
            bf16(4, packed, LANES),
            scratch=[pltpu.VMEM((4 * rows, cols), jnp.bfloat16)],
            flops=2 * gram.size * cols,
        )
        return exchange(parts, "y")

    once = total(gram_times(own))
    twice = gram_times(lax.all_gather(once.astype(jnp.bfloat16), "z_lo", axis=0))
    return call(
        update_kernel,
        [(iterate, ANY), (once, VMEM), (twice, VMEM)],
        bf16(rows, cols),
        scratch=[pltpu.VMEM(iterate.shape, iterate.dtype), sems],
    )


def solution(mesh):
    axes = ("z_lo", "y", "z_hi", "x", "core")
    fine = Mesh(mesh.devices.reshape(4, 4, 4, 4, 2), axes)
    placed = P(axes[:2], axes[2:])
    return jax.shard_map(
        shards, mesh=fine, in_specs=(placed,), out_specs=placed, check_vma=False
    )
```

time: 174 us -> 158 us (0.908)
  waiting for transfers between devices: 12.4 us -> 0.01 us
  starting transfers between devices: 14.7 us -> 10.4 us
  blocking collectives: 133 us -> 136 us
    all_to_all x2 -> x3, blocking collectives: 34.5 us -> 47.7 us  [exchange(): return lax.all_to_all(array, axes, 0, 0, tiled=True)]
    all_to_all x2 -> x1, waiting for transfers between devices: 12.4 us -> 0.01 us  [exchange(): return lax.all_to_all(array, axes, 0, 0, tiled=True)]
    all_gather x2 -> x3, blocking collectives: 58.5 us -> 49.7 us  [the longest x2 30.8 us: shards(): lax.all_gather(piece, ('z_hi', 'core'), axis=0, axis_index_groups=groups)]
    all_to_all x2 -> x1, starting transfers between devices: 14.7 us -> 10.4 us  [exchange(): return lax.all_to_all(array, axes, 0, 0, tiled=True)]
  transfers between devices with their start and end apart: 2 -> 1, of which waited for: 1 -> 0; matrix products, arithmetic and copies ran while one was open for 0% -> 0% of each run, Pallas kernels for 0% -> 0%
where the time goes in v15:
time: 158 us; the launch traced here: 156 us
  blocking collectives  136 us (86%)
  starting transfers between devices  10.4 us (7%)
  Pallas kernels  7.42 us (5%)
    all_to_all x3, blocking collectives, exchange(): return lax.all_to_all(array, axes, 0, 0, tiled=True)  47.7 us
    all_gather x2, blocking collectives, gather(): lax.all_gather(array.astype(jnp.float16), axes, axis=0).astype(jnp.bfloat16)  38.7 us
    all_gather x2, blocking collectives, shards(): lax.all_gather(piece, ('z_hi', 'core'), axis=0, axis_index_groups=groups)  30.8 us
    all_gather x1, blocking collectives, shards(): lax.all_gather(once.astype(jnp.bfloat16), 'z_lo', axis=0)  18.9 us
    all_to_all x1, starting transfers between devices, exchange(): return lax.all_to_all(array, axes, 0, 0, tiled=True)  10.4 us
    pallas_call x6, Pallas kernels, call(): pl.pallas_call(kernel, out_shape=output, in_specs=in_specs, out_specs=spe...  7.42 us
  transfers between devices with their start and end apart: 1, of which 0 were waited for; matrix products, arithmetic and copies ran while one was open for 0% of the time, Pallas kernels for 0%

profile of v15, /device:TPU:1, one launch (start us, length us, event | category | flops | bytes accessed | tf_op | source)
XLA Modules:
  0.0 156.0 jit_solution(2905077816417960527)
XLA Ops:
  0.0 0.0 copy-start
  0.0 1.0 copy-done
  1.0 1.0 shard_map.17
  2.0 10.4 %all-to-all-start = ((bf16[8,112,576]{2,1,0:T(8,128)(2,1)}), bf16[8,112,576]{2,1,0:T(8,128)(2,1)S(1)}, u32[]{:S(2)}, u32[]{:S(2)}) async-start(bf16[8,112,576]{2,1,0:T(8,128)(2,1)} %bitcast), calls=%async_computation | async-start | bytes 2293760 | tf_op jit(solution)/shard_map/all_to_all | solution.py:124
  12.4 0.1 convert_element_type.73
  12.4 22.6 %all-gather.7 = f16[8064,128]{1,0:T(8,128)(2,1)S(1)} all-gather(f16[1008,128]{1,0:T(8,128)(2,1)S(1)} %convert_element_type.73), channel_id=2, replica_groups=mesh['z_lo'=4,'y'=4,'z_hi'=4,'x'=4,'core'=2] {'z_lo','core'}, dimensions={0}, use_global_device_ids=true | all-gather | bytes 2322432 | tf_op jit(solution)/shard_map/all_gather | solution.py:120
  35.0 0.2 convert_element_type.88
  35.2 0.0 all-to-all-done
  35.2 1.7 %shard_map.18 = bf16[4,112,896]{2,1,0:T(8,128)(2,1)S(1)} custom-call(bf16[4,2,112,576]{3,2,1,0:T(8,128)(2,1)S(1)} %bitcast.11, bf16[4,2,1008,128]{3,2,1,0:T(8,128)(2,1)S(1)} %bitcast.9), custom_call_target="tpu_custom_call" | custom-call | flops 924844032 | bytes 3096576 | tf_op jit(solution)/shard_map/pallas_call | solution.py:28
  36.9 0.1 shard_map.19.right
  37.0 14.5 %all_to_all.20 = bf16[4,112,896]{2,1,0:T(8,128)(2,1)S(1)} all-to-all(bf16[4,112,896]{2,1,0:T(8,128)(2,1)S(1)} %shard_map.18), channel_id=1, replica_groups=mesh['z_lo'=4,'y'=4,'z_hi'=4,'x'=4,'core'=2] {'x'}, dimensions={0} | all-to-all | bytes 1605632 | tf_op jit(solution)/shard_map/all_to_all | solution.py:124
  51.5 0.1 convert_reduce_fusion.1
  51.7 16.6 %all-gather.1 = f16[224,896]{1,0:T(8,128)(2,1)S(1)} all-gather(f16[112,896]{1,0:T(8,128)(2,1)S(1)} %convert_element_type.76), channel_id=3, replica_groups={{0,8},{16,24},{9,17},{25,1},{2,10},{18,26},{11,19},{27,3},{4,12},{20,28..., dimensions={0}, use_global_device_ids=true | all-gather | bytes 602112 | tf_op jit(solution)/shard_map/all_gather | solution.py:157
  68.2 0.1 convert_reduce_fusion.3
  68.3 14.2 %all-gather.2 = f16[224,896]{1,0:T(8,128)(2,1)S(1)} all-gather(f16[112,896]{1,0:T(8,128)(2,1)S(1)} %convert_element_type.79), channel_id=4, replica_groups={{8,16},{24,0},{1,9},{17,25},{10,18},{26,2},{3,11},{19,27},{12,20},{28,4..., dimensions={0}, use_global_device_ids=true | all-gather | bytes 602112 | tf_op jit(solution)/shard_map/all_gather | solution.py:157
  82.6 0.1 convert_reduce_fusion.2
  82.7 16.1 %all-gather.8 = f16[896,896]{1,0:T(8,128)(2,1)S(1)} all-gather(f16[112,896]{1,0:T(8,128)(2,1)S(1)} %convert_element_type.82), channel_id=5, replica_groups=mesh['z_lo'=4,'y'=4,'z_hi'=4,'x'=4,'core'=2] {'x','core'}, dimensions={0}, use_global_device_ids=true | all-gather | bytes 1806336 | tf_op jit(solution)/shard_map/all_gather | solution.py:120
  98.8 0.3 convert_element_type.91.left
  99.0 1.7 %shard_map.20 = bf16[4,1008,128]{2,1,0:T(8,128)(2,1)S(1)} custom-call(bf16[896,896]{1,0:T(8,128)(2,1)S(1)} %convert_element_type.91.left, bf16[4,1008,128]{2,1,0:T(8,128)(2,1)S(1)} %shard_map.19.right), custom_call_target="tpu_custom_call" | custom-call | flops 924844032 | bytes 2637824 | tf_op jit(solution)/shard_map/pallas_call | solution.py:28
  100.8 18.7 %all_to_all.21 = bf16[4,1008,128]{2,1,0:T(8,128)(2,1)S(1)} all-to-all(bf16[4,1008,128]{2,1,0:T(8,128)(2,1)S(1)} %shard_map.20), channel_id=1, replica_groups=mesh['z_lo'=4,'y'=4,'z_hi'=4,'x'=4,'core'=2] {'y'}, dimensions={0} | all-to-all | bytes 2064384 | tf_op jit(solution)/shard_map/all_to_all | solution.py:124
  119.5 0.1 convert_reduce_fusion.once
  119.6 18.9 %all-gather.4 = bf16[4032,128]{1,0:T(8,128)(2,1)S(1)} all-gather(bf16[1008,128]{1,0:T(8,128)(2,1)S(1)} %convert_element_type.86), channel_id=6, replica_groups=mesh['z_lo'=4,'y'=4,'z_hi'=4,'x'=4,'core'=2] {'z_lo'}, dimensions={0}, use_global_device_ids=true | all-gather | bytes 1290240 | tf_op jit(solution)/shard_map/all_gather | solution.py:171
  138.6 1.7 %shard_map.21 = bf16[4,1008,128]{2,1,0:T(8,128)(2,1)S(1)} custom-call(bf16[896,896]{1,0:T(8,128)(2,1)S(1)} %convert_element_type.91.left, bf16[4,1008,128]{2,1,0:T(8,128)(2,1)S(1)} %bitcast.12), custom_call_target="tpu_custom_call" | custom-call | flops 924844032 | bytes 2637824 | tf_op jit(solution)/shard_map/pallas_call | solution.py:28
  140.4 0.0 copy-start.1
  140.4 14.4 %all_to_all.22.parts = bf16[4,1008,128]{2,1,0:T(8,128)(2,1)S(1)} all-to-all(bf16[4,1008,128]{2,1,0:T(8,128)(2,1)S(1)} %shard_map.21), channel_id=1, replica_groups=mesh['z_lo'=4,'y'=4,'z_hi'=4,'x'=4,'core'=2] {'y'}, dimensions={0} | all-to-all | bytes 2064384 | tf_op jit(solution)/shard_map/all_to_all | solution.py:124
  154.8 0.0 copy-done.1
  154.8 1.2 shard_map.22
  (4 shorter events, 0.1 us)
Async XLA Ops:
  0.0 1.0 copy-start
  2.0 33.2 %all-to-all-start = ((bf16[8,112,576]{2,1,0:T(8,128)(2,1)}), bf16[8,112,576]{2,1,0:T(8,128)(2,1)S(1)}, u32[]{:S(2)}, u32[]{:S(2)}) async-start(bf16[8,112,576]{2,1,0:T(8,128)(2,1)} %bitcast), calls=%async_computation | async-start | bytes 2293760 | tf_op jit(solution)/shard_map/all_to_all | solution.py:124
  140.4 14.4 %copy-start.1 = (bf16[224,576]{1,0:T(8,128)(2,1)S(1)}, bf16[224,576]{1,0:T(8,128)(2,1)}, u32[]{:S(2)}) copy-start(bf16[224,576]{1,0:T(8,128)(2,1)} %iterate.1) | copy-start | bytes 774148

commit v16 on v15

--- a/solution.py
+++ b/solution.py
@@ -23,7 +23,7 @@
 ANY = pl.BlockSpec(memory_space=pl.ANY)
 
 
-def call(kernel, operands, output, spec=VMEM, scratch=(), flops=0):
+def call(kernel, operands, output, spec=VMEM, scratch=(), flops=0, vmem=16):
     arrays, in_specs = zip(*operands)
     return pl.pallas_call(
         kernel,
@@ -31,7 +31,7 @@
         in_specs=in_specs,
         out_specs=spec,
         scratch_shapes=scratch,
-        compiler_params=pltpu.CompilerParams(vmem_limit_bytes=16 * 1024 * 1024),
+        compiler_params=pltpu.CompilerParams(vmem_limit_bytes=vmem * 1024 * 1024),
         cost_estimate=pl.CostEstimate(
             flops=flops,
             bytes_accessed=2 * sum(math.prod(array.shape) for array in arrays),
@@ -68,12 +68,16 @@
             out[row, col] = packed[i, packed_row, packed_col]
 
 
-def first_kernel(array, out, packed, sems):
-    copies = [pltpu.make_async_copy(array, out.at[i], sems.at[i]) for i in range(out.shape[0])]
+def first_kernel(array, out, packed, held, sems):
+    count = out.shape[0]
+    fetch = pltpu.make_async_copy(array, held, sems.at[count])
+    fetch.start()
+    fetch.wait()
+    copies = [pltpu.make_async_copy(held, out.at[i], sems.at[i]) for i in range(count)]
     for copy in copies:
         copy.start()
-    for row, col, packed_row, packed_col in pieces(*array.shape):
-        packed[packed_row, packed_col] = array[row, col]
+    for row, col, packed_row, packed_col in pieces(*held.shape):
+        packed[packed_row, packed_col] = held[row, col]
     for copy in copies:
         copy.wait()
 
@@ -133,10 +137,11 @@
     packed = rows * cols // LANES
     left, right = call(
         first_kernel,
-        [(iterate, VMEM)],
+        [(iterate, ANY)],
         (bf16(4, rows, cols), bf16(packed, LANES)),
         spec=(HBM, VMEM),
-        scratch=[sems((4,))],
+        scratch=[pltpu.VMEM(iterate.shape, iterate.dtype), sems((5,))],
+        vmem=56,
     )
     left = exchange(left.reshape(8, half, cols), ("y", "core")).reshape(4, 2, half, cols)
     right = gather(right, ("z_lo", "core")).reshape(4, 2, packed, LANES)

time: 158 us -> 159 us (level)
  Pallas kernels: 7.42 us -> 9.07 us
    pallas_call x6, Pallas kernels: 7.42 us -> 9.07 us  [call(): pl.pallas_call(kernel, out_shape=output, in_specs=in_specs, out_specs=spe...]
where the time goes in v16:
time: 159 us; the launch traced here: 157 us
  blocking collectives  136 us (86%)
  starting transfers between devices  10.5 us (7%)
  Pallas kernels  9.07 us (6%)
    all_to_all x3, blocking collectives, exchange(): return lax.all_to_all(array, axes, 0, 0, tiled=True)  47.7 us
    all_gather x2, blocking collectives, gather(): lax.all_gather(array.astype(jnp.float16), axes, axis=0).astype(jnp.bfloat16)  38.7 us
    all_gather x2, blocking collectives, shards(): lax.all_gather(piece, ('z_hi', 'core'), axis=0, axis_index_groups=groups)  30.8 us
    all_gather x1, blocking collectives, shards(): lax.all_gather(once.astype(jnp.bfloat16), 'z_lo', axis=0)  18.9 us
    all_to_all x1, starting transfers between devices, exchange(): return lax.all_to_all(array, axes, 0, 0, tiled=True)  10.5 us
    pallas_call x6, Pallas kernels, call(): pl.pallas_call(kernel, out_shape=output, in_specs=in_specs, out_specs=spe...  9.07 us
  transfers between devices with their start and end apart: 1, of which 0 were waited for; matrix products, arithmetic and copies ran while one was open for 0% of the time, Pallas kernels for 0%

profile of v16, /device:TPU:1, one launch (start us, length us, event | category | flops | bytes accessed | tf_op | source)
XLA Modules:
  0.0 156.8 jit_solution(15944019580667836350)
XLA Ops:
  0.0 2.7 %shard_map.17 = (bf16[4,224,576]{2,1,0:T(8,128)(2,1)}, bf16[1008,128]{1,0:T(8,128)(2,1)}) custom-call(bf16[224,576]{1,0:T(8,128)(2,1)} %iterate.1), custom_call_target="tpu_custom_call" | custom-call | bytes 258048 | tf_op jit(solution)/shard_map/pallas_call | solution.py:28
  2.7 0.0 copy-start.1
  2.7 10.5 %all-to-all-start = ((bf16[8,112,576]{2,1,0:T(8,128)(2,1)}), bf16[8,112,576]{2,1,0:T(8,128)(2,1)S(1)}, u32[]{:S(2)}, u32[]{:S(2)}) async-start(bf16[8,112,576]{2,1,0:T(8,128)(2,1)} %bitcast.15), calls=%async_computation | async-start | bytes 2293760 | tf_op jit(solution)/shard_map/all_to_all | solution.py:128
  13.2 0.0 copy-done.1
  13.2 0.1 convert_element_type.73
  13.3 22.5 %all-gather.7 = f16[8064,128]{1,0:T(8,128)(2,1)S(1)} all-gather(f16[1008,128]{1,0:T(8,128)(2,1)S(1)} %convert_element_type.73), channel_id=2, replica_groups=mesh['z_lo'=4,'y'=4,'z_hi'=4,'x'=4,'core'=2] {'z_lo','core'}, dimensions={0}, use_global_device_ids=true | all-gather | bytes 2322432 | tf_op jit(solution)/shard_map/all_gather | solution.py:124
  35.8 0.2 convert_element_type.88
  36.0 0.0 all-to-all-done
  36.0 1.7 %shard_map.18 = bf16[4,112,896]{2,1,0:T(8,128)(2,1)S(1)} custom-call(bf16[4,2,112,576]{3,2,1,0:T(8,128)(2,1)S(1)} %bitcast.11, bf16[4,2,1008,128]{3,2,1,0:T(8,128)(2,1)S(1)} %bitcast.9), custom_call_target="tpu_custom_call" | custom-call | flops 924844032 | bytes 3096576 | tf_op jit(solution)/shard_map/pallas_call | solution.py:28
  37.7 0.1 shard_map.19.right
  37.8 14.5 %all_to_all.20 = bf16[4,112,896]{2,1,0:T(8,128)(2,1)S(1)} all-to-all(bf16[4,112,896]{2,1,0:T(8,128)(2,1)S(1)} %shard_map.18), channel_id=1, replica_groups=mesh['z_lo'=4,'y'=4,'z_hi'=4,'x'=4,'core'=2] {'x'}, dimensions={0} | all-to-all | bytes 1605632 | tf_op jit(solution)/shard_map/all_to_all | solution.py:128
  52.3 0.1 convert_reduce_fusion.1
  52.5 16.6 %all-gather.1 = f16[224,896]{1,0:T(8,128)(2,1)S(1)} all-gather(f16[112,896]{1,0:T(8,128)(2,1)S(1)} %convert_element_type.76), channel_id=3, replica_groups={{0,8},{16,24},{9,17},{25,1},{2,10},{18,26},{11,19},{27,3},{4,12},{20,28..., dimensions={0}, use_global_device_ids=true | all-gather | bytes 602112 | tf_op jit(solution)/shard_map/all_gather | solution.py:162
  69.1 0.1 convert_reduce_fusion.3
  69.2 14.2 %all-gather.2 = f16[224,896]{1,0:T(8,128)(2,1)S(1)} all-gather(f16[112,896]{1,0:T(8,128)(2,1)S(1)} %convert_element_type.79), channel_id=4, replica_groups={{8,16},{24,0},{1,9},{17,25},{10,18},{26,2},{3,11},{19,27},{12,20},{28,4..., dimensions={0}, use_global_device_ids=true | all-gather | bytes 602112 | tf_op jit(solution)/shard_map/all_gather | solution.py:162
  83.4 0.1 convert_reduce_fusion.2
  83.5 16.1 %all-gather.8 = f16[896,896]{1,0:T(8,128)(2,1)S(1)} all-gather(f16[112,896]{1,0:T(8,128)(2,1)S(1)} %convert_element_type.82), channel_id=5, replica_groups=mesh['z_lo'=4,'y'=4,'z_hi'=4,'x'=4,'core'=2] {'x','core'}, dimensions={0}, use_global_device_ids=true | all-gather | bytes 1806336 | tf_op jit(solution)/shard_map/all_gather | solution.py:124
  99.6 0.3 convert_element_type.91.left
  99.8 1.7 %shard_map.20 = bf16[4,1008,128]{2,1,0:T(8,128)(2,1)S(1)} custom-call(bf16[896,896]{1,0:T(8,128)(2,1)S(1)} %convert_element_type.91.left, bf16[4,1008,128]{2,1,0:T(8,128)(2,1)S(1)} %shard_map.19.right), custom_call_target="tpu_custom_call" | custom-call | flops 924844032 | bytes 2637824 | tf_op jit(solution)/shard_map/pallas_call | solution.py:28
  101.6 18.7 %all_to_all.21 = bf16[4,1008,128]{2,1,0:T(8,128)(2,1)S(1)} all-to-all(bf16[4,1008,128]{2,1,0:T(8,128)(2,1)S(1)} %shard_map.20), channel_id=1, replica_groups=mesh['z_lo'=4,'y'=4,'z_hi'=4,'x'=4,'core'=2] {'y'}, dimensions={0} | all-to-all | bytes 2064384 | tf_op jit(solution)/shard_map/all_to_all | solution.py:128
  120.3 0.1 convert_reduce_fusion.once
  120.5 18.9 %all-gather.4 = bf16[4032,128]{1,0:T(8,128)(2,1)S(1)} all-gather(bf16[1008,128]{1,0:T(8,128)(2,1)S(1)} %convert_element_type.86), channel_id=6, replica_groups=mesh['z_lo'=4,'y'=4,'z_hi'=4,'x'=4,'core'=2] {'z_lo'}, dimensions={0}, use_global_device_ids=true | all-gather | bytes 1290240 | tf_op jit(solution)/shard_map/all_gather | solution.py:176
  139.4 1.7 %shard_map.21 = bf16[4,1008,128]{2,1,0:T(8,128)(2,1)S(1)} custom-call(bf16[896,896]{1,0:T(8,128)(2,1)S(1)} %convert_element_type.91.left, bf16[4,1008,128]{2,1,0:T(8,128)(2,1)S(1)} %bitcast.12), custom_call_target="tpu_custom_call" | custom-call | flops 924844032 | bytes 2637824 | tf_op jit(solution)/shard_map/pallas_call | solution.py:28
  141.2 0.0 copy-start
  141.2 14.4 %all_to_all.22.parts = bf16[4,1008,128]{2,1,0:T(8,128)(2,1)S(1)} all-to-all(bf16[4,1008,128]{2,1,0:T(8,128)(2,1)S(1)} %shard_map.21), channel_id=1, replica_groups=mesh['z_lo'=4,'y'=4,'z_hi'=4,'x'=4,'core'=2] {'y'}, dimensions={0} | all-to-all | bytes 2064384 | tf_op jit(solution)/shard_map/all_to_all | solution.py:128
  155.6 0.0 copy-done
  155.6 1.2 shard_map.22
  (4 shorter events, 0.1 us)
Async XLA Ops:
  2.7 10.5 %copy-start.1 = (bf16[1008,128]{1,0:T(8,128)(2,1)S(1)}, bf16[1008,128]{1,0:T(8,128)(2,1)}, u32[]{:S(2)}) copy-start(bf16[1008,128]{1,0:T(8,128)(2,1)} %get-tuple-element.12) | copy-start | bytes 774148
  2.7 33.3 %all-to-all-start = ((bf16[8,112,576]{2,1,0:T(8,128)(2,1)}), bf16[8,112,576]{2,1,0:T(8,128)(2,1)S(1)}, u32[]{:S(2)}, u32[]{:S(2)}) async-start(bf16[8,112,576]{2,1,0:T(8,128)(2,1)} %bitcast.15), calls=%async_computation | async-start | bytes 2293760 | tf_op jit(solution)/shard_map/all_to_all | solution.py:128
  141.2 14.4 %copy-start = (bf16[224,576]{1,0:T(8,128)(2,1)S(1)}, bf16[224,576]{1,0:T(8,128)(2,1)}, u32[]{:S(2)}) copy-start(bf16[224,576]{1,0:T(8,128)(2,1)} %iterate.1) | copy-start | bytes 774148

commit v17 on v15

--- a/solution.py
+++ b/solution.py
@@ -82,13 +82,13 @@
     blocks, cores, rows, cols = left.shape
     tile = jnp.zeros((blocks * rows, out.shape[-1]), jnp.float32)
     for k in range(cores):
-        unpack(right.at[:, k], held.at[k])
+        unpack(right.at[k], held.at[k])
         tile += dot(left[:, k].reshape(blocks * rows, cols), held[k], 1)
     out[...] = tile.astype(out.dtype).reshape(out.shape)
 
 
 def own_kernel(core, right, out):
-    out[...] = right[:, pl.ds(core[0], 1)].reshape(out.shape)
+    out[...] = right[core[0]]
 
 
 def product_kernel(left, right, out, held):
@@ -116,8 +116,9 @@
     return jnp.sum(parts.astype(jnp.float32), axis=0)
 
 
-def gather(array, axes):
-    return lax.all_gather(array.astype(jnp.float16), axes, axis=0).astype(jnp.bfloat16)
+def gather(array, axis):
+    array = lax.all_gather(array.astype(jnp.float16), axis, axis=0)
+    return lax.all_gather(array, "core", axis=0).astype(jnp.bfloat16)
 
 
 def exchange(array, axes):
@@ -139,7 +140,7 @@
         scratch=[sems((4,))],
     )
     left = exchange(left.reshape(8, half, cols), ("y", "core")).reshape(4, 2, half, cols)
-    right = gather(right, ("z_lo", "core")).reshape(4, 2, packed, LANES)
+    right = gather(right, "z_lo")
 
     tile = call(
         gram_kernel,
@@ -155,7 +156,7 @@
     for groups in PAIRS:
         piece = piece.astype(jnp.float16)
         piece = total(lax.all_gather(piece, ("z_hi", "core"), axis=0, axis_index_groups=groups))
-    gram = gather(piece, ("x", "core")).reshape(4 * rows, 4 * rows)
+    gram = gather(piece, "x").transpose(1, 0, 2, 3).reshape(4 * rows, 4 * rows)
 
     def gram_times(array):
         parts = call(

time: 158 us -> 163 us (1.032)
  blocking collectives: 136 us -> 141 us
    all_gather x2 -> x4, blocking collectives: 38.7 us -> 45.7 us  [the longest x2 31.5 us: gather(): array = lax.all_gather(array.astype(jnp.float16), axis, axis=0)]
    all_to_all x3, blocking collectives: 47.7 us -> 45.5 us  [exchange(): return lax.all_to_all(array, axes, 0, 0, tiled=True)]
where the time goes in v17:
time: 163 us; the launch traced here: 161 us
  blocking collectives  141 us (87%)
  starting transfers between devices  10.4 us (6%)
  Pallas kernels  7.43 us (5%)
    all_to_all x3, blocking collectives, exchange(): return lax.all_to_all(array, axes, 0, 0, tiled=True)  45.5 us
    all_gather x2, blocking collectives, gather(): array = lax.all_gather(array.astype(jnp.float16), axis, axis=0)  31.5 us
    all_gather x2, blocking collectives, shards(): lax.all_gather(piece, ('z_hi', 'core'), axis=0, axis_index_groups=groups)  30.5 us
    all_gather x1, blocking collectives, shards(): lax.all_gather(once.astype(jnp.bfloat16), 'z_lo', axis=0)  19 us
    all_gather x2, blocking collectives, gather(): return lax.all_gather(array, 'core', axis=0).astype(jnp.bfloat16)  14.2 us
    all_to_all x1, starting transfers between devices, exchange(): return lax.all_to_all(array, axes, 0, 0, tiled=True)  10.4 us
    pallas_call x6, Pallas kernels, call(): pl.pallas_call(kernel, out_shape=output, in_specs=in_specs, out_specs=spe...  7.43 us
  transfers between devices with their start and end apart: 1, of which 0 were waited for; matrix products, arithmetic and copies ran while one was open for 0% of the time, Pallas kernels for 0%

profile of v17, /device:TPU:1, one launch (start us, length us, event | category | flops | bytes accessed | tf_op | source)
XLA Modules:
  0.0 160.9 jit_solution(3013350389019947404)
XLA Ops:
  0.0 0.0 copy-start
  0.0 1.0 copy-done
  1.0 1.0 shard_map.17
  2.0 10.4 %all-to-all-start = ((bf16[8,112,576]{2,1,0:T(8,128)(2,1)}), bf16[8,112,576]{2,1,0:T(8,128)(2,1)S(1)}, u32[]{:S(2)}, u32[]{:S(2)}) async-start(bf16[8,112,576]{2,1,0:T(8,128)(2,1)} %bitcast), calls=%async_computation | async-start | bytes 2293760 | tf_op jit(solution)/shard_map/all_to_all | solution.py:125
  12.4 0.1 convert_element_type.73
  12.4 20.3 %all-gather = f16[4032,128]{1,0:T(8,128)(2,1)S(1)} all-gather(f16[1008,128]{1,0:T(8,128)(2,1)S(1)} %convert_element_type.73), channel_id=2, replica_groups=mesh['z_lo'=4,'y'=4,'z_hi'=4,'x'=4,'core'=2] {'z_lo'}, dimensions={0}, use_global_device_ids=true | all-gather | bytes 1290240 | tf_op jit(solution)/shard_map/all_gather | solution.py:120
  32.7 4.4 %all-gather.9 = f16[8,1008,128]{2,1,0:T(8,128)(2,1)S(1)} all-gather(f16[4,1008,128]{2,1,0:T(8,128)(2,1)S(1)} %bitcast.22), channel_id=3, replica_groups=mesh['z_lo'=4,'y'=4,'z_hi'=4,'x'=4,'core'=2] {'core'}, dimensions={0}, use_global_device_ids=true | all-gather | bytes 3096576 | tf_op jit(solution)/shard_map/all_gather | solution.py:121
  37.1 0.4 convert_element_type.88
  37.5 0.0 all-to-all-done
  37.5 1.7 %shard_map.18 = bf16[4,112,896]{2,1,0:T(8,128)(2,1)S(1)} custom-call(bf16[4,2,112,576]{3,2,1,0:T(8,128)(2,1)S(1)} %bitcast.19, bf16[2,4,1008,128]{3,2,1,0:T(8,128)(2,1)S(1)} %bitcast.15), custom_call_target="tpu_custom_call" | custom-call | flops 924844032 | bytes 3096576 | tf_op jit(solution)/shard_map/pallas_call | solution.py:28
  39.2 0.1 shard_map.19.right
  39.3 14.6 %all_to_all.20 = bf16[4,112,896]{2,1,0:T(8,128)(2,1)S(1)} all-to-all(bf16[4,112,896]{2,1,0:T(8,128)(2,1)S(1)} %shard_map.18), channel_id=1, replica_groups=mesh['z_lo'=4,'y'=4,'z_hi'=4,'x'=4,'core'=2] {'x'}, dimensions={0} | all-to-all | bytes 1605632 | tf_op jit(solution)/shard_map/all_to_all | solution.py:125
  53.9 0.1 convert_reduce_fusion.1
  54.0 16.7 %all-gather.2 = f16[224,896]{1,0:T(8,128)(2,1)S(1)} all-gather(f16[112,896]{1,0:T(8,128)(2,1)S(1)} %convert_element_type.76), channel_id=4, replica_groups={{0,8},{16,24},{9,17},{25,1},{2,10},{18,26},{11,19},{27,3},{4,12},{20,28..., dimensions={0}, use_global_device_ids=true | all-gather | bytes 602112 | tf_op jit(solution)/shard_map/all_gather | solution.py:158
  70.7 0.1 convert_reduce_fusion.3
  70.8 13.7 %all-gather.3 = f16[224,896]{1,0:T(8,128)(2,1)S(1)} all-gather(f16[112,896]{1,0:T(8,128)(2,1)S(1)} %convert_element_type.79), channel_id=5, replica_groups={{8,16},{24,0},{1,9},{17,25},{10,18},{26,2},{3,11},{19,27},{12,20},{28,4..., dimensions={0}, use_global_device_ids=true | all-gather | bytes 602112 | tf_op jit(solution)/shard_map/all_gather | solution.py:158
  84.6 0.1 convert_reduce_fusion.2
  84.7 11.1 %all-gather.4 = f16[448,896]{1,0:T(8,128)(2,1)S(1)} all-gather(f16[112,896]{1,0:T(8,128)(2,1)S(1)} %convert_element_type.82), channel_id=6, replica_groups=mesh['z_lo'=4,'y'=4,'z_hi'=4,'x'=4,'core'=2] {'x'}, dimensions={0}, use_global_device_ids=true | all-gather | bytes 1003520 | tf_op jit(solution)/shard_map/all_gather | solution.py:120
  95.8 9.8 %all-gather.10 = f16[8,112,896]{2,1,0:T(8,128)(2,1)S(1)} all-gather(f16[4,112,896]{2,1,0:T(8,128)(2,1)S(1)} %bitcast.23), channel_id=7, replica_groups=mesh['z_lo'=4,'y'=4,'z_hi'=4,'x'=4,'core'=2] {'core'}, dimensions={0}, use_global_device_ids=true | all-gather | bytes 2408448 | tf_op jit(solution)/shard_map/all_gather | solution.py:121
  105.6 0.3 convert_element_type.91
  105.9 0.1 copy.4
  106.0 1.7 %shard_map.20 = bf16[4,1008,128]{2,1,0:T(8,128)(2,1)S(1)} custom-call(bf16[896,896]{1,0:T(8,128)(2,1)S(1)} %bitcast.17, bf16[4,1008,128]{2,1,0:T(8,128)(2,1)S(1)} %shard_map.19.right), custom_call_target="tpu_custom_call" | custom-call | flops 924844032 | bytes 2637824 | tf_op jit(solution)/shard_map/pallas_call | solution.py:28
  107.8 17.1 %all_to_all.21 = bf16[4,1008,128]{2,1,0:T(8,128)(2,1)S(1)} all-to-all(bf16[4,1008,128]{2,1,0:T(8,128)(2,1)S(1)} %shard_map.20), channel_id=1, replica_groups=mesh['z_lo'=4,'y'=4,'z_hi'=4,'x'=4,'core'=2] {'y'}, dimensions={0} | all-to-all | bytes 2064384 | tf_op jit(solution)/shard_map/all_to_all | solution.py:125
  124.9 0.1 convert_reduce_fusion.once
  125.1 19.0 %all-gather.6 = bf16[4032,128]{1,0:T(8,128)(2,1)S(1)} all-gather(bf16[1008,128]{1,0:T(8,128)(2,1)S(1)} %convert_element_type.86), channel_id=8, replica_groups=mesh['z_lo'=4,'y'=4,'z_hi'=4,'x'=4,'core'=2] {'z_lo'}, dimensions={0}, use_global_device_ids=true | all-gather | bytes 1290240 | tf_op jit(solution)/shard_map/all_gather | solution.py:172
  144.1 1.7 %shard_map.21 = bf16[4,1008,128]{2,1,0:T(8,128)(2,1)S(1)} custom-call(bf16[896,896]{1,0:T(8,128)(2,1)S(1)} %bitcast.18, bf16[4,1008,128]{2,1,0:T(8,128)(2,1)S(1)} %bitcast.20), custom_call_target="tpu_custom_call" | custom-call | flops 924844032 | bytes 2637824 | tf_op jit(solution)/shard_map/pallas_call | solution.py:28
  145.8 0.0 copy-start.1
  145.9 13.8 %all_to_all.22.parts = bf16[4,1008,128]{2,1,0:T(8,128)(2,1)S(1)} all-to-all(bf16[4,1008,128]{2,1,0:T(8,128)(2,1)S(1)} %shard_map.21), channel_id=1, replica_groups=mesh['z_lo'=4,'y'=4,'z_hi'=4,'x'=4,'core'=2] {'y'}, dimensions={0} | all-to-all | bytes 2064384 | tf_op jit(solution)/shard_map/all_to_all | solution.py:125
  159.7 0.0 copy-done.1
  159.7 1.2 shard_map.22
  (4 shorter events, 0.1 us)
Async XLA Ops:
  0.0 1.0 copy-start
  2.0 35.5 %all-to-all-start = ((bf16[8,112,576]{2,1,0:T(8,128)(2,1)}), bf16[8,112,576]{2,1,0:T(8,128)(2,1)S(1)}, u32[]{:S(2)}, u32[]{:S(2)}) async-start(bf16[8,112,576]{2,1,0:T(8,128)(2,1)} %bitcast), calls=%async_computation | async-start | bytes 2293760 | tf_op jit(solution)/shard_map/all_to_all | solution.py:125
  145.8 13.9 %copy-start.1 = (bf16[224,576]{1,0:T(8,128)(2,1)S(1)}, bf16[224,576]{1,0:T(8,128)(2,1)}, u32[]{:S(2)}) copy-start(bf16[224,576]{1,0:T(8,128)(2,1)} %iterate.1) | copy-start | bytes 774148

commit v18 on v15

--- a/solution.py
+++ b/solution.py
@@ -16,7 +16,7 @@
 coef_quintic = 2.0315
 
 LANES = 128
-PAIRS = [[0, 2], [4, 6], [3, 5], [7, 1]], [[2, 4], [6, 0], [1, 3], [5, 7]]
+PAIRS = [[2, 4], [6, 0], [1, 3], [5, 7]], [[0, 2], [4, 6], [3, 5], [7, 1]]
 VMEM = pl.BlockSpec(memory_space=pltpu.VMEM)
 SMEM = pl.BlockSpec(memory_space=pltpu.SMEM)
 HBM = pl.BlockSpec(memory_space=pltpu.HBM)

time: 158 us -> 158 us (level)
  the two profiles are of different devices: /device:TPU:1 before, /device:TPU:32 now
where the time goes in v18:
time: 158 us
  blocking collectives  144 us (91%)
  Pallas kernels  7.42 us (5%)
  starting transfers between devices  4.48 us (3%)
    all_to_all x3, blocking collectives, exchange(): return lax.all_to_all(array, axes, 0, 0, tiled=True)  52 us
    all_gather x2, blocking collectives, gather(): lax.all_gather(array.astype(jnp.float16), axes, axis=0).astype(jnp.bfloat16)  39.1 us
    all_gather x1, blocking collectives, shards(): lax.all_gather(once.astype(jnp.bfloat16), 'z_lo', axis=0)  27.1 us
    all_gather x2, blocking collectives, shards(): lax.all_gather(piece, ('z_hi', 'core'), axis=0, axis_index_groups=groups)  25.4 us
    pallas_call x6, Pallas kernels, call(): pl.pallas_call(kernel, out_shape=output, in_specs=in_specs, out_specs=spe...  7.42 us
    all_to_all x1, starting transfers between devices, exchange(): return lax.all_to_all(array, axes, 0, 0, tiled=True)  4.48 us
  transfers between devices with their start and end apart: 1, of which 0 were waited for; matrix products, arithmetic and copies ran while one was open for 0% of the time, Pallas kernels for 0%

profile of v18, /device:TPU:32, one launch (start us, length us, event | category | flops | bytes accessed | tf_op | source)
XLA Modules:
  0.0 157.6 jit_solution(13096139748299923312)
XLA Ops:
  0.0 0.0 copy-start
  0.0 1.0 copy-done
  1.0 1.0 shard_map.17
  2.0 4.5 %all-to-all-start = ((bf16[8,112,576]{2,1,0:T(8,128)(2,1)}), bf16[8,112,576]{2,1,0:T(8,128)(2,1)S(1)}, u32[]{:S(2)}, u32[]{:S(2)}) async-start(bf16[8,112,576]{2,1,0:T(8,128)(2,1)} %bitcast), calls=%async_computation | async-start | bytes 2293760 | tf_op jit(solution)/shard_map/all_to_all | solution.py:124
  6.5 0.1 convert_element_type.73
  6.5 23.8 %all-gather.7 = f16[8064,128]{1,0:T(8,128)(2,1)S(1)} all-gather(f16[1008,128]{1,0:T(8,128)(2,1)S(1)} %convert_element_type.73), channel_id=2, replica_groups=mesh['z_lo'=4,'y'=4,'z_hi'=4,'x'=4,'core'=2] {'z_lo','core'}, dimensions={0}, use_global_device_ids=true | all-gather | bytes 2322432 | tf_op jit(solution)/shard_map/all_gather | solution.py:120
  30.3 0.2 convert_element_type.88
  30.5 0.0 all-to-all-done
  30.5 1.7 %shard_map.18 = bf16[4,112,896]{2,1,0:T(8,128)(2,1)S(1)} custom-call(bf16[4,2,112,576]{3,2,1,0:T(8,128)(2,1)S(1)} %bitcast.11, bf16[4,2,1008,128]{3,2,1,0:T(8,128)(2,1)S(1)} %bitcast.9), custom_call_target="tpu_custom_call" | custom-call | flops 924844032 | bytes 3096576 | tf_op jit(solution)/shard_map/pallas_call | solution.py:28
  32.2 0.1 shard_map.19.right
  32.3 16.9 %all_to_all.20 = bf16[4,112,896]{2,1,0:T(8,128)(2,1)S(1)} all-to-all(bf16[4,112,896]{2,1,0:T(8,128)(2,1)S(1)} %shard_map.18), channel_id=1, replica_groups=mesh['z_lo'=4,'y'=4,'z_hi'=4,'x'=4,'core'=2] {'x'}, dimensions={0} | all-to-all | bytes 1605632 | tf_op jit(solution)/shard_map/all_to_all | solution.py:124
  49.2 0.1 convert_reduce_fusion.1
  49.4 15.0 %all-gather.1 = f16[224,896]{1,0:T(8,128)(2,1)S(1)} all-gather(f16[112,896]{1,0:T(8,128)(2,1)S(1)} %convert_element_type.76), channel_id=3, replica_groups={{8,16},{24,0},{1,9},{17,25},{10,18},{26,2},{3,11},{19,27},{12,20},{28,4..., dimensions={0}, use_global_device_ids=true | all-gather | bytes 602112 | tf_op jit(solution)/shard_map/all_gather | solution.py:157
  64.4 0.1 convert_reduce_fusion.3
  64.5 10.4 %all-gather.2 = f16[224,896]{1,0:T(8,128)(2,1)S(1)} all-gather(f16[112,896]{1,0:T(8,128)(2,1)S(1)} %convert_element_type.79), channel_id=4, replica_groups={{0,8},{16,24},{9,17},{25,1},{2,10},{18,26},{11,19},{27,3},{4,12},{20,28..., dimensions={0}, use_global_device_ids=true | all-gather | bytes 602112 | tf_op jit(solution)/shard_map/all_gather | solution.py:157
  74.9 0.1 convert_reduce_fusion.2
  75.0 15.3 %all-gather.8 = f16[896,896]{1,0:T(8,128)(2,1)S(1)} all-gather(f16[112,896]{1,0:T(8,128)(2,1)S(1)} %convert_element_type.82), channel_id=5, replica_groups=mesh['z_lo'=4,'y'=4,'z_hi'=4,'x'=4,'core'=2] {'x','core'}, dimensions={0}, use_global_device_ids=true | all-gather | bytes 1806336 | tf_op jit(solution)/shard_map/all_gather | solution.py:120
  90.3 0.3 convert_element_type.91.left
  90.5 1.7 %shard_map.20 = bf16[4,1008,128]{2,1,0:T(8,128)(2,1)S(1)} custom-call(bf16[896,896]{1,0:T(8,128)(2,1)S(1)} %convert_element_type.91.left, bf16[4,1008,128]{2,1,0:T(8,128)(2,1)S(1)} %shard_map.19.right), custom_call_target="tpu_custom_call" | custom-call | flops 924844032 | bytes 2637824 | tf_op jit(solution)/shard_map/pallas_call | solution.py:28
  92.3 19.2 %all_to_all.21 = bf16[4,1008,128]{2,1,0:T(8,128)(2,1)S(1)} all-to-all(bf16[4,1008,128]{2,1,0:T(8,128)(2,1)S(1)} %shard_map.20), channel_id=1, replica_groups=mesh['z_lo'=4,'y'=4,'z_hi'=4,'x'=4,'core'=2] {'y'}, dimensions={0} | all-to-all | bytes 2064384 | tf_op jit(solution)/shard_map/all_to_all | solution.py:124
  111.5 0.1 convert_reduce_fusion.once
  111.7 27.1 %all-gather.4 = bf16[4032,128]{1,0:T(8,128)(2,1)S(1)} all-gather(bf16[1008,128]{1,0:T(8,128)(2,1)S(1)} %convert_element_type.86), channel_id=6, replica_groups=mesh['z_lo'=4,'y'=4,'z_hi'=4,'x'=4,'core'=2] {'z_lo'}, dimensions={0}, use_global_device_ids=true | all-gather | bytes 1290240 | tf_op jit(solution)/shard_map/all_gather | solution.py:171
  138.8 1.7 %shard_map.21 = bf16[4,1008,128]{2,1,0:T(8,128)(2,1)S(1)} custom-call(bf16[896,896]{1,0:T(8,128)(2,1)S(1)} %convert_element_type.91.left, bf16[4,1008,128]{2,1,0:T(8,128)(2,1)S(1)} %bitcast.12), custom_call_target="tpu_custom_call" | custom-call | flops 924844032 | bytes 2637824 | tf_op jit(solution)/shard_map/pallas_call | solution.py:28
  140.5 0.0 copy-start.1
  140.5 15.9 %all_to_all.22.parts = bf16[4,1008,128]{2,1,0:T(8,128)(2,1)S(1)} all-to-all(bf16[4,1008,128]{2,1,0:T(8,128)(2,1)S(1)} %shard_map.21), channel_id=1, replica_groups=mesh['z_lo'=4,'y'=4,'z_hi'=4,'x'=4,'core'=2] {'y'}, dimensions={0} | all-to-all | bytes 2064384 | tf_op jit(solution)/shard_map/all_to_all | solution.py:124
  156.4 0.0 copy-done.1
  156.4 1.2 shard_map.22
  (4 shorter events, 0.1 us)
Async XLA Ops:
  0.0 1.0 copy-start
  2.0 28.5 %all-to-all-start = ((bf16[8,112,576]{2,1,0:T(8,128)(2,1)}), bf16[8,112,576]{2,1,0:T(8,128)(2,1)S(1)}, u32[]{:S(2)}, u32[]{:S(2)}) async-start(bf16[8,112,576]{2,1,0:T(8,128)(2,1)} %bitcast), calls=%async_computation | async-start | bytes 2293760 | tf_op jit(solution)/shard_map/all_to_all | solution.py:124
  140.5 15.9 %copy-start.1 = (bf16[224,576]{1,0:T(8,128)(2,1)S(1)}, bf16[224,576]{1,0:T(8,128)(2,1)}, u32[]{:S(2)}) copy-start(bf16[224,576]{1,0:T(8,128)(2,1)} %iterate.1) | copy-start | bytes 774148

commit v19 on v15

--- a/solution.py
+++ b/solution.py
@@ -19,7 +19,6 @@
 PAIRS = [[0, 2], [4, 6], [3, 5], [7, 1]], [[2, 4], [6, 0], [1, 3], [5, 7]]
 VMEM = pl.BlockSpec(memory_space=pltpu.VMEM)
 SMEM = pl.BlockSpec(memory_space=pltpu.SMEM)
-HBM = pl.BlockSpec(memory_space=pltpu.HBM)
 ANY = pl.BlockSpec(memory_space=pl.ANY)
 
 
@@ -68,14 +67,9 @@
             out[row, col] = packed[i, packed_row, packed_col]
 
 
-def first_kernel(array, out, packed, sems):
-    copies = [pltpu.make_async_copy(array, out.at[i], sems.at[i]) for i in range(out.shape[0])]
-    for copy in copies:
-        copy.start()
+def pack_kernel(array, packed):
     for row, col, packed_row, packed_col in pieces(*array.shape):
         packed[packed_row, packed_col] = array[row, col]
-    for copy in copies:
-        copy.wait()
 
 
 def gram_kernel(left, right, out, held):
@@ -131,14 +125,9 @@
     sems = pltpu.SemaphoreType.DMA
 
     packed = rows * cols // LANES
-    left, right = call(
-        first_kernel,
-        [(iterate, VMEM)],
-        (bf16(4, rows, cols), bf16(packed, LANES)),
-        spec=(HBM, VMEM),
-        scratch=[sems((4,))],
-    )
+    left = jnp.broadcast_to(iterate, (4, rows, cols))
     left = exchange(left.reshape(8, half, cols), ("y", "core")).reshape(4, 2, half, cols)
+    right = call(pack_kernel, [(iterate, VMEM)], bf16(packed, LANES))
     right = gather(right, ("z_lo", "core")).reshape(4, 2, packed, LANES)
 
     tile = call(

time: 158 us -> 158 us (level)
    broadcast_in_dim x0 -> x1, local copies, waits for them, and re-layouts: none -> 2.12 us  [shards(): left = jnp.broadcast_to(iterate, (4, rows, cols))]
where the time goes in v19:
time: 158 us; the launch traced here: 156 us
  blocking collectives  136 us (86%)
  starting transfers between devices  10.3 us (7%)
  Pallas kernels  6.49 us (4%)
  local copies, waits for them, and re-layouts  2.13 us (1%)
    all_to_all x3, blocking collectives, exchange(): return lax.all_to_all(array, axes, 0, 0, tiled=True)  47.6 us
    all_gather x2, blocking collectives, gather(): lax.all_gather(array.astype(jnp.float16), axes, axis=0).astype(jnp.bfloat16)  38.7 us
    all_gather x2, blocking collectives, shards(): lax.all_gather(piece, ('z_hi', 'core'), axis=0, axis_index_groups=groups)  30.7 us
    all_gather x1, blocking collectives, shards(): lax.all_gather(once.astype(jnp.bfloat16), 'z_lo', axis=0)  19 us
    all_to_all x1, starting transfers between devices, exchange(): return lax.all_to_all(array, axes, 0, 0, tiled=True)  10.3 us
    pallas_call x6, Pallas kernels, call(): pl.pallas_call(kernel, out_shape=output, in_specs=in_specs, out_specs=spe...  6.49 us
  transfers between devices with their start and end apart: 1, of which 0 were waited for; matrix products, arithmetic and copies ran while one was open for 0% of the time, Pallas kernels for 0%

profile of v19, /device:TPU:1, one launch (start us, length us, event | category | flops | bytes accessed | tf_op | source)
XLA Modules:
  0.0 156.0 jit_solution(7367183291260675428)
XLA Ops:
  0.0 0.0 copy-start
  0.0 2.1 %broadcast_in_dim.3 = bf16[4,224,576]{2,1,0:T(8,128)(2,1)} broadcast(bf16[224,576]{1,0:T(8,128)(2,1)} %iterate.1), dimensions={1,2} | broadcast | bytes 1290240 | tf_op jit(solution)/shard_map/broadcast_in_dim | solution.py:128
  2.1 10.3 %all-to-all-start = ((bf16[8,112,576]{2,1,0:T(8,128)(2,1)}), bf16[8,112,576]{2,1,0:T(8,128)(2,1)S(1)}, u32[]{:S(2)}, u32[]{:S(2)}) async-start(bf16[8,112,576]{2,1,0:T(8,128)(2,1)} %bitcast), calls=%async_computation | async-start | bytes 2293760 | tf_op jit(solution)/shard_map/all_to_all | solution.py:118
  12.5 0.0 copy-done
  12.5 0.1 shard_map.17
  12.6 0.1 convert_element_type.73
  12.6 22.6 %all-gather.7 = f16[8064,128]{1,0:T(8,128)(2,1)S(1)} all-gather(f16[1008,128]{1,0:T(8,128)(2,1)S(1)} %convert_element_type.73), channel_id=2, replica_groups=mesh['z_lo'=4,'y'=4,'z_hi'=4,'x'=4,'core'=2] {'z_lo','core'}, dimensions={0}, use_global_device_ids=true | all-gather | bytes 2322432 | tf_op jit(solution)/shard_map/all_gather | solution.py:114
  35.2 0.2 convert_element_type.88
  35.5 0.0 all-to-all-done
  35.5 1.7 %shard_map.18 = bf16[4,112,896]{2,1,0:T(8,128)(2,1)S(1)} custom-call(bf16[4,2,112,576]{3,2,1,0:T(8,128)(2,1)S(1)} %bitcast.11, bf16[4,2,1008,128]{3,2,1,0:T(8,128)(2,1)S(1)} %bitcast.9), custom_call_target="tpu_custom_call" | custom-call | flops 924844032 | bytes 3096576 | tf_op jit(solution)/shard_map/pallas_call | solution.py:27
  37.1 0.1 shard_map.19.right
  37.2 14.5 %all_to_all.20 = bf16[4,112,896]{2,1,0:T(8,128)(2,1)S(1)} all-to-all(bf16[4,112,896]{2,1,0:T(8,128)(2,1)S(1)} %shard_map.18), channel_id=1, replica_groups=mesh['z_lo'=4,'y'=4,'z_hi'=4,'x'=4,'core'=2] {'x'}, dimensions={0} | all-to-all | bytes 1605632 | tf_op jit(solution)/shard_map/all_to_all | solution.py:118
  51.8 0.1 convert_reduce_fusion.1
  51.9 16.6 %all-gather.1 = f16[224,896]{1,0:T(8,128)(2,1)S(1)} all-gather(f16[112,896]{1,0:T(8,128)(2,1)S(1)} %convert_element_type.76), channel_id=3, replica_groups={{0,8},{16,24},{9,17},{25,1},{2,10},{18,26},{11,19},{27,3},{4,12},{20,28..., dimensions={0}, use_global_device_ids=true | all-gather | bytes 602112 | tf_op jit(solution)/shard_map/all_gather | solution.py:146
  68.5 0.1 convert_reduce_fusion.3
  68.6 14.2 %all-gather.2 = f16[224,896]{1,0:T(8,128)(2,1)S(1)} all-gather(f16[112,896]{1,0:T(8,128)(2,1)S(1)} %convert_element_type.79), channel_id=4, replica_groups={{8,16},{24,0},{1,9},{17,25},{10,18},{26,2},{3,11},{19,27},{12,20},{28,4..., dimensions={0}, use_global_device_ids=true | all-gather | bytes 602112 | tf_op jit(solution)/shard_map/all_gather | solution.py:146
  82.7 0.1 convert_reduce_fusion.2
  82.8 16.1 %all-gather.8 = f16[896,896]{1,0:T(8,128)(2,1)S(1)} all-gather(f16[112,896]{1,0:T(8,128)(2,1)S(1)} %convert_element_type.82), channel_id=5, replica_groups=mesh['z_lo'=4,'y'=4,'z_hi'=4,'x'=4,'core'=2] {'x','core'}, dimensions={0}, use_global_device_ids=true | all-gather | bytes 1806336 | tf_op jit(solution)/shard_map/all_gather | solution.py:114
  98.9 0.3 convert_element_type.91.left
  99.2 1.7 %shard_map.20 = bf16[4,1008,128]{2,1,0:T(8,128)(2,1)S(1)} custom-call(bf16[896,896]{1,0:T(8,128)(2,1)S(1)} %convert_element_type.91.left, bf16[4,1008,128]{2,1,0:T(8,128)(2,1)S(1)} %shard_map.19.right), custom_call_target="tpu_custom_call" | custom-call | flops 924844032 | bytes 2637824 | tf_op jit(solution)/shard_map/pallas_call | solution.py:27
  101.0 18.7 %all_to_all.21 = bf16[4,1008,128]{2,1,0:T(8,128)(2,1)S(1)} all-to-all(bf16[4,1008,128]{2,1,0:T(8,128)(2,1)S(1)} %shard_map.20), channel_id=1, replica_groups=mesh['z_lo'=4,'y'=4,'z_hi'=4,'x'=4,'core'=2] {'y'}, dimensions={0} | all-to-all | bytes 2064384 | tf_op jit(solution)/shard_map/all_to_all | solution.py:118
  119.7 0.1 convert_reduce_fusion.once
  119.9 19.0 %all-gather.4 = bf16[4032,128]{1,0:T(8,128)(2,1)S(1)} all-gather(bf16[1008,128]{1,0:T(8,128)(2,1)S(1)} %convert_element_type.86), channel_id=6, replica_groups=mesh['z_lo'=4,'y'=4,'z_hi'=4,'x'=4,'core'=2] {'z_lo'}, dimensions={0}, use_global_device_ids=true | all-gather | bytes 1290240 | tf_op jit(solution)/shard_map/all_gather | solution.py:160
  138.8 1.7 %shard_map.21 = bf16[4,1008,128]{2,1,0:T(8,128)(2,1)S(1)} custom-call(bf16[896,896]{1,0:T(8,128)(2,1)S(1)} %convert_element_type.91.left, bf16[4,1008,128]{2,1,0:T(8,128)(2,1)S(1)} %bitcast.12), custom_call_target="tpu_custom_call" | custom-call | flops 924844032 | bytes 2637824 | tf_op jit(solution)/shard_map/pallas_call | solution.py:27
  140.6 14.3 %all_to_all.22.parts = bf16[4,1008,128]{2,1,0:T(8,128)(2,1)S(1)} all-to-all(bf16[4,1008,128]{2,1,0:T(8,128)(2,1)S(1)} %shard_map.21), channel_id=1, replica_groups=mesh['z_lo'=4,'y'=4,'z_hi'=4,'x'=4,'core'=2] {'y'}, dimensions={0} | all-to-all | bytes 2064384 | tf_op jit(solution)/shard_map/all_to_all | solution.py:118
  154.9 1.2 shard_map.22
  (4 shorter events, 0.1 us)
Async XLA Ops:
  0.0 12.5 %copy-start = (bf16[224,576]{1,0:T(8,128)(2,1)S(1)}, bf16[224,576]{1,0:T(8,128)(2,1)}, u32[]{:S(2)}) copy-start(bf16[224,576]{1,0:T(8,128)(2,1)} %iterate.1) | copy-start | bytes 774148
  2.1 33.3 %all-to-all-start = ((bf16[8,112,576]{2,1,0:T(8,128)(2,1)}), bf16[8,112,576]{2,1,0:T(8,128)(2,1)S(1)}, u32[]{:S(2)}, u32[]{:S(2)}) async-start(bf16[8,112,576]{2,1,0:T(8,128)(2,1)} %bitcast), calls=%async_computation | async-start | bytes 2293760 | tf_op jit(solution)/shard_map/all_to_all | solution.py:118

commit v20 on v19

--- a/solution.py
+++ b/solution.py
@@ -20,9 +20,10 @@
 VMEM = pl.BlockSpec(memory_space=pltpu.VMEM)
 SMEM = pl.BlockSpec(memory_space=pltpu.SMEM)
 ANY = pl.BlockSpec(memory_space=pl.ANY)
-
-
-def call(kernel, operands, output, spec=VMEM, scratch=(), flops=0):
+HBM = pl.BlockSpec(memory_space=pltpu.HBM)
+
+
+def call(kernel, operands, output, spec=VMEM, scratch=(), flops=0, vmem=16):
     arrays, in_specs = zip(*operands)
     return pl.pallas_call(
         kernel,
@@ -30,7 +31,7 @@
         in_specs=in_specs,
         out_specs=spec,
         scratch_shapes=scratch,
-        compiler_params=pltpu.CompilerParams(vmem_limit_bytes=16 * 1024 * 1024),
+        compiler_params=pltpu.CompilerParams(vmem_limit_bytes=vmem * 1024 * 1024),
         cost_estimate=pl.CostEstimate(
             flops=flops,
             bytes_accessed=2 * sum(math.prod(array.shape) for array in arrays),
@@ -65,6 +66,27 @@
         for row, col, packed_row, packed_col in pieces(rows, out.shape[1]):
             row = slice(i * rows + row.start, i * rows + row.stop)
             out[row, col] = packed[i, packed_row, packed_col]
+
+
+def copies_kernel(array, out, held, sems):
+    rows, count = array.shape[0] // 2, out.shape[0]
+    halves = [pl.ds(half * rows, rows) for half in range(2)]
+    fetches = [
+        pltpu.make_async_copy(array.at[half], held.at[half], sems.at[count, k])
+        for k, half in enumerate(halves)
+    ]
+    copies = [
+        [pltpu.make_async_copy(held.at[half], out.at[i, half], sems.at[i, k]) for i in range(count)]
+        for k, half in enumerate(halves)
+    ]
+    for fetch in fetches:
+        fetch.start()
+    for fetch, sends in zip(fetches, copies):
+        fetch.wait()
+        for copy in sends:
+            copy.start()
+    for copy in copies[0] + copies[1]:
+        copy.wait()
 
 
 def pack_kernel(array, packed):
@@ -125,7 +147,14 @@
     sems = pltpu.SemaphoreType.DMA
 
     packed = rows * cols // LANES
-    left = jnp.broadcast_to(iterate, (4, rows, cols))
+    left = call(
+        copies_kernel,
+        [(iterate, ANY)],
+        bf16(4, rows, cols),
+        spec=HBM,
+        scratch=[pltpu.VMEM(iterate.shape, iterate.dtype), sems((5, 2))],
+        vmem=56,
+    )
     left = exchange(left.reshape(8, half, cols), ("y", "core")).reshape(4, 2, half, cols)
     right = call(pack_kernel, [(iterate, VMEM)], bf16(packed, LANES))
     right = gather(right, ("z_lo", "core")).reshape(4, 2, packed, LANES)

time: 158 us -> 158 us (level)
  local copies, waits for them, and re-layouts: 2.13 us -> 0.01 us
  Pallas kernels: 6.49 us -> 8.55 us
    broadcast_in_dim x1 -> x0, local copies, waits for them, and re-layouts: 2.12 us -> none  [shards(): left = jnp.broadcast_to(iterate, (4, rows, cols))]
    pallas_call x6 -> x7, Pallas kernels: 6.49 us -> 8.55 us  [call(): pl.pallas_call(kernel, out_shape=output, in_specs=in_specs, out_specs=spe...]
where the time goes in v20:
time: 158 us; the launch traced here: 156 us
  blocking collectives  136 us (86%)
  starting transfers between devices  10.4 us (7%)
  Pallas kernels  8.55 us (5%)
    all_to_all x3, blocking collectives, exchange(): return lax.all_to_all(array, axes, 0, 0, tiled=True)  47.6 us
    all_gather x2, blocking collectives, gather(): lax.all_gather(array.astype(jnp.float16), axes, axis=0).astype(jnp.bfloat16)  38.7 us
    all_gather x2, blocking collectives, shards(): lax.all_gather(piece, ('z_hi', 'core'), axis=0, axis_index_groups=groups)  30.7 us
    all_gather x1, blocking collectives, shards(): lax.all_gather(once.astype(jnp.bfloat16), 'z_lo', axis=0)  18.9 us
    all_to_all x1, starting transfers between devices, exchange(): return lax.all_to_all(array, axes, 0, 0, tiled=True)  10.4 us
    pallas_call x7, Pallas kernels, call(): pl.pallas_call(kernel, out_shape=output, in_specs=in_specs, out_specs=spe...  8.55 us
  transfers between devices with their start and end apart: 1, of which 0 were waited for; matrix products, arithmetic and copies ran while one was open for 0% of the time, Pallas kernels for 0%

profile of v20, /device:TPU:1, one launch (start us, length us, event | category | flops | bytes accessed | tf_op | source)
XLA Modules:
  0.0 156.0 jit_solution(14654875858824721793)
XLA Ops:
  0.0 0.0 copy-start
  0.0 2.1 %shard_map.17 = bf16[4,224,576]{2,1,0:T(8,128)(2,1)} custom-call(bf16[224,576]{1,0:T(8,128)(2,1)} %iterate.1), custom_call_target="tpu_custom_call" | custom-call | bytes 258048 | tf_op jit(solution)/shard_map/pallas_call | solution.py:28
  2.1 10.4 %all-to-all-start = ((bf16[8,112,576]{2,1,0:T(8,128)(2,1)}), bf16[8,112,576]{2,1,0:T(8,128)(2,1)S(1)}, u32[]{:S(2)}, u32[]{:S(2)}) async-start(bf16[8,112,576]{2,1,0:T(8,128)(2,1)} %bitcast.13), calls=%async_computation | async-start | bytes 2293760 | tf_op jit(solution)/shard_map/all_to_all | solution.py:140
  12.4 0.0 copy-done
  12.4 0.1 shard_map.18
  12.6 0.1 convert_element_type.73
  12.6 22.6 %all-gather.7 = f16[8064,128]{1,0:T(8,128)(2,1)S(1)} all-gather(f16[1008,128]{1,0:T(8,128)(2,1)S(1)} %convert_element_type.73), channel_id=2, replica_groups=mesh['z_lo'=4,'y'=4,'z_hi'=4,'x'=4,'core'=2] {'z_lo','core'}, dimensions={0}, use_global_device_ids=true | all-gather | bytes 2322432 | tf_op jit(solution)/shard_map/all_gather | solution.py:136
  35.2 0.2 convert_element_type.88
  35.4 0.0 all-to-all-done
  35.4 1.7 %shard_map.19 = bf16[4,112,896]{2,1,0:T(8,128)(2,1)S(1)} custom-call(bf16[4,2,112,576]{3,2,1,0:T(8,128)(2,1)S(1)} %bitcast.11, bf16[4,2,1008,128]{3,2,1,0:T(8,128)(2,1)S(1)} %bitcast.9), custom_call_target="tpu_custom_call" | custom-call | flops 924844032 | bytes 3096576 | tf_op jit(solution)/shard_map/pallas_call | solution.py:28
  37.1 0.1 shard_map.20.right
  37.2 14.5 %all_to_all.20 = bf16[4,112,896]{2,1,0:T(8,128)(2,1)S(1)} all-to-all(bf16[4,112,896]{2,1,0:T(8,128)(2,1)S(1)} %shard_map.19), channel_id=1, replica_groups=mesh['z_lo'=4,'y'=4,'z_hi'=4,'x'=4,'core'=2] {'x'}, dimensions={0} | all-to-all | bytes 1605632 | tf_op jit(solution)/shard_map/all_to_all | solution.py:140
  51.8 0.1 convert_reduce_fusion.1
  51.9 16.6 %all-gather.1 = f16[224,896]{1,0:T(8,128)(2,1)S(1)} all-gather(f16[112,896]{1,0:T(8,128)(2,1)S(1)} %convert_element_type.76), channel_id=3, replica_groups={{0,8},{16,24},{9,17},{25,1},{2,10},{18,26},{11,19},{27,3},{4,12},{20,28..., dimensions={0}, use_global_device_ids=true | all-gather | bytes 602112 | tf_op jit(solution)/shard_map/all_gather | solution.py:175
  68.5 0.1 convert_reduce_fusion.3
  68.6 14.2 %all-gather.2 = f16[224,896]{1,0:T(8,128)(2,1)S(1)} all-gather(f16[112,896]{1,0:T(8,128)(2,1)S(1)} %convert_element_type.79), channel_id=4, replica_groups={{8,16},{24,0},{1,9},{17,25},{10,18},{26,2},{3,11},{19,27},{12,20},{28,4..., dimensions={0}, use_global_device_ids=true | all-gather | bytes 602112 | tf_op jit(solution)/shard_map/all_gather | solution.py:175
  82.8 0.1 convert_reduce_fusion.2
  82.9 16.1 %all-gather.8 = f16[896,896]{1,0:T(8,128)(2,1)S(1)} all-gather(f16[112,896]{1,0:T(8,128)(2,1)S(1)} %convert_element_type.82), channel_id=5, replica_groups=mesh['z_lo'=4,'y'=4,'z_hi'=4,'x'=4,'core'=2] {'x','core'}, dimensions={0}, use_global_device_ids=true | all-gather | bytes 1806336 | tf_op jit(solution)/shard_map/all_gather | solution.py:136
  99.0 0.2 convert_element_type.91.left
  99.2 1.7 %shard_map.21 = bf16[4,1008,128]{2,1,0:T(8,128)(2,1)S(1)} custom-call(bf16[896,896]{1,0:T(8,128)(2,1)S(1)} %convert_element_type.91.left, bf16[4,1008,128]{2,1,0:T(8,128)(2,1)S(1)} %shard_map.20.right), custom_call_target="tpu_custom_call" | custom-call | flops 924844032 | bytes 2637824 | tf_op jit(solution)/shard_map/pallas_call | solution.py:28
  100.9 18.7 %all_to_all.21 = bf16[4,1008,128]{2,1,0:T(8,128)(2,1)S(1)} all-to-all(bf16[4,1008,128]{2,1,0:T(8,128)(2,1)S(1)} %shard_map.21), channel_id=1, replica_groups=mesh['z_lo'=4,'y'=4,'z_hi'=4,'x'=4,'core'=2] {'y'}, dimensions={0} | all-to-all | bytes 2064384 | tf_op jit(solution)/shard_map/all_to_all | solution.py:140
  119.7 0.1 convert_reduce_fusion.once
  119.8 18.9 %all-gather.4 = bf16[4032,128]{1,0:T(8,128)(2,1)S(1)} all-gather(bf16[1008,128]{1,0:T(8,128)(2,1)S(1)} %convert_element_type.86), channel_id=6, replica_groups=mesh['z_lo'=4,'y'=4,'z_hi'=4,'x'=4,'core'=2] {'z_lo'}, dimensions={0}, use_global_device_ids=true | all-gather | bytes 1290240 | tf_op jit(solution)/shard_map/all_gather | solution.py:189
  138.8 1.7 %shard_map.22 = bf16[4,1008,128]{2,1,0:T(8,128)(2,1)S(1)} custom-call(bf16[896,896]{1,0:T(8,128)(2,1)S(1)} %convert_element_type.91.left, bf16[4,1008,128]{2,1,0:T(8,128)(2,1)S(1)} %bitcast.12), custom_call_target="tpu_custom_call" | custom-call | flops 924844032 | bytes 2637824 | tf_op jit(solution)/shard_map/pallas_call | solution.py:28
  140.5 14.3 %all_to_all.22.parts = bf16[4,1008,128]{2,1,0:T(8,128)(2,1)S(1)} all-to-all(bf16[4,1008,128]{2,1,0:T(8,128)(2,1)S(1)} %shard_map.22), channel_id=1, replica_groups=mesh['z_lo'=4,'y'=4,'z_hi'=4,'x'=4,'core'=2] {'y'}, dimensions={0} | all-to-all | bytes 2064384 | tf_op jit(solution)/shard_map/all_to_all | solution.py:140
  154.8 1.2 shard_map.23
  (4 shorter events, 0.1 us)
Async XLA Ops:
  0.0 12.4 %copy-start = (bf16[224,576]{1,0:T(8,128)(2,1)S(1)}, bf16[224,576]{1,0:T(8,128)(2,1)}, u32[]{:S(2)}) copy-start(bf16[224,576]{1,0:T(8,128)(2,1)} %iterate.1) | copy-start | bytes 774148
  2.1 33.3 %all-to-all-start = ((bf16[8,112,576]{2,1,0:T(8,128)(2,1)}), bf16[8,112,576]{2,1,0:T(8,128)(2,1)S(1)}, u32[]{:S(2)}, u32[]{:S(2)}) async-start(bf16[8,112,576]{2,1,0:T(8,128)(2,1)} %bitcast.13), calls=%async_computation | async-start | bytes 2293760 | tf_op jit(solution)/shard_map/all_to_all | solution.py:140

commit v21 on v15

--- a/solution.py
+++ b/solution.py
@@ -80,10 +80,20 @@
 
 def gram_kernel(left, right, out, held):
     blocks, cores, rows, cols = left.shape
-    tile = jnp.zeros((blocks * rows, out.shape[-1]), jnp.float32)
-    for k in range(cores):
-        unpack(right.at[:, k], held.at[k])
-        tile += dot(left[:, k].reshape(blocks * rows, cols), held[k], 1)
+    whole = cols - cols % LANES
+    size = held.shape[0] // blocks
+    for i in range(blocks):
+        for k in range(cores):
+            for row, col, packed_row, packed_col in pieces(size, cols):
+                start = k * whole + col.start
+                if col.start >= whole:
+                    start = cores * whole + k * (cols - whole)
+                place = slice(start, start + col.stop - col.start)
+                row = slice(i * size + row.start, i * size + row.stop)
+                held[row, place] = right[i, k, packed_row, packed_col]
+    lhs = [left[:, k, :, :whole] for k in range(cores)]
+    lhs = jnp.concatenate(lhs + [left[:, k, :, whole:] for k in range(cores)], axis=-1)
+    tile = dot(lhs.reshape(blocks * rows, cores * cols), held[...], 1)
     out[...] = tile.astype(out.dtype).reshape(out.shape)
 
 
@@ -145,7 +155,7 @@
         gram_kernel,
         [(left, VMEM), (right, VMEM)],
         bf16(4, half, 4 * rows),
-        scratch=[pltpu.VMEM((2, 4 * rows, cols), jnp.bfloat16)],
+        scratch=[pltpu.VMEM((4 * rows, 2 * cols), jnp.bfloat16)],
         flops=4 * 4 * half * 4 * rows * cols,
     )
     tile, right = lax.optimization_barrier((tile, right))

time: 158 us -> 158 us (level)
  no operation moved by 1% of the time
where the time goes in v21:
time: 158 us; the launch traced here: 156 us
  blocking collectives  136 us (86%)
  starting transfers between devices  10.4 us (7%)
  Pallas kernels  7.25 us (5%)
    all_to_all x3, blocking collectives, exchange(): return lax.all_to_all(array, axes, 0, 0, tiled=True)  47.7 us
    all_gather x2, blocking collectives, gather(): lax.all_gather(array.astype(jnp.float16), axes, axis=0).astype(jnp.bfloat16)  38.7 us
    all_gather x2, blocking collectives, shards(): lax.all_gather(piece, ('z_hi', 'core'), axis=0, axis_index_groups=groups)  30.7 us
    all_gather x1, blocking collectives, shards(): lax.all_gather(once.astype(jnp.bfloat16), 'z_lo', axis=0)  18.9 us
    all_to_all x1, starting transfers between devices, exchange(): return lax.all_to_all(array, axes, 0, 0, tiled=True)  10.4 us
    pallas_call x6, Pallas kernels, call(): pl.pallas_call(kernel, out_shape=output, in_specs=in_specs, out_specs=spe...  7.25 us
  transfers between devices with their start and end apart: 1, of which 0 were waited for; matrix products, arithmetic and copies ran while one was open for 0% of the time, Pallas kernels for 0%

profile of v21, /device:TPU:1, one launch (start us, length us, event | category | flops | bytes accessed | tf_op | source)
XLA Modules:
  0.0 155.8 jit_solution(4092085280243695798)
XLA Ops:
  0.0 0.0 copy-start
  0.0 1.0 copy-done
  1.0 1.0 shard_map.17
  2.0 10.4 %all-to-all-start = ((bf16[8,112,576]{2,1,0:T(8,128)(2,1)}), bf16[8,112,576]{2,1,0:T(8,128)(2,1)S(1)}, u32[]{:S(2)}, u32[]{:S(2)}) async-start(bf16[8,112,576]{2,1,0:T(8,128)(2,1)} %bitcast), calls=%async_computation | async-start | bytes 2293760 | tf_op jit(solution)/shard_map/all_to_all | solution.py:134
  12.4 0.1 convert_element_type.73
  12.4 22.6 %all-gather.7 = f16[8064,128]{1,0:T(8,128)(2,1)S(1)} all-gather(f16[1008,128]{1,0:T(8,128)(2,1)S(1)} %convert_element_type.73), channel_id=2, replica_groups=mesh['z_lo'=4,'y'=4,'z_hi'=4,'x'=4,'core'=2] {'z_lo','core'}, dimensions={0}, use_global_device_ids=true | all-gather | bytes 2322432 | tf_op jit(solution)/shard_map/all_gather | solution.py:130
  35.0 0.2 convert_element_type.88
  35.2 0.0 all-to-all-done
  35.2 1.5 shard_map.18
  36.7 0.1 shard_map.19.right
  36.8 14.5 %all_to_all.20 = bf16[4,112,896]{2,1,0:T(8,128)(2,1)S(1)} all-to-all(bf16[4,112,896]{2,1,0:T(8,128)(2,1)S(1)} %shard_map.18), channel_id=1, replica_groups=mesh['z_lo'=4,'y'=4,'z_hi'=4,'x'=4,'core'=2] {'x'}, dimensions={0} | all-to-all | bytes 1605632 | tf_op jit(solution)/shard_map/all_to_all | solution.py:134
  51.4 0.1 convert_reduce_fusion.1
  51.5 16.6 %all-gather.1 = f16[224,896]{1,0:T(8,128)(2,1)S(1)} all-gather(f16[112,896]{1,0:T(8,128)(2,1)S(1)} %convert_element_type.76), channel_id=3, replica_groups={{0,8},{16,24},{9,17},{25,1},{2,10},{18,26},{11,19},{27,3},{4,12},{20,28..., dimensions={0}, use_global_device_ids=true | all-gather | bytes 602112 | tf_op jit(solution)/shard_map/all_gather | solution.py:167
  68.1 0.1 convert_reduce_fusion.3
  68.2 14.2 %all-gather.2 = f16[224,896]{1,0:T(8,128)(2,1)S(1)} all-gather(f16[112,896]{1,0:T(8,128)(2,1)S(1)} %convert_element_type.79), channel_id=4, replica_groups={{8,16},{24,0},{1,9},{17,25},{10,18},{26,2},{3,11},{19,27},{12,20},{28,4..., dimensions={0}, use_global_device_ids=true | all-gather | bytes 602112 | tf_op jit(solution)/shard_map/all_gather | solution.py:167
  82.3 0.1 convert_reduce_fusion.2
  82.4 16.1 %all-gather.8 = f16[896,896]{1,0:T(8,128)(2,1)S(1)} all-gather(f16[112,896]{1,0:T(8,128)(2,1)S(1)} %convert_element_type.82), channel_id=5, replica_groups=mesh['z_lo'=4,'y'=4,'z_hi'=4,'x'=4,'core'=2] {'x','core'}, dimensions={0}, use_global_device_ids=true | all-gather | bytes 1806336 | tf_op jit(solution)/shard_map/all_gather | solution.py:130
  98.5 0.3 convert_element_type.91.left
  98.8 1.7 %shard_map.20 = bf16[4,1008,128]{2,1,0:T(8,128)(2,1)S(1)} custom-call(bf16[896,896]{1,0:T(8,128)(2,1)S(1)} %convert_element_type.91.left, bf16[4,1008,128]{2,1,0:T(8,128)(2,1)S(1)} %shard_map.19.right), custom_call_target="tpu_custom_call" | custom-call | flops 924844032 | bytes 2637824 | tf_op jit(solution)/shard_map/pallas_call | solution.py:28
  100.6 18.7 %all_to_all.21 = bf16[4,1008,128]{2,1,0:T(8,128)(2,1)S(1)} all-to-all(bf16[4,1008,128]{2,1,0:T(8,128)(2,1)S(1)} %shard_map.20), channel_id=1, replica_groups=mesh['z_lo'=4,'y'=4,'z_hi'=4,'x'=4,'core'=2] {'y'}, dimensions={0} | all-to-all | bytes 2064384 | tf_op jit(solution)/shard_map/all_to_all | solution.py:134
  119.3 0.1 convert_reduce_fusion.once
  119.5 18.9 %all-gather.4 = bf16[4032,128]{1,0:T(8,128)(2,1)S(1)} all-gather(bf16[1008,128]{1,0:T(8,128)(2,1)S(1)} %convert_element_type.86), channel_id=6, replica_groups=mesh['z_lo'=4,'y'=4,'z_hi'=4,'x'=4,'core'=2] {'z_lo'}, dimensions={0}, use_global_device_ids=true | all-gather | bytes 1290240 | tf_op jit(solution)/shard_map/all_gather | solution.py:181
  138.4 1.7 %shard_map.21 = bf16[4,1008,128]{2,1,0:T(8,128)(2,1)S(1)} custom-call(bf16[896,896]{1,0:T(8,128)(2,1)S(1)} %convert_element_type.91.left, bf16[4,1008,128]{2,1,0:T(8,128)(2,1)S(1)} %bitcast.12), custom_call_target="tpu_custom_call" | custom-call | flops 924844032 | bytes 2637824 | tf_op jit(solution)/shard_map/pallas_call | solution.py:28
  140.2 0.0 copy-start.1
  140.2 14.4 %all_to_all.22.parts = bf16[4,1008,128]{2,1,0:T(8,128)(2,1)S(1)} all-to-all(bf16[4,1008,128]{2,1,0:T(8,128)(2,1)S(1)} %shard_map.21), channel_id=1, replica_groups=mesh['z_lo'=4,'y'=4,'z_hi'=4,'x'=4,'core'=2] {'y'}, dimensions={0} | all-to-all | bytes 2064384 | tf_op jit(solution)/shard_map/all_to_all | solution.py:134
  154.6 0.0 copy-done.1
  154.6 1.2 shard_map.22
  (4 shorter events, 0.1 us)
Async XLA Ops:
  0.0 1.0 copy-start
  2.0 33.2 %all-to-all-start = ((bf16[8,112,576]{2,1,0:T(8,128)(2,1)}), bf16[8,112,576]{2,1,0:T(8,128)(2,1)S(1)}, u32[]{:S(2)}, u32[]{:S(2)}) async-start(bf16[8,112,576]{2,1,0:T(8,128)(2,1)} %bitcast), calls=%async_computation | async-start | bytes 2293760 | tf_op jit(solution)/shard_map/all_to_all | solution.py:134
  140.2 14.4 %copy-start.1 = (bf16[224,576]{1,0:T(8,128)(2,1)S(1)}, bf16[224,576]{1,0:T(8,128)(2,1)}, u32[]{:S(2)}) copy-start(bf16[224,576]{1,0:T(8,128)(2,1)} %iterate.1) | copy-start | bytes 774148

commit v22 on v21

--- a/solution.py
+++ b/solution.py
@@ -97,8 +97,8 @@
     out[...] = tile.astype(out.dtype).reshape(out.shape)
 
 
-def own_kernel(core, right, out):
-    out[...] = right[:, pl.ds(core[0], 1)].reshape(out.shape)
+def own_product_kernel(core, left, right, out, held):
+    product_kernel(left, right.at[:, core[0]], out, held)
 
 
 def product_kernel(left, right, out, held):
@@ -158,27 +158,27 @@
         scratch=[pltpu.VMEM((4 * rows, 2 * cols), jnp.bfloat16)],
         flops=4 * 4 * half * 4 * rows * cols,
     )
-    tile, right = lax.optimization_barrier((tile, right))
-    own = call(own_kernel, [(core, SMEM), (right, VMEM)], bf16(4, packed, LANES))
-    tile, own = lax.optimization_barrier((tile, own))
     piece = total(exchange(tile, "x"))
     for groups in PAIRS:
         piece = piece.astype(jnp.float16)
         piece = total(lax.all_gather(piece, ("z_hi", "core"), axis=0, axis_index_groups=groups))
     gram = gather(piece, ("x", "core")).reshape(4 * rows, 4 * rows)
 
-    def gram_times(array):
+    def gram_times(kernel, *operands):
         parts = call(
-            product_kernel,
-            [(gram, VMEM), (array, VMEM)],
+            kernel,
+            operands,
             bf16(4, packed, LANES),
             scratch=[pltpu.VMEM((4 * rows, cols), jnp.bfloat16)],
             flops=2 * gram.size * cols,
         )
         return exchange(parts, "y")
 
-    once = total(gram_times(own))
-    twice = gram_times(lax.all_gather(once.astype(jnp.bfloat16), "z_lo", axis=0))
+    once = total(
+        gram_times(own_product_kernel, (core, SMEM), (gram, VMEM), (right, VMEM))
+    )
+    twice = lax.all_gather(once.astype(jnp.bfloat16), "z_lo", axis=0)
+    twice = gram_times(product_kernel, (gram, VMEM), (twice, VMEM))
     return call(
         update_kernel,
         [(iterate, ANY), (once, VMEM), (twice, VMEM)],

time: 158 us -> 160 us (1.013)
  blocking collectives: 136 us -> 122 us
  waiting for transfers between devices: 0.01 us -> 12.4 us
  starting transfers between devices: 10.4 us -> 13.8 us
    all_to_all x3 -> x2, blocking collectives: 47.7 us -> 33.3 us  [exchange(): return lax.all_to_all(array, axes, 0, 0, tiled=True)]
    all_to_all x1 -> x2, waiting for transfers between devices: 0.01 us -> 12.4 us  [exchange(): return lax.all_to_all(array, axes, 0, 0, tiled=True)]
    all_to_all x1 -> x2, starting transfers between devices: 10.4 us -> 13.8 us  [exchange(): return lax.all_to_all(array, axes, 0, 0, tiled=True)]
    pallas_call x6 -> x5, Pallas kernels: 7.25 us -> 7.18 us  [call(): pl.pallas_call(kernel, out_shape=output, in_specs=in_specs, out_specs=spe...]
  transfers between devices with their start and end apart: 1 -> 2, of which waited for: 0 -> 1; matrix products, arithmetic and copies ran while one was open for 0% -> 0% of each run, Pallas kernels for 0% -> 0%
where the time goes in v22:
time: 160 us; the launch traced here: 158 us
  blocking collectives  122 us (76%)
  starting transfers between devices  13.8 us (9%)
  waiting for transfers between devices  12.4 us (8%)
  Pallas kernels  7.18 us (4%)
  local copies, waits for them, and re-layouts  1.85 us (1%)
    all_gather x2, blocking collectives, gather(): lax.all_gather(array.astype(jnp.float16), axes, axis=0).astype(jnp.bfloat16)  40 us
    all_to_all x2, blocking collectives, exchange(): return lax.all_to_all(array, axes, 0, 0, tiled=True)  33.3 us
    all_gather x2, blocking collectives, shards(): lax.all_gather(piece, ('z_hi', 'core'), axis=0, axis_index_groups=groups)  29.7 us
    all_gather x1, blocking collectives, shards(): twice = lax.all_gather(once.astype(jnp.bfloat16), 'z_lo', axis=0)  19 us
    all_to_all x2, starting transfers between devices, exchange(): return lax.all_to_all(array, axes, 0, 0, tiled=True)  13.8 us
    all_to_all x2, waiting for transfers between devices, exchange(): return lax.all_to_all(array, axes, 0, 0, tiled=True)  12.4 us
    pallas_call x5, Pallas kernels, call(): pl.pallas_call(kernel, out_shape=output, in_specs=in_specs, out_specs=spe...  7.18 us
  transfers between devices with their start and end apart: 2, of which 1 were waited for; matrix products, arithmetic and copies ran while one was open for 0% of the time, Pallas kernels for 0%

profile of v22, /device:TPU:1, one launch (start us, length us, event | category | flops | bytes accessed | tf_op | source)
XLA Modules:
  0.0 158.4 jit_solution(4946257956270559419)
XLA Ops:
  0.0 0.0 copy-start.1
  0.0 1.0 copy-done.1
  1.0 1.0 shard_map.17
  2.0 10.4 %all-to-all-start = ((bf16[8,112,576]{2,1,0:T(8,128)(2,1)}), bf16[8,112,576]{2,1,0:T(8,128)(2,1)S(1)}, u32[]{:S(2)}, u32[]{:S(2)}) async-start(bf16[8,112,576]{2,1,0:T(8,128)(2,1)} %bitcast.1), calls=%async_computation | async-start | bytes 2293760 | tf_op jit(solution)/shard_map/all_to_all | solution.py:134
  12.4 0.1 convert_element_type.73
  12.4 22.6 %all-gather.7 = f16[8064,128]{1,0:T(8,128)(2,1)S(1)} all-gather(f16[1008,128]{1,0:T(8,128)(2,1)S(1)} %convert_element_type.73), channel_id=2, replica_groups=mesh['z_lo'=4,'y'=4,'z_hi'=4,'x'=4,'core'=2] {'z_lo','core'}, dimensions={0}, use_global_device_ids=true | all-gather | bytes 2322432 | tf_op jit(solution)/shard_map/all_gather | solution.py:130
  35.0 0.2 convert_element_type.88
  35.2 0.0 all-to-all-done
  35.2 1.5 shard_map.18
  36.7 0.0 copy-start
  36.7 0.9 copy-done
  37.6 3.5 %all-to-all-start.1 = ((bf16[4,112,896]{2,1,0:T(8,128)(2,1)}), bf16[4,112,896]{2,1,0:T(8,128)(2,1)S(1)}, u32[]{:S(2)}, u32[]{:S(2)}) async-start(bf16[4,112,896]{2,1,0:T(8,128)(2,1)} %copy-done), calls=%async_computation.1 | async-start | bytes 1605632 | tf_op jit(solution)/shard_map/all_to_all | solution.py:134
  41.1 12.4 %all-to-all-done.1 = bf16[4,112,896]{2,1,0:T(8,128)(2,1)S(1)} async-done(((bf16[4,112,896]{2,1,0:T(8,128)(2,1)}), bf16[4,112,896]{2,1,0:T(8,128)(2,1)S(1)}, u32[]{:S(2)}, u32[]{:S(2)}) %all-to-all-start.1) | async-done | bytes 802848 | tf_op jit(solution)/shard_map/all_to_all | solution.py:134
  53.5 0.1 convert_reduce_fusion.1
  53.7 15.8 %all-gather.1 = f16[224,896]{1,0:T(8,128)(2,1)S(1)} all-gather(f16[112,896]{1,0:T(8,128)(2,1)S(1)} %convert_element_type.76), channel_id=3, replica_groups={{0,8},{16,24},{9,17},{25,1},{2,10},{18,26},{11,19},{27,3},{4,12},{20,28..., dimensions={0}, use_global_device_ids=true | all-gather | bytes 602112 | tf_op jit(solution)/shard_map/all_gather | solution.py:164
  69.4 0.1 convert_reduce_fusion.3
  69.5 14.0 %all-gather.2 = f16[224,896]{1,0:T(8,128)(2,1)S(1)} all-gather(f16[112,896]{1,0:T(8,128)(2,1)S(1)} %convert_element_type.79), channel_id=4, replica_groups={{8,16},{24,0},{1,9},{17,25},{10,18},{26,2},{3,11},{19,27},{12,20},{28,4..., dimensions={0}, use_global_device_ids=true | all-gather | bytes 602112 | tf_op jit(solution)/shard_map/all_gather | solution.py:164
  83.5 0.1 convert_reduce_fusion.2
  83.6 17.4 %all-gather.8 = f16[896,896]{1,0:T(8,128)(2,1)S(1)} all-gather(f16[112,896]{1,0:T(8,128)(2,1)S(1)} %convert_element_type.82), channel_id=5, replica_groups=mesh['z_lo'=4,'y'=4,'z_hi'=4,'x'=4,'core'=2] {'x','core'}, dimensions={0}, use_global_device_ids=true | all-gather | bytes 1806336 | tf_op jit(solution)/shard_map/all_gather | solution.py:130
  101.0 0.3 convert_element_type.91.left
  101.3 1.7 %shard_map.19 = bf16[4,1008,128]{2,1,0:T(8,128)(2,1)S(1)} custom-call(s32[1]{0:T(128)} %bitcast.core, bf16[896,896]{1,0:T(8,128)(2,1)S(1)} %convert_element_type.91.left, bf16[4,2,1008,128]{3,2,1,0:T(8,128)(2,1)S(1)} %bitcast.10), custom_call_target="tpu_custom_call" | custom-call | flops 924844032 | bytes 3670018 | tf_op jit(solution)/shard_map/pallas_call | solution.py:28
  103.0 18.8 %all_to_all.20 = bf16[4,1008,128]{2,1,0:T(8,128)(2,1)S(1)} all-to-all(bf16[4,1008,128]{2,1,0:T(8,128)(2,1)S(1)} %shard_map.19), channel_id=1, replica_groups=mesh['z_lo'=4,'y'=4,'z_hi'=4,'x'=4,'core'=2] {'y'}, dimensions={0} | all-to-all | bytes 2064384 | tf_op jit(solution)/shard_map/all_to_all | solution.py:134
  121.8 0.1 convert_reduce_fusion.once
  122.0 19.0 %all-gather.4 = bf16[4032,128]{1,0:T(8,128)(2,1)S(1)} all-gather(bf16[1008,128]{1,0:T(8,128)(2,1)S(1)} %convert_element_type.86), channel_id=6, replica_groups=mesh['z_lo'=4,'y'=4,'z_hi'=4,'x'=4,'core'=2] {'z_lo'}, dimensions={0}, use_global_device_ids=true | all-gather | bytes 1290240 | tf_op jit(solution)/shard_map/all_gather | solution.py:180
  141.0 1.7 %shard_map.20 = bf16[4,1008,128]{2,1,0:T(8,128)(2,1)S(1)} custom-call(bf16[896,896]{1,0:T(8,128)(2,1)S(1)} %convert_element_type.91.left, bf16[4,1008,128]{2,1,0:T(8,128)(2,1)S(1)} %bitcast.12), custom_call_target="tpu_custom_call" | custom-call | flops 924844032 | bytes 2637824 | tf_op jit(solution)/shard_map/pallas_call | solution.py:28
  142.7 0.0 copy-start.2
  142.7 14.5 %all_to_all.21.parts = bf16[4,1008,128]{2,1,0:T(8,128)(2,1)S(1)} all-to-all(bf16[4,1008,128]{2,1,0:T(8,128)(2,1)S(1)} %shard_map.20), channel_id=1, replica_groups=mesh['z_lo'=4,'y'=4,'z_hi'=4,'x'=4,'core'=2] {'y'}, dimensions={0} | all-to-all | bytes 2064384 | tf_op jit(solution)/shard_map/all_to_all | solution.py:134
  157.3 0.0 copy-done.2
  157.3 1.2 shard_map.21
  (4 shorter events, 0.1 us)
Async XLA Ops:
  0.0 1.0 copy-start.1
  2.0 33.2 %all-to-all-start = ((bf16[8,112,576]{2,1,0:T(8,128)(2,1)}), bf16[8,112,576]{2,1,0:T(8,128)(2,1)S(1)}, u32[]{:S(2)}, u32[]{:S(2)}) async-start(bf16[8,112,576]{2,1,0:T(8,128)(2,1)} %bitcast.1), calls=%async_computation | async-start | bytes 2293760 | tf_op jit(solution)/shard_map/all_to_all | solution.py:134
  36.7 0.9 copy-start
  37.6 15.9 %all-to-all-start.1 = ((bf16[4,112,896]{2,1,0:T(8,128)(2,1)}), bf16[4,112,896]{2,1,0:T(8,128)(2,1)S(1)}, u32[]{:S(2)}, u32[]{:S(2)}) async-start(bf16[4,112,896]{2,1,0:T(8,128)(2,1)} %copy-done), calls=%async_computation.1 | async-start | bytes 1605632 | tf_op jit(solution)/shard_map/all_to_all | solution.py:134
  142.7 14.6 %copy-start.2 = (bf16[224,576]{1,0:T(8,128)(2,1)S(1)}, bf16[224,576]{1,0:T(8,128)(2,1)}, u32[]{:S(2)}) copy-start(bf16[224,576]{1,0:T(8,128)(2,1)} %iterate.1) | copy-start | bytes 774148
